TPU v7x, 256 devices: a whole 4x4x8 slice. The times are simulated.
256 devices in a mesh: tm: 32 (over z, y), freq: 8 (over x, core).
Axes of the slice: x: 4, y: 4, z: 8, core: 2. Of those that a mesh axis runs over, the one named last changes fastest.
Arguments:
- spectrum: bfloat16 [256, 1024, 256], P('tm', 'freq'), may hold values from -6 to 6
- conv_weight: bfloat16 [2, 3, 3, 128, 128], replicated, may hold values from -0.125 to 0.125
- qkv_weight: bfloat16 [256, 1536], replicated, may hold values from -0.375 to 0.375
- out_weight: bfloat16 [512, 256], replicated, may hold values from -1.5 to 1.5
- cotangent: bfloat16 [256, 1024, 256], P(('tm', 'freq')), may hold values from -6 to 6
Outputs:
- enhanced: bfloat16 [256, 1024, 256], P(('tm', 'freq'))
- grad_spectrum: bfloat16 [256, 1024, 256], P('tm', 'freq')
- grad_conv: float32 [294912], P(('tm', 'freq'))
- grad_qkv: float32 [393216], P(('tm', 'freq'))
- grad_out: float32 [131072], P(('tm', 'freq'))
All inputs are finite; a program needn't handle non-finite values.
Results may differ from a plain program's by a relative error of at most 0.014.
Values may be sent and summed in bfloat16 or wider, within the bound.
No kernel may reach another device: no remote copies, remote signals or barrier semaphores. Data moves between devices by JAX's collectives and lax.ppermute only.
A program may use at most 128 MiB of HBM per device.

v0:
```python
import math

import jax
import jax.numpy as jnp
from jax import lax
from jax.sharding import PartitionSpec as P

HEADS = 4


def padded_2(array, sides, width):
    for axis, dim in sides:
        size, length = (lax.axis_size(axis), array.shape[dim])
        up = [(i, (i + 1) % size) for i in range(size - 1)]
        down = [(j, i) for i, j in up]
        last = lax.slice_in_dim(array, length - width, length, axis=dim)
        first = lax.slice_in_dim(array, 0, width, axis=dim)
        before = lax.ppermute(last, axis, up)
        after = lax.ppermute(first, axis, down)
        array = jnp.concatenate([before, array, after], axis=dim)
    return array


def block_matrix(conv_weight):
    real_part = conv_weight[0]
    imag_part = conv_weight[1]
    upper_half = jnp.concatenate([real_part, imag_part], axis=-1)
    lower_half = jnp.concatenate([-imag_part, real_part], axis=-1)
    return jnp.concatenate([upper_half, lower_half], axis=-2)


def tap_windows(padded, frame_count, bin_count, flipped):
    pieces = []
    for row_tap in range(3):
        for col_tap in range(3):
            row_at = 2 - row_tap if flipped else row_tap
            col_at = 2 - col_tap if flipped else col_tap
            pieces.append(padded[row_at : row_at + frame_count, col_at : col_at + bin_count])
    stacked = jnp.concatenate(pieces, axis=-1)
    return stacked.reshape(frame_count * bin_count, -1)


def head_pass(parts):
    queries, key_rows, values, grad_attn = parts
    factor = 1.0 / math.sqrt(queries.shape[-1])
    scores = jnp.dot(queries, key_rows.T, preferred_element_type=jnp.float32) * factor
    raised = jnp.exp(scores)
    probs_f = raised / jnp.sum(raised, axis=-1, keepdims=True)
    probs_b = probs_f.astype(jnp.bfloat16)
    attended = jnp.dot(probs_b, values, preferred_element_type=jnp.float32).astype(jnp.bfloat16)
    grad_probs = jnp.dot(grad_attn, values.T, preferred_element_type=jnp.float32)
    grad_values = jnp.dot(probs_b.T, grad_attn, preferred_element_type=jnp.float32).astype(
        jnp.bfloat16
    )
    row_inner = jnp.sum(grad_probs * probs_f, axis=-1, keepdims=True)
    grad_scores = (probs_f * (grad_probs - row_inner) * factor).astype(jnp.bfloat16)
    grad_queries = jnp.dot(grad_scores, key_rows, preferred_element_type=jnp.float32).astype(
        jnp.bfloat16
    )
    grad_keys = jnp.dot(grad_scores.T, queries, preferred_element_type=jnp.float32).astype(
        jnp.bfloat16
    )
    return (attended, grad_queries, grad_keys, grad_values)


def frame_pass(hidden, cotangent, qkv_weight, out_weight):
    bin_count = hidden.shape[0]
    hidden_f = hidden.astype(jnp.float32)
    inv_rms = lax.rsqrt(jnp.mean(hidden_f * hidden_f, axis=-1, keepdims=True) + 1e-06)
    normed_f = hidden_f * inv_rms
    normed = normed_f.astype(jnp.bfloat16)
    qkv = jnp.dot(normed, qkv_weight, preferred_element_type=jnp.float32).astype(jnp.bfloat16)
    grad_attn = jnp.dot(cotangent, out_weight.T, preferred_element_type=jnp.float32).astype(
        jnp.bfloat16
    )
    split_qkv = qkv.reshape(bin_count, 3, HEADS, -1).transpose(1, 2, 0, 3)
    grad_split = grad_attn.reshape(bin_count, HEADS, -1).transpose(1, 0, 2)
    attended, grad_q, grad_k, grad_v = lax.map(
        head_pass, (split_qkv[0], split_qkv[1], split_qkv[2], grad_split)
    )
    attended = attended.transpose(1, 0, 2).reshape(bin_count, -1)
    grad_cells = jnp.stack([grad_q, grad_k, grad_v]).transpose(2, 0, 1, 3).reshape(bin_count, -1)
    enhanced = (
        hidden_f + jnp.dot(attended, out_weight, preferred_element_type=jnp.float32)
    ).astype(jnp.bfloat16)
    grad_normed = jnp.dot(grad_cells, qkv_weight.T, preferred_element_type=jnp.float32)
    mixing = jnp.mean(grad_normed * normed_f, axis=-1, keepdims=True)
    grad_hidden = (
        cotangent.astype(jnp.float32) + inv_rms * (grad_normed - normed_f * mixing)
    ).astype(jnp.bfloat16)
    grad_out = jnp.dot(attended.T, cotangent, preferred_element_type=jnp.float32)
    grad_qkv = jnp.dot(normed.T, grad_cells, preferred_element_type=jnp.float32)
    return (enhanced, grad_hidden, grad_qkv, grad_out)


def attend_frames(hidden, cotangent, qkv_weight, out_weight):
    zero_sums = (jnp.zeros(qkv_weight.shape, jnp.float32), jnp.zeros(out_weight.shape, jnp.float32))

    def frame_step(running, frame_items):
        enhanced, grad_hidden, grad_qkv, grad_out = frame_pass(
            frame_items[0], frame_items[1], qkv_weight, out_weight
        )
        return ((running[0] + grad_qkv, running[1] + grad_out), (enhanced, grad_hidden))

    summed, results = lax.scan(frame_step, zero_sums, (hidden, cotangent))
    return (results[0], results[1], summed[0], summed[1])


def shards(spectrum, conv_weight, qkv_weight, out_weight, cotangent):
    frame_count, bin_count, width = spectrum.shape
    cells = frame_count * bin_count
    block_weight = block_matrix(conv_weight)
    padded = padded_2(spectrum, (("tm", 0), ("freq", 1)), 1)
    windows_x = tap_windows(padded, frame_count, bin_count, False)
    conv = jnp.dot(
        windows_x, block_weight.reshape(9 * width, width), preferred_element_type=jnp.float32
    )
    hidden = (spectrum.reshape(cells, width).astype(jnp.float32) + jax.nn.silu(conv)).astype(
        jnp.bfloat16
    )
    hidden = hidden.reshape(frame_count, bin_count, width)
    frames = lax.all_to_all(hidden, "freq", split_axis=0, concat_axis=1, tiled=True)
    enhanced, grad_frames, grad_qkv_sum, grad_out_sum = attend_frames(
        frames, cotangent, qkv_weight, out_weight
    )
    grad_hidden = lax.all_to_all(grad_frames, "freq", split_axis=1, concat_axis=0, tiled=True)
    grad_flat = grad_hidden.reshape(cells, width).astype(jnp.float32)
    sigma = jax.nn.sigmoid(conv)
    grad_conv_out = (grad_flat * sigma * (1.0 + conv * (1.0 - sigma))).astype(jnp.bfloat16)
    grad_tile = grad_conv_out.reshape(frame_count, bin_count, width)
    grad_padded = padded_2(grad_tile, (("tm", 0), ("freq", 1)), 1)
    windows_grad = tap_windows(grad_padded, frame_count, bin_count, True)
    flipped_weight = block_weight.transpose(0, 1, 3, 2).reshape(9 * width, width)
    grad_input = grad_flat + jnp.dot(
        windows_grad, flipped_weight, preferred_element_type=jnp.float32
    )
    grad_spectrum = grad_input.astype(jnp.bfloat16).reshape(frame_count, bin_count, width)
    grad_block = jnp.dot(windows_x.T, grad_conv_out, preferred_element_type=jnp.float32).reshape(
        3, 3, width, width
    )
    chans = width // 2
    grad_real = grad_block[:, :, :chans, :chans] + grad_block[:, :, chans:, chans:]
    grad_imag = grad_block[:, :, :chans, chans:] - grad_block[:, :, chans:, :chans]
    total_cells = frame_count * lax.axis_size("tm") * frames.shape[1]
    norm_factor = 1.0 / math.sqrt(total_cells)
    conv_terms = (jnp.stack([grad_real, grad_imag]) * norm_factor).reshape(-1)
    qkv_terms = (grad_qkv_sum * norm_factor).reshape(-1)
    out_terms = (grad_out_sum * norm_factor).reshape(-1)
    grad_conv, grad_qkv, grad_out = (
        lax.psum_scatter(conv_terms, ("tm", "freq"), scatter_dimension=0, tiled=True),
        lax.psum_scatter(qkv_terms, ("tm", "freq"), scatter_dimension=0, tiled=True),
        lax.psum_scatter(out_terms, ("tm", "freq"), scatter_dimension=0, tiled=True),
    )
    return (enhanced, grad_spectrum, grad_conv, grad_qkv, grad_out)


def solution(mesh):
    placed = (P("tm", "freq", None), P(), P(), P(), P(("tm", "freq"), None, None))
    return jax.shard_map(
        shards,
        mesh=mesh,
        in_specs=placed,
        out_specs=(
            P(("tm", "freq"), None, None),
            P("tm", "freq", None),
            P(("tm", "freq")),
            P(("tm", "freq")),
            P(("tm", "freq")),
        ),
        check_vma=False,
    )
```

profile of v0, /device:TPU:32, one launch (start us, length us, event | category | flops | bytes accessed | tf_op | source)
XLA Modules:
  0.0 457.2 jit_solution(9076310058036920416)
XLA Ops:
  8.2 3.5 collective-permute-start
  11.7 4.5 collective-permute-start.1
  22.4 3.3 collective-permute-done.3
  26.5 2.6 fusion.40
  29.2 6.0 %all-to-all-start = ((bf16[8,128,256]{2,1,0:T(8,128)(2,1)}), bf16[8,128,256]{2,1,0:T(8,128)(2,1)S(1)}, u32[]{:S(2)}, u32[]{:S(2)}) async-start(bf16[8,128,256]{2,1,0:T(8,128)(2,1)} %bitcast.13), calls=%async_computation | async-start | bytes 1048576 | tf_op jit(solution)/shard_map/all_to_all | solution.py:122
  36.7 2.2 copy.37
  40.5 6.6 %copy.47 = bf16[1024,2304]{0,1:T(8,128)(2,1)} copy(bf16[1024,2304]{1,0:T(8,128)(2,1)} %bitcast.183) | data formatting | bytes 9437184 | tf_op jit(solution)/shard_map/reshape | solution.py:40
  47.6 2.6 convolution_convert_fusion.4
  50.3 6.3 %reshape.127 = bf16[1024,3,4,128]{3,2,1,0:T(4,128)(2,1)} reshape(bf16[1024,1536]{1,0:T(8,128)(2,1)} %convolution_convert_fusion.4) | data formatting | bytes 6291456 | tf_op jit(solution)/shard_map/while/body/eval_jaxpr/reshape | solution.py:76
  56.6 2.4 copy.63
  60.8 75.4 %while.29 = (s32[]{:T(128)}, bf16[4,1024,128]{1,2,0:T(8,128)(2,1)}, bf16[4,1024,128]{1,2,0:T(8,128)(2,1)}, bf16[4,1024,128]{1,2,0:T(8,128)(2,1)}, bf16[4,1024,12...) while((s32[]{:T(128)}, bf16[4,1024,128]{1,2,0:T(8,128)(2,1)}, ...), condition=%wide.region_4.5_spmd, body=%wide.region_1.4_spmd.sunk | while | flops 1630009344 | bytes 59799712 | solution.py:78
  62.5 2.4 multiply_reduce_fusion.4
  68.1 3.8 fusion.107
  73.8 3.0 fusion.108
  81.4 2.4 multiply_reduce_fusion.4
  86.9 3.8 fusion.107
  92.6 3.0 fusion.108
  100.2 2.4 multiply_reduce_fusion.4
  105.7 3.8 fusion.107
  111.5 3.0 fusion.108
  119.1 2.4 multiply_reduce_fusion.4
  124.6 3.8 fusion.107
  130.3 3.0 fusion.108
  136.2 2.3 pad_maximum_fusion
  141.5 3.8 reduce.4
  146.3 4.8 %all-to-all-start.1 = ((bf16[8,2,16384]{2,1,0:T(2,128)(2,1)}), bf16[8,2,16384]{2,1,0:T(2,128)(2,1)}, u32[]{:S(2)}, u32[]{:S(2)}) async-start(bf16[8,2,16384]{2,1,0:T(2,128)(2,1)} %reshape.140), calls=%async_computation.1 | async-start | bytes 1048576 | tf_op jit(solution)/shard_map/all_to_all | solution.py:126
  151.3 3.0 convolution_multiply_fusion
  158.3 2.5 fusion.37
  164.2 5.0 %collective-permute-start.5 = (bf16[1,128,256]{2,1,0:T(8,128)(2,1)S(1)}, bf16[1,128,256]{2,1,0:T(8,128)(2,1)S(1)}, u32[]{:S(2)}, u32[]{:S(2)}) collective-permute-start(bf16[1,128,256]{2,1,0:T(8,128)(2,1)S(1)} %get-tuple-element.139), channel_id=1, source_target_pairs={{8,0},{16,8},{24,16},{32,24},{40,32},{48,40},{56,48},{64,56},{72,6... | collective-permute-start | bytes 196616 | tf_op jit(solution)/shard_map/ppermute | solution.py:19
  171.1 3.8 fusion.56
  180.2 3.3 collective-permute-done.6
  187.6 258.7 %all-reduce.6.cloned.1.call-done = (f32[294912]{0:T(1024)}, f32[393216]{0:T(1024)}, f32[131072]{0:T(1024)}) async-done(((f32[294912]{0:T(1024)}, f32[393216]{0:T(1024)}, f32[131072]{0:T(1024)}), (f32[294912]{0:T(1024)}, f32[393216]{0:T(1024)}, f32[131072]{0:T(1024)})) %all-reduce.6.cloned.1.call-update) | async-done | bytes 3276816
  (144 shorter events, 78.2 us)
Async XLA Ops:
  7.2 40.4 %copy-start = (bf16[256,1536]{1,0:T(8,128)(2,1)S(1)}, bf16[256,1536]{1,0:T(8,128)(2,1)}, u32[]{:S(2)}) copy-start(bf16[256,1536]{1,0:T(8,128)(2,1)} %param.9) | copy-start | bytes 2359300
  7.2 15.2 %copy-start.5 = (bf16[8,128,256]{2,1,0:T(8,128)(2,1)S(1)}, bf16[8,128,256]{2,1,0:T(8,128)(2,1)}, u32[]{:S(2)}) copy-start(bf16[8,128,256]{2,1,0:T(8,128)(2,1)} %param.7) | copy-start | bytes 1572868
  8.2 10.1 %collective-permute-start = (bf16[1,128,256]{2,1,0:T(8,128)(2,1)S(1)}, bf16[1,128,256]{2,1,0:T(8,128)(2,1)S(1)}, u32[]{:S(2)}, u32[]{:S(2)}) collective-permute-start(bf16[1,128,256]{2,1,0:T(8,128)(2,1)S(1)} %get-tuple-element.141), channel_id=1, source_target_pairs={{0,8},{8,16},{16,24},{24,32},{32,40},{40,48},{48,56},{56,64},{64,7... | collective-permute-start | bytes 196616 | tf_op jit(solution)/shard_map/ppermute | solution.py:18
  11.7 7.7 %collective-permute-start.1 = (bf16[1,128,256]{2,1,0:T(8,128)(2,1)S(1)}, bf16[1,128,256]{2,1,0:T(8,128)(2,1)S(1)}, u32[]{:S(2)}, u32[]{:S(2)}) collective-permute-start(bf16[1,128,256]{2,1,0:T(8,128)(2,1)S(1)} %get-tuple-element.140), channel_id=1, source_target_pairs={{8,0},{16,8},{24,16},{32,24},{40,32},{48,40},{56,48},{64,56},{72,6... | collective-permute-start | bytes 196616 | tf_op jit(solution)/shard_map/ppermute | solution.py:19
  19.4 2.8 collective-permute-start.2
  20.9 4.8 %collective-permute-start.3 = (bf16[10,1,256]{2,1,0:T(2,128)(2,1)S(1)}, bf16[10,1,256]{2,1,0:T(2,128)(2,1)S(1)}, u32[]{:S(2)}, u32[]{:S(2)}) collective-permute-start(bf16[10,1,256]{2,1,0:T(2,128)(2,1)S(1)} %get-tuple-element.132), channel_id=1, source_target_pairs={{1,0},{2,1},{3,2},{4,3},{5,4},{6,5},{7,6},{9,8},{10,9},{11,10},{12... | collective-permute-start | bytes 15368 | tf_op jit(solution)/shard_map/ppermute | solution.py:19
  26.5 2.7 copy-start.6
  26.5 8.7 %copy-start.7 = (bf16[1,1024,256]{2,1,0:T(8,128)(2,1)S(1)}, bf16[1,1024,256]{2,1,0:T(8,128)(2,1)}, u32[]{:S(2)}) copy-start(bf16[1,1024,256]{2,1,0:T(8,128)(2,1)} %param.11) | copy-start | bytes 1572868
  26.5 8.7 %copy-start.11 = (bf16[512,256]{1,0:T(8,128)(2,1)S(1)}, bf16[512,256]{1,0:T(8,128)(2,1)}, u32[]{:S(2)}) copy-start(bf16[512,256]{1,0:T(8,128)(2,1)} %param.10) | copy-start | bytes 786436
  29.2 18.0 %all-to-all-start = ((bf16[8,128,256]{2,1,0:T(8,128)(2,1)}), bf16[8,128,256]{2,1,0:T(8,128)(2,1)S(1)}, u32[]{:S(2)}, u32[]{:S(2)}) async-start(bf16[8,128,256]{2,1,0:T(8,128)(2,1)} %bitcast.13), calls=%async_computation | async-start | bytes 1048576 | tf_op jit(solution)/shard_map/all_to_all | solution.py:122
  47.2 3.1 copy-start.2
  62.5 2.4 copy-start.1
  81.4 2.4 copy-start.1
  100.2 2.4 copy-start.1
  119.0 2.4 copy-start.1
  136.1 2.3 copy-start.3
  138.4 1.8 copy-start.4
  138.4 1.4 copy-start.8
  146.3 15.2 %all-to-all-start.1 = ((bf16[8,2,16384]{2,1,0:T(2,128)(2,1)}), bf16[8,2,16384]{2,1,0:T(2,128)(2,1)}, u32[]{:S(2)}, u32[]{:S(2)}) async-start(bf16[8,2,16384]{2,1,0:T(2,128)(2,1)} %reshape.140), calls=%async_computation.1 | async-start | bytes 1048576 | tf_op jit(solution)/shard_map/all_to_all | solution.py:126
  151.0 295.2 %all-reduce.6.cloned.1.call-start = ((), (), s32[]{:S(2)}) async-start(), calls=%async_computation.2 | async-start | bytes 6553600
  157.2 6.5 %copy-start.10 = (f32[1024,256]{1,0:T(8,128)S(1)}, f32[1024,256]{1,0:T(8,128)}, u32[]{:S(2)}) copy-start(f32[1024,256]{1,0:T(8,128)} %get-tuple-element.145) | copy-start | bytes 3145732
  164.2 12.0 %collective-permute-start.5 = (bf16[1,128,256]{2,1,0:T(8,128)(2,1)S(1)}, bf16[1,128,256]{2,1,0:T(8,128)(2,1)S(1)}, u32[]{:S(2)}, u32[]{:S(2)}) collective-permute-start(bf16[1,128,256]{2,1,0:T(8,128)(2,1)S(1)} %get-tuple-element.139), channel_id=1, source_target_pairs={{8,0},{16,8},{24,16},{32,24},{40,32},{48,40},{56,48},{64,56},{72,6... | collective-permute-start | bytes 196616 | tf_op jit(solution)/shard_map/ppermute | solution.py:19
  169.2 8.3 %collective-permute-start.4 = (bf16[1,128,256]{2,1,0:T(8,128)(2,1)S(1)}, bf16[1,128,256]{2,1,0:T(8,128)(2,1)S(1)}, u32[]{:S(2)}, u32[]{:S(2)}) collective-permute-start(bf16[1,128,256]{2,1,0:T(8,128)(2,1)S(1)} %get-tuple-element.138), channel_id=1, source_target_pairs={{0,8},{8,16},{16,24},{24,32},{32,40},{40,48},{48,56},{56,64},{64,7... | collective-permute-start | bytes 196616 | tf_op jit(solution)/shard_map/ppermute | solution.py:18
  177.5 2.7 collective-permute-start.7
  178.8 4.6 %collective-permute-start.6 = (bf16[10,1,256]{2,1,0:T(2,128)(2,1)S(1)}, bf16[10,1,256]{2,1,0:T(2,128)(2,1)S(1)}, u32[]{:S(2)}, u32[]{:S(2)}) collective-permute-start(bf16[10,1,256]{2,1,0:T(2,128)(2,1)S(1)} %get-tuple-element.131), channel_id=1, source_target_pairs={{1,0},{2,1},{3,2},{4,3},{5,4},{6,5},{7,6},{9,8},{10,9},{11,10},{12... | collective-permute-start | bytes 15368 | tf_op jit(solution)/shard_map/ppermute | solution.py:19
  184.1 1.3 copy-start.9
Sparse Core Ops, SparseCore 0:
  176.3 269.8 all-reduce.5
where the time goes:
time: 461 us; the launch traced here: 457 us
  waiting for transfers between devices  267 us (58%)
  matrix products  78.5 us (17%)
  local copies, waits for them, and re-layouts  49.8 us (11%)
  starting transfers between devices  30.9 us (7%)
  other arithmetic  16 us (3%)
  between operations  14.6 us (3%)
    unnamed x2, waiting for transfers between devices  259 us
    dot_general x4, matrix products, head_pass(): jnp.dot(probs_b, values, preferred_element_type=jnp.float32)  15.2 us
    dynamic_update_slice x24, local copies, waits for them, and re-layouts, frame_pass(): lax.map(head_pass, (split_qkv[0], split_qkv[1], split_qkv[2], grad_split))  12.8 us
    ppermute x4, starting transfers between devices, padded_2(): after = lax.ppermute(first, axis, down)  12.1 us
    dot_general x4, matrix products, head_pass(): jnp.dot(probs_b.T, grad_attn, preferred_element_type=jnp.float32)  12 us
    unnamed x40, local copies, waits for them, and re-layouts  11.4 us
    dot_general x4, matrix products, head_pass(): jnp.dot(grad_attn, values.T, preferred_element_type=jnp.float32)  9.61 us
  transfers between devices with their start and end apart: 11, of which 5 were waited for; matrix products, arithmetic and copies ran while one was open for 7% of the time, Pallas kernels for 0%

commit v1 on v0

v1 whole, which is shorter than its diff:
```python
import functools
import math

import jax
import jax.numpy as jnp
from jax import lax
from jax.experimental import pallas as pl
from jax.experimental.pallas import tpu as pltpu
from jax.sharding import PartitionSpec as P

HEADS = 4
HEAD = 128
BF = jnp.bfloat16
F32 = jnp.float32
NN = (((1,), (0,)), ((), ()))
NT = (((1,), (1,)), ((), ()))
TN = (((0,), (0,)), ((), ()))
QUERY_BLOCK = 512


def mm(a, b, dims=NN):
    return lax.dot_general(a, b, dims, preferred_element_type=F32)


def vmem_call(body, out_shape, scratch, name, cost, limit=48):
    def run(*args):
        return pl.pallas_call(
            body,
            out_shape=out_shape,
            in_specs=[pl.BlockSpec(memory_space=pltpu.VMEM)] * len(args),
            out_specs=jax.tree.map(lambda _: pl.BlockSpec(memory_space=pltpu.VMEM), out_shape),
            scratch_shapes=scratch,
            compiler_params=pltpu.CompilerParams(vmem_limit_bytes=limit * 2**20),
            cost_estimate=pl.CostEstimate(flops=cost[0], bytes_accessed=cost[1], transcendentals=0),
            name=name,
        )(*args)

    return run


def shape(dims, kind=BF):
    return jax.ShapeDtypeStruct(dims, kind)


def shifted(mid, up, down, left, right):
    rows = jnp.concatenate([up, mid, down], axis=0)
    wide = rows.astype(F32)
    bins = wide.shape[1]
    at = lax.broadcasted_iota(jnp.int32, wide.shape, 1)
    before = jnp.where(at == 0, left.astype(F32), pltpu.roll(wide, 1, 1)).astype(BF)
    after = jnp.where(at == bins - 1, right.astype(F32), pltpu.roll(wide, bins - 1, 1)).astype(BF)
    return before, rows, after


def conv_forward_body(mid, up, down, left, right, weight, hidden, slope, stacked, matrix):
    frames, bins, width = mid.shape
    half = width // 2
    before, rows, after = shifted(mid[...], up[...], down[...], left[...], right[...])
    stacked[:, :, :width] = before
    stacked[:, :, width : 2 * width] = rows
    stacked[:, :, 2 * width :] = after
    conv = None
    for i in range(3):
        for j in range(3):
            real, imag = weight[0, i, j], weight[1, i, j]
            at = j * width
            matrix[i, at : at + half, :half] = real
            matrix[i, at : at + half, half:] = imag
            matrix[i, at + half : at + width, :half] = -imag
            matrix[i, at + half : at + width, half:] = real
        part = mm(stacked[i : i + frames].reshape(frames * bins, 3 * width), matrix[i])
        conv = part if conv is None else conv + part
    sigma = 1.0 / (1.0 + jnp.exp(-conv))
    hidden[...] = (mid[...].reshape(frames * bins, width).astype(F32) + conv * sigma).astype(BF)
    slope[...] = sigma * (1.0 + conv * (1.0 - sigma))


def conv_weight_body(frames, grad_hidden, slope, stacked, grad_conv_out, grad_weight):
    _, bins, triple = stacked.shape
    width = triple // 3
    half = width // 2
    cells = frames * bins
    grad = (grad_hidden[...].reshape(cells, width).astype(F32) * slope[...]).astype(BF)
    grad_conv_out[...] = grad.reshape(frames, bins, width)
    flipped = grad.T
    for i in range(3):
        block = mm(flipped, stacked[i : i + frames].reshape(cells, triple))
        for j in range(3):
            at = j * width
            upper = block[:half, at : at + half] + block[half:, at + half : at + width]
            lower = block[half:, at : at + half] - block[:half, at + half : at + width]
            grad_weight[0, i, j] = upper.T * (1.0 / 512)
            grad_weight[1, i, j] = lower.T * (1.0 / 512)


def conv_data_body(mid, up, down, left, right, weight, grad_hidden, out, stacked, matrix):
    frames, bins, width = mid.shape
    half = width // 2
    before, rows, after = shifted(mid[...], up[...], down[...], left[...], right[...])
    stacked[:, :, :width] = after
    stacked[:, :, width : 2 * width] = rows
    stacked[:, :, 2 * width :] = before
    total = grad_hidden[...].reshape(frames * bins, width).astype(F32)
    for i in range(3):
        for j in range(3):
            real, imag = weight[0, i, j], weight[1, i, j]
            at = j * width
            matrix[i, :half, at : at + half] = real
            matrix[i, :half, at + half : at + width] = imag
            matrix[i, half:, at : at + half] = -imag
            matrix[i, half:, at + half : at + width] = real
        rows_at = 2 - i
        total = total + mm(
            stacked[rows_at : rows_at + frames].reshape(frames * bins, 3 * width), matrix[i], NT
        )
    out[...] = total.astype(BF).reshape(frames, bins, width)


def attend_body(
    hidden, cotangent, qkv_w, out_w, enhanced, grad_hidden, grad_qkv, grad_out,
    qkv, grad_att, attended, grad_cells, sum_keys, sum_values,
):
    cells = hidden.shape[0]
    wide = HEADS * HEAD
    log2e = math.log2(math.e)
    factor = 1.0 / math.sqrt(HEAD)
    hidden_f = hidden[...].astype(F32)
    inv_rms = lax.rsqrt(jnp.mean(hidden_f * hidden_f, axis=-1, keepdims=True) + 1e-6)
    normed = (hidden_f * inv_rms).astype(BF)
    qkv[:, :wide] = (mm(normed, qkv_w[:, :wide]) * (factor * log2e)).astype(BF)
    qkv[:, wide:] = mm(normed, qkv_w[:, wide:]).astype(BF)
    grad_att[...] = mm(cotangent[...], out_w[...], NT).astype(BF)
    ones = jnp.ones((cells, HEAD), BF)

    def columns(part, h):
        return pl.ds(pl.multiple_of(part * wide + h * HEAD, HEAD), HEAD)

    def head(h, carry):
        keys = qkv[:, columns(1, h)]
        values = qkv[:, columns(2, h)]
        values_ones = jnp.concatenate([values, ones], axis=1)
        for block in range(cells // QUERY_BLOCK):
            rows = slice(block * QUERY_BLOCK, (block + 1) * QUERY_BLOCK)
            queries = qkv[rows, columns(0, h)]
            scores = mm(queries, keys, NT)
            raised = jnp.exp2(scores - jnp.max(scores, axis=-1, keepdims=True))
            raised_b = raised.astype(BF)
            sums = mm(raised_b, values_ones)
            inverse = 1.0 / sums[:, HEAD:]
            result = sums[:, :HEAD] * inverse
            attended[rows, columns(0, h)] = result.astype(BF)
            scaled = grad_att[rows, columns(0, h)].astype(F32) * inverse
            inner = jnp.sum(scaled * result, axis=-1, keepdims=True)
            scaled_b = scaled.astype(BF)
            grad_probs = mm(scaled_b, values, NT)
            grad_scores = (raised * (grad_probs - inner)).astype(BF)
            grad_cells[rows, columns(0, h)] = (mm(grad_scores, keys) * factor).astype(BF)
            new_keys = mm(queries.T, grad_scores)
            new_values = mm(scaled_b.T, raised_b)
            if block == 0:
                sum_keys[...] = new_keys
                sum_values[...] = new_values
            else:
                sum_keys[...] += new_keys
                sum_values[...] += new_values
        grad_cells[:, columns(1, h)] = (sum_keys[...] * (1.0 / log2e)).T.astype(BF)
        grad_cells[:, columns(2, h)] = sum_values[...].T.astype(BF)
        return carry

    lax.fori_loop(0, HEADS, head, 0)
    enhanced[...] = (hidden_f + mm(attended[...], out_w[...])).astype(BF)
    grad_normed = mm(grad_cells[...], qkv_w[...], NT)
    normed_f = hidden_f * inv_rms
    mixing = jnp.mean(grad_normed * normed_f, axis=-1, keepdims=True)
    grad_hidden[...] = (
        cotangent[...].astype(F32) + inv_rms * (grad_normed - normed_f * mixing)
    ).astype(BF)
    grad_qkv[...] = (mm(normed, grad_cells[...], TN) * (1.0 / 512)).astype(BF)
    grad_out[...] = (mm(attended[...], cotangent[...], TN) * (1.0 / 512)).astype(BF)


def halos(tile):
    frames, bins, _ = tile.shape
    size = lax.axis_size("tm")
    forward = [(i, i + 1) for i in range(size - 1)]
    back = [(i + 1, i) for i in range(size - 1)]
    up = lax.ppermute(tile[frames - 1 :], "tm", forward)
    down = lax.ppermute(tile[:1], "tm", back)
    size = lax.axis_size("freq")
    forward = [(i, i + 1) for i in range(size - 1)]
    back = [(i + 1, i) for i in range(size - 1)]
    last = jnp.concatenate([up[:, -1:], tile[:, -1:], down[:, -1:]], axis=0)
    first = jnp.concatenate([up[:, :1], tile[:, :1], down[:, :1]], axis=0)
    left = lax.ppermute(last, "freq", forward)
    right = lax.ppermute(first, "freq", back)
    return up, down, left, right


def reduce_share(terms):
    tm, freq = lax.axis_size("tm"), lax.axis_size("freq")
    n = terms.shape[-1]
    grouped = terms.reshape(tm, freq, n).transpose(1, 0, 2)
    came = lax.all_to_all(grouped, "freq", split_axis=0, concat_axis=0, tiled=True)
    part = jnp.sum(came.astype(F32), axis=0).astype(BF)
    part = part.reshape(tm, n // 128, 128)
    came = lax.all_to_all(part, "tm", split_axis=0, concat_axis=0, tiled=True)
    return jnp.sum(came.astype(F32), axis=0).reshape(n)


def shards(spectrum, conv_weight, qkv_weight, out_weight, cotangent):
    frames, bins, width = spectrum.shape
    cells = frames * bins
    conv_cost = (2 * 9 * cells * width * width, 6 * 2**20)
    up, down, left, right = halos(spectrum)
    hidden, slope, stacked = vmem_call(
        conv_forward_body,
        (shape((cells, width)), shape((cells, width), F32), shape((frames + 2, bins, 3 * width))),
        [pltpu.VMEM((3, 3 * width, width), BF)],
        "conv_forward",
        conv_cost,
    )(spectrum, up, down, left, right, conv_weight)
    hidden = hidden.reshape(frames, bins, width)
    frame = lax.all_to_all(hidden, "freq", split_axis=0, concat_axis=0, tiled=True)
    frame = frame.reshape(cells, width)
    wide = HEADS * HEAD
    enhanced, grad_frame, grad_qkv, grad_out = vmem_call(
        attend_body,
        (
            shape((cells, width)),
            shape((cells, width)),
            shape((width, 3 * wide)),
            shape((wide, width)),
        ),
        [
            pltpu.VMEM((cells, 3 * wide), BF),
            pltpu.VMEM((cells, wide), BF),
            pltpu.VMEM((cells, wide), BF),
            pltpu.VMEM((cells, 3 * wide), BF),
            pltpu.VMEM((HEAD, cells), F32),
            pltpu.VMEM((HEAD, cells), F32),
        ],
        "attend",
        (16 * 10**9, 6 * 2**20),
    )(frame, cotangent.reshape(cells, width), qkv_weight, out_weight)
    grad_frame = grad_frame.reshape(frames, bins, width)
    grad_hidden = lax.all_to_all(grad_frame, "freq", split_axis=0, concat_axis=0, tiled=True)
    ranks = lax.axis_size("tm") * lax.axis_size("freq")
    terms = jnp.concatenate([grad_qkv.reshape(ranks, -1), grad_out.reshape(ranks, -1)], axis=1)
    share = reduce_share(terms)
    cut = grad_qkv.size // ranks
    grad_conv_out, grad_weight = vmem_call(
        functools.partial(conv_weight_body, frames),
        (shape((frames, bins, width)), shape(conv_weight.shape, F32)),
        [],
        "conv_weight_grad",
        conv_cost,
    )(grad_hidden, slope, stacked)
    conv_share = reduce_share(grad_weight.astype(BF).reshape(ranks, -1))
    up, down, left, right = halos(grad_conv_out)
    grad_spectrum = vmem_call(
        conv_data_body,
        shape((frames, bins, width)),
        [
            pltpu.VMEM((frames + 2, bins, 3 * width), BF),
            pltpu.VMEM((3, width, 3 * width), BF),
        ],
        "conv_data_grad",
        conv_cost,
    )(grad_conv_out, up, down, left, right, conv_weight, grad_hidden)
    return (
        enhanced.reshape(1, cells, width),
        grad_spectrum,
        conv_share,
        share[:cut],
        share[cut:],
    )


def solution(mesh):
    placed = (P("tm", "freq", None), P(), P(), P(), P(("tm", "freq"), None, None))
    return jax.shard_map(
        shards,
        mesh=mesh,
        in_specs=placed,
        out_specs=(
            P(("tm", "freq"), None, None),
            P("tm", "freq", None),
            P(("tm", "freq")),
            P(("tm", "freq")),
            P(("tm", "freq")),
        ),
        check_vma=False,
    )
```

time: 461 us -> 148 us (0.32)
  waiting for transfers between devices: 267 us -> 38.3 us
  matrix products: 78.5 us -> 0 us
  local copies, waits for them, and re-layouts: 49.8 us -> 9.57 us
  blocking collectives: 0 us -> 29 us
  Pallas kernels: 0 us -> 26.3 us
  between operations: 14.6 us -> 0.93 us
  other arithmetic: 16 us -> 2.95 us
  starting transfers between devices: 30.9 us -> 39.3 us
    unnamed x2 -> x0, waiting for transfers between devices: 259 us -> none
    dot_general x33 -> x0, matrix products: 78.5 us -> none  [the longest x4 15.2 us: head_pass(): jnp.dot(probs_b, values, preferred_element_type=jnp.float32)]
    all_to_all x0 -> x2, blocking collectives: none -> 29 us  [the longest x1 16.2 us: shards(): lax.all_to_all(hidden, 'freq', split_axis=0, concat_axis=0, tiled=True)]
    all_to_all x2 -> x4, waiting for transfers between devices: 0.63 us -> 27.5 us  [the longest x2 17.3 us: reduce_share(): lax.all_to_all(grouped, 'freq', split_axis=0, concat_axis=0, tiled=True)]
    pallas_call x0 -> x4, Pallas kernels: none -> 26.3 us  [run(): pl.pallas_call(body, out_shape=out_shape, in_specs=[pl.BlockSpec(memory_s...]
    reshape x5 -> x1, local copies, waits for them, and re-layouts: 18.9 us -> 0.7 us  [reduce_share(): part = part.reshape(tm, n // 128, 128)]
    dynamic_update_slice x24 -> x0, local copies, waits for them, and re-layouts: 12.8 us -> none  [frame_pass(): lax.map(head_pass, (split_qkv[0], split_qkv[1], split_qkv[2], grad_split))]
    all_to_all x2 -> x4, starting transfers between devices: 10.8 us -> 21.8 us  [the longest x2 14.7 us: reduce_share(): came = lax.all_to_all(part, 'tm', split_axis=0, concat_axis=0, tiled=True)]
  transfers between devices with their start and end apart: 11 -> 12, of which waited for: 5 -> 7; matrix products, arithmetic and copies ran while one was open for 7% -> 4% of each run, Pallas kernels for 0% -> 2%
where the time goes in v1:
time: 148 us; the launch traced here: 146 us
  starting transfers between devices  39.3 us (27%)
  waiting for transfers between devices  38.3 us (26%)
  blocking collectives  29 us (20%)
  Pallas kernels  26.3 us (18%)
  local copies, waits for them, and re-layouts  9.57 us (6%)
  other arithmetic  2.95 us (2%)
    pallas_call x4, Pallas kernels, run(): pl.pallas_call(body, out_shape=out_shape, in_specs=[pl.BlockSpec(memory_s...  26.3 us
    all_to_all x2, waiting for transfers between devices, reduce_share(): lax.all_to_all(grouped, 'freq', split_axis=0, concat_axis=0, tiled=True)  17.3 us
    all_to_all x1, blocking collectives, shards(): lax.all_to_all(hidden, 'freq', split_axis=0, concat_axis=0, tiled=True)  16.2 us
    all_to_all x2, starting transfers between devices, reduce_share(): came = lax.all_to_all(part, 'tm', split_axis=0, concat_axis=0, tiled=True)  14.7 us
    all_to_all x1, blocking collectives, shards(): lax.all_to_all(grad_frame, 'freq', split_axis=0, concat_axis=0, tiled=True)  12.8 us
    all_to_all x2, waiting for transfers between devices, reduce_share(): came = lax.all_to_all(part, 'tm', split_axis=0, concat_axis=0, tiled=True)  10.3 us
    all_to_all x2, starting transfers between devices, reduce_share(): lax.all_to_all(grouped, 'freq', split_axis=0, concat_axis=0, tiled=True)  7.09 us
    ppermute x2, starting transfers between devices, halos(): down = lax.ppermute(tile[:1], 'tm', back)  6.52 us
  transfers between devices with their start and end apart: 12, of which 7 were waited for; matrix products, arithmetic and copies ran while one was open for 4% of the time, Pallas kernels for 2%

profile of v1, /device:TPU:32, one launch (start us, length us, event | category | flops | bytes accessed | tf_op | source)
XLA Modules:
  0.0 146.4 jit_solution(1549898507745358130)
XLA Ops:
  0.6 0.9 fusion.3
  1.5 4.5 %collective-permute-start.1 = (bf16[1,128,256]{2,1,0:T(8,128)(2,1)S(1)}, bf16[1,128,256]{2,1,0:T(8,128)(2,1)S(1)}, u32[]{:S(2)}, u32[]{:S(2)}) collective-permute-start(bf16[1,128,256]{2,1,0:T(8,128)(2,1)S(1)} %get-tuple-element.29), channel_id=1, source_target_pairs={{8,0},{16,8},{24,16},{32,24},{40,32},{48,40},{56,48},{64,56},{72,6... | collective-permute-start | bytes 196616 | tf_op jit(solution)/shard_map/ppermute | solution.py:188
  6.0 1.9 %collective-permute-start = (bf16[1,128,256]{2,1,0:T(8,128)(2,1)S(1)}, bf16[1,128,256]{2,1,0:T(8,128)(2,1)S(1)}, u32[]{:S(2)}, u32[]{:S(2)}) collective-permute-start(bf16[1,128,256]{2,1,0:T(8,128)(2,1)S(1)} %get-tuple-element.30), channel_id=1, source_target_pairs={{0,8},{8,16},{16,24},{24,32},{32,40},{40,48},{48,56},{56,64},{64,7... | collective-permute-start | bytes 196616 | tf_op jit(solution)/shard_map/ppermute | solution.py:187
  7.9 0.8 fusion.2
  8.7 5.5 %collective-permute-done.up = bf16[1,128,256]{2,1,0:T(8,128)(2,1)S(1)} collective-permute-done((bf16[1,128,256]{2,1,0:T(8,128)(2,1)S(1)}, bf16[1,128,256]{2,1,0:T(8,128)(2,1)S(1)}, u32[]{:S(2)}, u32[]{:S(2)}) %collective-permute-start) | collective-permute-done | bytes 65568 | tf_op jit(solution)/shard_map/ppermute | solution.py:187
  14.3 1.3 collective-permute-start.2
  15.6 1.3 collective-permute-start.3
  16.9 3.5 %collective-permute-done.3.right = bf16[10,1,256]{2,1,0:T(2,128)(2,1)S(1)} collective-permute-done((bf16[10,1,256]{2,1,0:T(2,128)(2,1)S(1)}, bf16[10,1,256]{2,1,0:T(2,128)(2,1)S(1)}, u32[]{:S(2)}, u32[]{:S(2)}) %collective-permute-start.3) | collective-permute-done | bytes 5152 | tf_op jit(solution)/shard_map/ppermute | solution.py:195
  20.4 1.0 copy-done
  21.5 1.1 copy-done.2
  22.5 1.8 %conv_forward.1 = (bf16[1024,256]{1,0:T(8,128)(2,1)S(1)}, f32[1024,256]{1,0:T(8,128)S(1)}, bf16[10,128,768]{2,1,0:T(8,128)(2,1)S(1)}) custom-call(bf16[8,128,256]{2,1,0:T(8,128)(2,1)S(1)} %copy-done, bf16[1,128,256]{2,1,0:T(8,128)(2,1)S(1)} %collective-permute-done.up, bf16[1,128,256]{2,1,0:T(8,128)(2,1)S(1)} %collective-permute-done.1.down, ...), custom_call_target="tpu_custom_call" | custom-call | flops 1207959552 | bytes 6291456 | tf_op jit(solution)/shard_map/conv_forward/pallas_call | solution.py:27
  24.4 16.2 %all_to_all.30 = bf16[8,128,256]{2,1,0:T(8,128)(2,1)S(1)} all-to-all(bf16[8,128,256]{2,1,0:T(8,128)(2,1)S(1)} %bitcast.21), channel_id=1, replica_groups=mesh['tm'=32,'freq'=8] {'freq'}, dimensions={0} | all-to-all | bytes 1048576 | tf_op jit(solution)/shard_map/all_to_all | solution.py:223
  40.6 20.6 %attend.1 = (bf16[1024,256]{1,0:T(8,128)(2,1)}, bf16[1024,256]{1,0:T(8,128)(2,1)S(1)}, bf16[256,1536]{1,0:T(8,128)(2,1)S(1)}, bf16[512,256]{1,0:T(8,128)(2,1)S(1)}) custom-call(bf16[1024,256]{1,0:T(8,128)(2,1)S(1)} %bitcast.22, bf16[1024,256]{1,0:T(8,128)(2,1)S(1)} %bitcast.24, bf16[256,1536]{1,0:T(8,128)(2,1)S(1)} %copy-done.1, bf16[512,256]{1,0:T(8,128)(2,1)S(1)} %copy-done.5), custom_call_target="tpu_custom_call" | custom-call | flops 16000000000 | bytes 6291456 | tf_op jit(solution)/shard_map/attend/pallas_call | solution.py:27
  61.2 12.8 %all_to_all.31.grad_hidden = bf16[8,128,256]{2,1,0:T(8,128)(2,1)S(1)} all-to-all(bf16[8,128,256]{2,1,0:T(8,128)(2,1)S(1)} %bitcast.23), channel_id=1, replica_groups=mesh['tm'=32,'freq'=8] {'freq'}, dimensions={0} | all-to-all | bytes 1048576 | tf_op jit(solution)/shard_map/all_to_all | solution.py:246
  74.0 1.6 %conv_weight_grad.1 = (bf16[8,128,256]{2,1,0:T(8,128)(2,1)S(1)}, f32[2,3,3,128,128]{4,3,2,1,0:T(8,128)S(1)}) custom-call(bf16[8,128,256]{2,1,0:T(8,128)(2,1)S(1)} %all_to_all.31.grad_hidden, f32[1024,256]{1,0:T(8,128)S(1)} %get-tuple-element.17.slope, bf16[10,128,768]{2,1,0:T(8,128)(2,1)S(1)} %get-tuple-element.18.stacked), custom_call_target="tpu_custom_call" | custom-call | flops 1207959552 | bytes 6291456 | tf_op jit(solution)/shard_map/conv_weight_grad/pallas_call | solution.py:27
  76.4 0.9 copy.18
  77.3 3.5 %all-to-all-start.2 = ((bf16[8,32,1152]{2,1,0:T(8,128)(2,1)}), bf16[8,32,1152]{2,1,0:T(8,128)(2,1)S(1)}, u32[]{:S(2)}, u32[]{:S(2)}) async-start(bf16[8,32,1152]{2,1,0:T(8,128)(2,1)} %bitcast.19), calls=%async_computation.2 | async-start | bytes 1179648 | tf_op jit(solution)/shard_map/all_to_all | solution.py:203
  81.3 1.1 maximum_bitcast_fusion
  82.4 9.4 %all-to-all-done.2 = bf16[8,32,1152]{2,1,0:T(8,128)(2,1)S(1)} async-done(((bf16[8,32,1152]{2,1,0:T(8,128)(2,1)}), bf16[8,32,1152]{2,1,0:T(8,128)(2,1)S(1)}, u32[]{:S(2)}, u32[]{:S(2)}) %all-to-all-start.2) | async-done | bytes 589856 | tf_op jit(solution)/shard_map/all_to_all | solution.py:203
  91.8 3.6 %all-to-all-start.4 = ((bf16[8,32,2048]{2,1,0:T(8,128)(2,1)}), bf16[8,32,2048]{2,1,0:T(8,128)(2,1)S(1)}, u32[]{:S(2)}, u32[]{:S(2)}) async-start(bf16[8,32,2048]{2,1,0:T(8,128)(2,1)} %maximum_bitcast_fusion), calls=%async_computation.4 | async-start | bytes 2097152 | tf_op jit(solution)/shard_map/all_to_all | solution.py:203
  95.4 2.1 %collective-permute-start.5 = (bf16[1,128,256]{2,1,0:T(8,128)(2,1)S(1)}, bf16[1,128,256]{2,1,0:T(8,128)(2,1)S(1)}, u32[]{:S(2)}, u32[]{:S(2)}) collective-permute-start(bf16[1,128,256]{2,1,0:T(8,128)(2,1)S(1)} %get-tuple-element.25), channel_id=1, source_target_pairs={{8,0},{16,8},{24,16},{32,24},{40,32},{48,40},{56,48},{64,56},{72,6... | collective-permute-start | bytes 196616 | tf_op jit(solution)/shard_map/ppermute | solution.py:188
  98.1 3.9 %collective-permute-start.4 = (bf16[1,128,256]{2,1,0:T(8,128)(2,1)S(1)}, bf16[1,128,256]{2,1,0:T(8,128)(2,1)S(1)}, u32[]{:S(2)}, u32[]{:S(2)}) collective-permute-start(bf16[1,128,256]{2,1,0:T(8,128)(2,1)S(1)} %get-tuple-element.26), channel_id=1, source_target_pairs={{0,8},{8,16},{16,24},{24,32},{32,40},{40,48},{48,56},{56,64},{64,7... | collective-permute-start | bytes 196616 | tf_op jit(solution)/shard_map/ppermute | solution.py:187
  103.4 7.9 %all-to-all-done.4 = bf16[8,32,2048]{2,1,0:T(8,128)(2,1)S(1)} async-done(((bf16[8,32,2048]{2,1,0:T(8,128)(2,1)}), bf16[8,32,2048]{2,1,0:T(8,128)(2,1)S(1)}, u32[]{:S(2)}, u32[]{:S(2)}) %all-to-all-start.4) | async-done | bytes 1048608 | tf_op jit(solution)/shard_map/all_to_all | solution.py:203
  111.3 9.9 %all-to-all-start.3 = ((bf16[32,9,128]{2,1,0:T(8,128)(2,1)}), bf16[32,9,128]{2,1,0:T(8,128)(2,1)S(1)}, u32[]{:S(2)}, u32[]{:S(2)}) async-start(bf16[32,9,128]{2,1,0:T(8,128)(2,1)} %reshape.47), calls=%async_computation.3 | async-start | bytes 262144 | tf_op jit(solution)/shard_map/all_to_all | solution.py:206
  121.3 0.7 pad_maximum_fusion.2
  122.0 1.3 collective-permute-start.6
  124.1 6.7 %all-to-all-done.3 = bf16[32,9,128]{2,1,0:T(8,128)(2,1)S(1)} async-done(((bf16[32,9,128]{2,1,0:T(8,128)(2,1)}), bf16[32,9,128]{2,1,0:T(8,128)(2,1)S(1)}, u32[]{:S(2)}, u32[]{:S(2)}) %all-to-all-start.3) | async-done | bytes 73760 | tf_op jit(solution)/shard_map/all_to_all | solution.py:206
  130.8 4.7 %all-to-all-start.5 = ((bf16[32,16,128]{2,1,0:T(8,128)(2,1)}), bf16[32,16,128]{2,1,0:T(8,128)(2,1)S(1)}, u32[]{:S(2)}, u32[]{:S(2)}) async-start(bf16[32,16,128]{2,1,0:T(8,128)(2,1)} %bitcast.13), calls=%async_computation.5 | async-start | bytes 262144 | tf_op jit(solution)/shard_map/all_to_all | solution.py:206
  135.6 1.3 collective-permute-start.7
  136.9 1.8 %collective-permute-done.7.right = bf16[10,1,256]{2,1,0:T(2,128)(2,1)S(1)} collective-permute-done((bf16[10,1,256]{2,1,0:T(2,128)(2,1)S(1)}, bf16[10,1,256]{2,1,0:T(2,128)(2,1)S(1)}, u32[]{:S(2)}, u32[]{:S(2)}) %collective-permute-start.7) | collective-permute-done | bytes 5152 | tf_op jit(solution)/shard_map/ppermute | solution.py:195
  138.7 2.3 %conv_data_grad.1 = bf16[8,128,256]{2,1,0:T(8,128)(2,1)} custom-call(bf16[8,128,256]{2,1,0:T(8,128)(2,1)S(1)} %get-tuple-element.19.mid, bf16[1,128,256]{2,1,0:T(8,128)(2,1)S(1)} %collective-permute-done.4.up, bf16[1,128,256]{2,1,0:T(8,128)(2,1)S(1)} %collective-permute-done.5.down, bf16[10,1,256]{2,1,0:T(2,128)(2,1)S(1)} %collective-permute-done.6.left, ...), custom_call_target="tpu_custom_call" | custom-call | flops 1207959552 | bytes 6291456 | tf_op jit(solution)/shard_map/conv_data_grad/pallas_call | solution.py:27
  141.6 3.6 %all-to-all-done.5 = bf16[32,16,128]{2,1,0:T(8,128)(2,1)S(1)} async-done(((bf16[32,16,128]{2,1,0:T(8,128)(2,1)}), bf16[32,16,128]{2,1,0:T(8,128)(2,1)S(1)}, u32[]{:S(2)}, u32[]{:S(2)}) %all-to-all-start.5) | async-done | bytes 131104 | tf_op jit(solution)/shard_map/all_to_all | solution.py:206
  (39 shorter events, 6.0 us)
Async XLA Ops:
  1.5 7.2 %collective-permute-start.1 = (bf16[1,128,256]{2,1,0:T(8,128)(2,1)S(1)}, bf16[1,128,256]{2,1,0:T(8,128)(2,1)S(1)}, u32[]{:S(2)}, u32[]{:S(2)}) collective-permute-start(bf16[1,128,256]{2,1,0:T(8,128)(2,1)S(1)} %get-tuple-element.29), channel_id=1, source_target_pairs={{8,0},{16,8},{24,16},{32,24},{40,32},{48,40},{56,48},{64,56},{72,6... | collective-permute-start | bytes 196616 | tf_op jit(solution)/shard_map/ppermute | solution.py:188
  6.0 8.3 %collective-permute-start = (bf16[1,128,256]{2,1,0:T(8,128)(2,1)S(1)}, bf16[1,128,256]{2,1,0:T(8,128)(2,1)S(1)}, u32[]{:S(2)}, u32[]{:S(2)}) collective-permute-start(bf16[1,128,256]{2,1,0:T(8,128)(2,1)S(1)} %get-tuple-element.30), channel_id=1, source_target_pairs={{0,8},{8,16},{16,24},{24,32},{32,40},{40,48},{48,56},{56,64},{64,7... | collective-permute-start | bytes 196616 | tf_op jit(solution)/shard_map/ppermute | solution.py:187
  14.3 2.6 %collective-permute-start.2 = (bf16[10,1,256]{2,1,0:T(2,128)(2,1)S(1)}, bf16[10,1,256]{2,1,0:T(2,128)(2,1)S(1)}, u32[]{:S(2)}, u32[]{:S(2)}) collective-permute-start(bf16[10,1,256]{2,1,0:T(2,128)(2,1)S(1)} %pad_maximum_fusion), channel_id=1, source_target_pairs={{0,1},{1,2},{2,3},{3,4},{4,5},{5,6},{6,7},{8,9},{9,10},{10,11},{11... | collective-permute-start | bytes 15368 | tf_op jit(solution)/shard_map/ppermute | solution.py:194
  15.6 4.8 %collective-permute-start.3 = (bf16[10,1,256]{2,1,0:T(2,128)(2,1)S(1)}, bf16[10,1,256]{2,1,0:T(2,128)(2,1)S(1)}, u32[]{:S(2)}, u32[]{:S(2)}) collective-permute-start(bf16[10,1,256]{2,1,0:T(2,128)(2,1)S(1)} %pad_maximum_fusion.1), channel_id=1, source_target_pairs={{1,0},{2,1},{3,2},{4,3},{5,4},{6,5},{7,6},{9,8},{10,9},{11,10},{12... | collective-permute-start | bytes 15368 | tf_op jit(solution)/shard_map/ppermute | solution.py:195
  20.4 1.0 copy-start
  21.5 1.1 copy-start.2
  22.5 18.1 %copy-start.1 = (bf16[256,1536]{1,0:T(8,128)(2,1)S(1)}, bf16[256,1536]{1,0:T(8,128)(2,1)}, u32[]{:S(2)}) copy-start(bf16[256,1536]{1,0:T(8,128)(2,1)} %qkv_w.1) | copy-start | bytes 2359300
  22.5 18.1 %copy-start.4 = (bf16[1,1024,256]{2,1,0:T(8,128)(2,1)S(1)}, bf16[1,1024,256]{2,1,0:T(8,128)(2,1)}, u32[]{:S(2)}) copy-start(bf16[1,1024,256]{2,1,0:T(8,128)(2,1)} %param.9) | copy-start | bytes 1572868
  22.5 18.1 %copy-start.5 = (bf16[512,256]{1,0:T(8,128)(2,1)S(1)}, bf16[512,256]{1,0:T(8,128)(2,1)}, u32[]{:S(2)}) copy-start(bf16[512,256]{1,0:T(8,128)(2,1)} %out_w.1) | copy-start | bytes 786436
  77.3 14.5 %all-to-all-start.2 = ((bf16[8,32,1152]{2,1,0:T(8,128)(2,1)}), bf16[8,32,1152]{2,1,0:T(8,128)(2,1)S(1)}, u32[]{:S(2)}, u32[]{:S(2)}) async-start(bf16[8,32,1152]{2,1,0:T(8,128)(2,1)} %bitcast.19), calls=%async_computation.2 | async-start | bytes 1179648 | tf_op jit(solution)/shard_map/all_to_all | solution.py:203
  91.8 19.4 %all-to-all-start.4 = ((bf16[8,32,2048]{2,1,0:T(8,128)(2,1)}), bf16[8,32,2048]{2,1,0:T(8,128)(2,1)S(1)}, u32[]{:S(2)}, u32[]{:S(2)}) async-start(bf16[8,32,2048]{2,1,0:T(8,128)(2,1)} %maximum_bitcast_fusion), calls=%async_computation.4 | async-start | bytes 2097152 | tf_op jit(solution)/shard_map/all_to_all | solution.py:203
  95.4 43.2 %copy-start.3 = (bf16[2,3,3,128,128]{4,3,2,1,0:T(8,128)(2,1)S(1)}, bf16[2,3,3,128,128]{4,3,2,1,0:T(8,128)(2,1)}, u32[]{:S(2)}) copy-start(bf16[2,3,3,128,128]{4,3,2,1,0:T(8,128)(2,1)} %weight.3) | copy-start | bytes 1769476
  95.4 6.6 %collective-permute-start.5 = (bf16[1,128,256]{2,1,0:T(8,128)(2,1)S(1)}, bf16[1,128,256]{2,1,0:T(8,128)(2,1)S(1)}, u32[]{:S(2)}, u32[]{:S(2)}) collective-permute-start(bf16[1,128,256]{2,1,0:T(8,128)(2,1)S(1)} %get-tuple-element.25), channel_id=1, source_target_pairs={{8,0},{16,8},{24,16},{32,24},{40,32},{48,40},{56,48},{64,56},{72,6... | collective-permute-start | bytes 196616 | tf_op jit(solution)/shard_map/ppermute | solution.py:188
  98.1 23.1 %collective-permute-start.4 = (bf16[1,128,256]{2,1,0:T(8,128)(2,1)S(1)}, bf16[1,128,256]{2,1,0:T(8,128)(2,1)S(1)}, u32[]{:S(2)}, u32[]{:S(2)}) collective-permute-start(bf16[1,128,256]{2,1,0:T(8,128)(2,1)S(1)} %get-tuple-element.26), channel_id=1, source_target_pairs={{0,8},{8,16},{16,24},{24,32},{32,40},{40,48},{48,56},{56,64},{64,7... | collective-permute-start | bytes 196616 | tf_op jit(solution)/shard_map/ppermute | solution.py:187
  102.7 32.8 %copy-start.6 = (bf16[1,1,256]{2,1,0:T(2,128)(2,1)S(1)}, bf16[1,1,256]{2,1,0:T(2,128)(2,1)}, u32[]{:S(2)}) copy-start(bf16[1,1,256]{2,1,0:T(2,128)(2,1)} %get-tuple-element.33) | copy-start | bytes 1540
  111.3 19.5 %all-to-all-start.3 = ((bf16[32,9,128]{2,1,0:T(8,128)(2,1)}), bf16[32,9,128]{2,1,0:T(8,128)(2,1)S(1)}, u32[]{:S(2)}, u32[]{:S(2)}) async-start(bf16[32,9,128]{2,1,0:T(8,128)(2,1)} %reshape.47), calls=%async_computation.3 | async-start | bytes 262144 | tf_op jit(solution)/shard_map/all_to_all | solution.py:206
  122.0 14.9 %collective-permute-start.6 = (bf16[10,1,256]{2,1,0:T(2,128)(2,1)S(1)}, bf16[10,1,256]{2,1,0:T(2,128)(2,1)S(1)}, u32[]{:S(2)}, u32[]{:S(2)}) collective-permute-start(bf16[10,1,256]{2,1,0:T(2,128)(2,1)S(1)} %pad_maximum_fusion.2), channel_id=1, source_target_pairs={{0,1},{1,2},{2,3},{3,4},{4,5},{5,6},{6,7},{8,9},{9,10},{10,11},{11... | collective-permute-start | bytes 15368 | tf_op jit(solution)/shard_map/ppermute | solution.py:194
  130.8 14.4 %all-to-all-start.5 = ((bf16[32,16,128]{2,1,0:T(8,128)(2,1)}), bf16[32,16,128]{2,1,0:T(8,128)(2,1)S(1)}, u32[]{:S(2)}, u32[]{:S(2)}) async-start(bf16[32,16,128]{2,1,0:T(8,128)(2,1)} %bitcast.13), calls=%async_computation.5 | async-start | bytes 262144 | tf_op jit(solution)/shard_map/all_to_all | solution.py:206
  135.6 3.1 %collective-permute-start.7 = (bf16[10,1,256]{2,1,0:T(2,128)(2,1)S(1)}, bf16[10,1,256]{2,1,0:T(2,128)(2,1)S(1)}, u32[]{:S(2)}, u32[]{:S(2)}) collective-permute-start(bf16[10,1,256]{2,1,0:T(2,128)(2,1)S(1)} %pad_maximum_fusion.3), channel_id=1, source_target_pairs={{1,0},{2,1},{3,2},{4,3},{5,4},{6,5},{7,6},{9,8},{10,9},{11,10},{12... | collective-permute-start | bytes 15368 | tf_op jit(solution)/shard_map/ppermute | solution.py:195

commit v2 on v0

v2 whole, which is shorter than its diff:
```python
import math

import jax
import jax.numpy as jnp
from jax import lax
from jax.experimental import pallas as pl
from jax.experimental.pallas import tpu as pltpu
from jax.sharding import PartitionSpec as P

HEADS = 4
HEAD = 128
EARLY = 3
EXTRA = 16
SCALE = 1.0 / 512
LOG2E = math.log2(math.e)
FACTOR = 1.0 / math.sqrt(HEAD)
BF = jnp.bfloat16
F32 = jnp.float32
NN = (((1,), (0,)), ((), ()))
NT = (((1,), (1,)), ((), ()))
QUERY_BLOCK = 512


def mm(a, b, dims=NN):
    return lax.dot_general(a, b, dims, preferred_element_type=F32)


def kernel_call(body, name, outs, *args, scratch=(), mflops=0, limit=48):
    outs = [jax.ShapeDtypeStruct(dims, kind) for dims, kind in outs]
    size = sum(a.size * a.dtype.itemsize for a in (*args, *outs))
    return pl.pallas_call(
        body,
        out_shape=outs,
        in_specs=[pl.BlockSpec(memory_space=pltpu.VMEM)] * len(args),
        out_specs=[pl.BlockSpec(memory_space=pltpu.VMEM)] * len(outs),
        scratch_shapes=list(scratch),
        compiler_params=pltpu.CompilerParams(vmem_limit_bytes=limit * 2**20),
        cost_estimate=pl.CostEstimate(
            flops=mflops * 10**6, bytes_accessed=size, transcendentals=0
        ),
        name=name,
    )(*args)


def sigmoid(v):
    return 1.0 / (1.0 + jnp.exp(-v))


def slope_of(v, sigma):
    return sigma * (1.0 + v * (1.0 - sigma))


def moved_down(rows):
    at = lax.broadcasted_iota(jnp.int32, rows.shape, 0)
    return jnp.where(at == 0, 0.0, pltpu.roll(rows, 1, 0))


def moved_up(rows):
    last = rows.shape[0] - 1
    at = lax.broadcasted_iota(jnp.int32, rows.shape, 0)
    return jnp.where(at == last, 0.0, pltpu.roll(rows, last, 0))


def with_borders(inner, first, last):
    at = lax.broadcasted_iota(jnp.int32, inner.shape, 1)
    inner = jnp.where(at == 0, first[:, None, :], inner)
    return jnp.where(at == inner.shape[1] - 1, last[:, None, :], inner)


def bins_before(rows, left):
    at = lax.broadcasted_iota(jnp.int32, rows.shape, 1)
    return jnp.where(at == 0, left, pltpu.roll(rows, 1, 1))


def bins_after(rows, right):
    last = rows.shape[1] - 1
    at = lax.broadcasted_iota(jnp.int32, rows.shape, 1)
    return jnp.where(at == last, right, pltpu.roll(rows, last, 1))


def conv_own_body(mid, weight, conv, borders, matrix, matrix_back, stacked):
    frames, bins, width = mid.shape
    half = width // 2
    wide = mid[...].astype(F32)
    stacked[:, :, :width] = bins_before(wide, 0.0).astype(BF)
    stacked[:, :, width : 2 * width] = mid[...]
    stacked[:, :, 2 * width :] = bins_after(wide, 0.0).astype(BF)
    for i in range(3):
        for j in range(3):
            real, imag = weight[0, i, j], weight[1, i, j]
            at = j * width
            matrix[i, at : at + half, :half] = real
            matrix[i, at : at + half, half:] = imag
            matrix[i, at + half : at + width, :half] = -imag
            matrix[i, at + half : at + width, half:] = real
            matrix_back[i, :half, at : at + half] = real
            matrix_back[i, :half, at + half : at + width] = imag
            matrix_back[i, half:, at : at + half] = -imag
            matrix_back[i, half:, at + half : at + width] = real
    inner = (frames - 1) * bins
    everything = stacked[...].reshape(frames * bins, 3 * width)
    conv[...] = mm(everything, matrix[1])
    conv[bins:] += mm(everything[:inner], matrix[0])
    conv[:inner] += mm(everything[bins:], matrix[2])
    borders[0] = mid[:, 0, :].astype(F32)
    borders[1] = mid[:, bins - 1, :].astype(F32)


def conv_finish_body(mid, up, down, own, borders, matrix, payload, slope, conv, pieces):
    frames, bins, width = mid.shape
    cells = frames * bins

    def stack(row):
        wide = row[...].astype(F32)
        before = bins_before(wide, 0.0).astype(BF)
        after = bins_after(wide, 0.0).astype(BF)
        return jnp.concatenate([before[0], row[0], after[0]], axis=1)

    conv[...] = own[...].reshape(frames, bins, width)
    conv[0] += mm(stack(up), matrix[0])
    conv[frames - 1] += mm(stack(down), matrix[2])

    def beyond(bin_at, side, tap):
        rows = jnp.concatenate(
            [up[:, bin_at, :].astype(F32), borders[side], down[:, bin_at, :].astype(F32)], axis=0
        )
        total = None
        for i in range(3):
            term = mm(
                rows[i : i + frames].astype(BF), matrix[i, tap * width : (tap + 1) * width, :]
            )
            total = term if total is None else total + term
        return total

    parts = (
        beyond(0, 0, 2),
        conv[:, 0, :],
        conv[:, bins - 1, :],
        beyond(bins - 1, 1, 0),
    )
    pieces[...] = jnp.zeros(pieces.shape, F32)
    for at, part in enumerate(parts):
        high = part.astype(BF).astype(F32)
        pieces[:, 2 * at, :] = high
        pieces[:, 2 * at + 1, :] = part - high
    values = conv[...]
    sigma = sigmoid(values)
    slope[...] = slope_of(values, sigma)
    hidden = mid[...].astype(F32) + values * sigma
    payload[:, :bins, :] = with_borders(hidden, borders[0], borders[1]).astype(BF)
    payload[:, bins:, :] = pieces[...].astype(BF)


def prepare_body(mid, up, down, cotangent, out_w, turned, grad_att):
    frames, bins, width = mid.shape
    turned[:, :bins] = up[0].T
    turned[:, bins : (frames + 1) * bins] = mid[...].reshape(frames * bins, width).T
    turned[:, (frames + 1) * bins :] = down[0].T
    grad_att[...] = mm(cotangent[...], out_w[...], NT).astype(BF)


def columns(part, h):
    at = part * HEADS * HEAD + h * HEAD
    if not isinstance(h, int):
        at = pl.multiple_of(at, HEAD)
    return pl.ds(at, HEAD)


def one_head(h, qkv, grad_att, attended, grad_cells, sum_keys, sum_values):
    cells = qkv.shape[0]
    keys = qkv[:, columns(1, h)]
    values = qkv[:, columns(2, h)]
    values_ones = jnp.concatenate([values, jnp.ones((cells, HEAD), BF)], axis=1)
    for block in range(cells // QUERY_BLOCK):
        rows = slice(block * QUERY_BLOCK, (block + 1) * QUERY_BLOCK)
        queries = qkv[rows, columns(0, h)]
        scores = mm(queries, keys, NT)
        raised = jnp.exp2(scores - jnp.max(scores, axis=-1, keepdims=True))
        raised_b = raised.astype(BF)
        sums = mm(raised_b, values_ones)
        inverse = 1.0 / sums[:, HEAD:]
        result = sums[:, :HEAD] * inverse
        attended[rows, columns(0, h)] = result.astype(BF)
        scaled = grad_att[rows, columns(0, h)].astype(F32) * inverse
        inner = jnp.sum(scaled * result, axis=-1, keepdims=True)
        scaled_b = scaled.astype(BF)
        grad_probs = mm(scaled_b, values, NT)
        grad_scores = (raised * (grad_probs - inner)).astype(BF)
        grad_cells[rows, columns(0, h)] = (mm(grad_scores, keys) * FACTOR).astype(BF)
        new_keys = mm(queries.T, grad_scores)
        new_values = mm(scaled_b.T, raised_b)
        if block == 0:
            sum_keys[...] = new_keys
            sum_values[...] = new_values
        else:
            sum_keys[...] += new_keys
            sum_values[...] += new_values
    grad_cells[:, columns(1, h)] = (sum_keys[...] * (1.0 / LOG2E)).T.astype(BF)
    grad_cells[:, columns(2, h)] = sum_values[...].T.astype(BF)


def normed_parts(hidden_f):
    inv_rms = lax.rsqrt(jnp.mean(hidden_f * hidden_f, axis=-1, keepdims=True) + 1e-6)
    normed_f = hidden_f * inv_rms
    return inv_rms, normed_f, normed_f.astype(BF)


def split_columns(target, at, values):
    for n in range(values.shape[1] // 128):
        target[at + n] = values[:, n * 128 : (n + 1) * 128]


def spread_rows(message, at, source, group, first, step, count):
    for f in range(message.shape[0]):
        rows = source[group, pl.ds(first(f), count, stride=step), :]
        message[f, at : at + count, :] = rows.astype(BF)


def attend_first_body(
    came, qkv_w, grad_att, cotangent, hidden, border_slope, qkv, attended, grad_cells, message,
    sum_keys, sum_values, grads, grads_out, pieces,
):
    chunks, long, width = came.shape
    bins = long - EXTRA
    wide = HEADS * HEAD
    pieces[...] = came[:, bins:, :].astype(F32)
    here_first = pieces[:, 2, :] + pieces[:, 3, :]
    here_last = pieces[:, 4, :] + pieces[:, 5, :]
    first = here_first + moved_down(pieces[:, 6, :] + pieces[:, 7, :])
    last = here_last + moved_up(pieces[:, 0, :] + pieces[:, 1, :])
    sigma_first, sigma_last = sigmoid(first), sigmoid(last)
    border_slope[0] = slope_of(first, sigma_first)
    border_slope[1] = slope_of(last, sigma_last)
    fixed_first = came[:, 0, :].astype(F32) + first * sigma_first
    fixed_last = came[:, bins - 1, :].astype(F32) + last * sigma_last
    cells = with_borders(came[:, :bins, :].astype(F32), fixed_first, fixed_last)
    hidden[...] = cells.astype(BF).reshape(chunks * bins, width)
    _, _, normed = normed_parts(hidden[...].astype(F32))
    qkv[:, :wide] = (mm(normed, qkv_w[:, :wide]) * (FACTOR * LOG2E)).astype(BF)
    qkv[:, wide:] = mm(normed, qkv_w[:, wide:]).astype(BF)

    def head(h, carry):
        one_head(h, qkv, grad_att, attended, grad_cells, sum_keys, sum_values)
        return carry

    lax.fori_loop(0, EARLY, head, 0)
    turned = normed.T
    narrow = EARLY * HEAD
    for part in range(3):
        values = mm(turned, grad_cells[:, part * wide : part * wide + narrow])
        split_columns(grads, part * EARLY, SCALE * values)
    split_columns(grads_out, 0, SCALE * mm(attended[:, :narrow].T, cotangent[...]))
    tm = width // 8
    for group in range(3 * EARLY):
        spread_rows(message, group * tm, grads, group, lambda f: f, 8, tm)
    for group in range(4):
        b, c = divmod(group, 2)
        few = tm * EARLY // HEADS
        spread_rows(
            message, 3 * EARLY * tm + group * few, grads_out, c,
            lambda f: 2 * f + b, 16, few,
        )


def attend_last_body(
    hidden, border_slope, qkv, attended_in, grad_cells_in, grad_att, cotangent, qkv_w, out_w,
    payload, enhanced, message,
    attended, grad_cells, sum_keys, sum_values, grads, grads_out, rows_f, pieces,
):
    chunks, long, width = payload.shape
    bins = long - EXTRA
    wide = HEADS * HEAD
    narrow = EARLY * HEAD
    attended[:, :narrow] = attended_in[:, :narrow]
    for part in range(3):
        cut = slice(part * wide, part * wide + narrow)
        grad_cells[:, cut] = grad_cells_in[:, cut]
    for h in range(EARLY, HEADS):
        one_head(h, qkv, grad_att, attended, grad_cells, sum_keys, sum_values)
    hidden_f = hidden[...].astype(F32)
    inv_rms, normed_f, normed = normed_parts(hidden_f)
    grad_normed = mm(grad_cells[...], qkv_w[...], NT)
    mixing = jnp.mean(grad_normed * normed_f, axis=-1, keepdims=True)
    grad = cotangent[...].astype(F32) + inv_rms * (grad_normed - normed_f * mixing)
    grad_b = grad.astype(BF).reshape(chunks, bins, width)
    payload[:, :bins, :] = grad_b
    rows_f[...] = grad_b.astype(F32)
    first = rows_f[:, 0, :] * border_slope[0]
    last = rows_f[:, bins - 1, :] * border_slope[1]
    pieces[...] = jnp.zeros(pieces.shape, F32)
    pieces[:, 0, :] = moved_down(last)
    pieces[:, 1, :] = first
    pieces[:, 2, :] = last
    pieces[:, 3, :] = moved_up(first)
    payload[:, bins:, :] = pieces[...].astype(BF)
    enhanced[...] = (hidden_f + mm(attended[...], out_w[...])).astype(BF)
    turned = normed.T
    tm = width // 8
    for part in range(3):
        split_columns(grads, part, SCALE * mm(turned, grad_cells[:, columns(part, EARLY)]))
        spread_rows(message, part * tm, grads, part, lambda f: f, 8, tm)
    split_columns(grads_out, 0, SCALE * mm(attended[:, narrow:].T, cotangent[...]))
    few = tm // HEADS
    for group in range(4):
        b, c = divmod(group, 2)
        spread_rows(
            message, 3 * tm + group * few, grads_out, c, lambda f: 2 * f + b, 16, few
        )


def stack_back(rows, left, right):
    after = bins_after(rows, right).astype(BF)
    before = bins_before(rows, left).astype(BF)
    return jnp.concatenate([after, rows.astype(BF), before], axis=-1)


def conv_weight_body(came, slope, turned, head_message, stacked, edges, message, grads, pieces):
    frames, long, width = came.shape
    bins = long - EXTRA
    half = width // 2
    cells = frames * bins
    pieces[...] = came[:, bins:, :].astype(F32)
    grad = came[:, :bins, :].astype(F32) * slope[...]
    grad = with_borders(grad, pieces[:, 1, :], pieces[:, 2, :])
    grad_b = grad.astype(BF)
    for side, frame in enumerate((0, frames - 1)):
        edges[side, :, :bins, :] = grad_b[frame : frame + 1]
        edges[side, :, bins:, :] = came[frame : frame + 1, bins:, :]
    stacked[...] = stack_back(
        grad_b.astype(F32), pieces[:, 0, :][:, None, :], pieces[:, 3, :][:, None, :]
    )
    flat = stacked[...].reshape(cells, 3 * width)
    for i in range(3):
        block = mm(turned[:, i * bins : i * bins + cells], flat)
        for j in range(3):
            at = j * width
            upper = block[:half, at : at + half] + block[half:, at + half : at + width]
            lower = block[:half, at + half : at + width] - block[half:, at : at + half]
            tap = (3 * i + j) * half
            grads[tap : tap + half] = upper * SCALE
            grads[9 * half + tap : 9 * half + tap + half] = lower * SCALE
    early = head_message.shape[1]
    message[:, :early, :] = head_message[...]
    tm = width // 8
    for f in range(8):
        for e in range(9):
            rows = grads[pl.ds(9 * f + e, tm, stride=72), :]
            message[f, early + e * tm : early + (e + 1) * tm, :] = rows.astype(BF)


def conv_data_body(came, stacked, matrix, total):
    frames, bins, triple = stacked.shape
    width = triple // 3
    inner = (frames - 1) * bins
    flat = stacked[...].reshape(frames * bins, triple)
    total[...] = came[:, :bins, :].reshape(frames * bins, width).astype(F32) + mm(
        flat, matrix[1], NT
    )
    total[:inner] += mm(flat[bins:], matrix[0], NT)
    total[bins:] += mm(flat[:inner], matrix[2], NT)


def conv_data_finish_body(total, up, down, matrix, out):
    frames, bins, width = out.shape

    def stack(edge):
        extra = edge[0, :, bins:, :].astype(F32)
        rows = edge[0, :, :bins, :].astype(F32)
        return stack_back(rows, extra[:, 0:1, :], extra[:, 3:4, :])[0]

    out[...] = total[...].reshape(frames, bins, width).astype(BF)
    out[0] = (total[:bins] + mm(stack(up), matrix[2], NT)).astype(BF)
    out[frames - 1] = (total[(frames - 1) * bins :] + mm(stack(down), matrix[0], NT)).astype(BF)


def sum_body(came, out):
    total = came[0].astype(F32)
    for source in range(1, came.shape[0]):
        total = total + came[source].astype(F32)
    out[...] = total


def regroup_body(early, came, chunk, late, rows):
    tm = chunk.shape[0]
    sum_body(came, late)
    few, more = tm // HEADS, tm * EARLY // HEADS
    base = 3 * tm + 4 * few
    rows[...] = jnp.zeros(rows.shape, F32)
    for t in range(tm):
        rows[t, 0:9, :] = late[pl.ds(base + t, 9, stride=tm), :]
        rows[t, 9:18, :] = early[pl.ds(t, 3 * EARLY, stride=tm), :]
        rows[t, 18:21, :] = late[pl.ds(t, 3, stride=tm), :]
        if t < more:
            rows[t, 21:25, :] = early[pl.ds(3 * EARLY * tm + t, 4, stride=more), :]
        else:
            rows[t, 21:25, :] = late[pl.ds(3 * tm + t - more, 4, stride=few), :]
    chunk[...] = rows[...].astype(BF)


def share_body(came, conv, qkv, out, total):
    sum_body(came, total)
    conv[...] = total[0:9]
    for part in range(3):
        qkv[4 * part : 4 * part + 3, :] = total[9 + 3 * part : 12 + 3 * part]
        qkv[4 * part + 3 : 4 * part + 4, :] = total[18 + part : 19 + part]
    out[...] = total[21:25]


def along_tm(last, first):
    size = lax.axis_size("tm")
    up = lax.ppermute(last, "tm", [(i, i + 1) for i in range(size - 1)])
    down = lax.ppermute(first, "tm", [(i + 1, i) for i in range(size - 1)])
    return up, down


def exchange(array, axis):
    return lax.all_to_all(array, axis, split_axis=0, concat_axis=0, tiled=True)


def shards(spectrum, conv_weight, qkv_weight, out_weight, cotangent):
    frames, bins, width = spectrum.shape
    cells = frames * bins
    wide = HEADS * HEAD
    long = bins + EXTRA
    tm = lax.axis_size("tm")
    vmem = pltpu.VMEM
    cotangent = cotangent.reshape(cells, width)
    up, down = along_tm(spectrum[frames - 1 :], spectrum[:1])
    own, borders, matrix, matrix_back = kernel_call(
        conv_own_body, "conv_own",
        [
            ((cells, width), F32), ((2, frames, width), F32),
            ((3, 3 * width, width), BF), ((3, width, 3 * width), BF),
        ],
        spectrum, conv_weight,
        scratch=[vmem((frames, bins, 3 * width), BF)], mflops=1200,
    )
    payload, slope = kernel_call(
        conv_finish_body, "conv_finish",
        [((frames, long, width), BF), ((frames, bins, width), F32)],
        spectrum, up, down, own, borders, matrix,
        scratch=[vmem((frames, bins, width), F32), vmem((frames, EXTRA, width), F32)], mflops=200,
    )
    frame = exchange(payload, "freq")
    turned, grad_att = kernel_call(
        prepare_body, "prepare",
        [((width, cells + 2 * bins), BF), ((cells, wide), BF)],
        spectrum, up, down, cotangent, out_weight, mflops=300,
    )
    sums = [vmem((HEAD, cells), F32), vmem((HEAD, cells), F32)]
    more = tm * EARLY // HEADS
    hidden, border_slope, qkv, attended, grad_cells, message = kernel_call(
        attend_first_body, "attend_first",
        [
            ((cells, width), BF), ((2, frames, width), F32), ((cells, 3 * wide), BF),
            ((cells, wide), BF), ((cells, 3 * wide), BF),
            ((8, 3 * EARLY * tm + 4 * more, 128), BF),
        ],
        frame, qkv_weight, grad_att, cotangent,
        scratch=sums + [
            vmem((3 * EARLY, width, HEAD), F32), vmem((2, EARLY * HEAD, HEAD), F32),
            vmem((frames, EXTRA, width), F32),
        ],
        mflops=10000,
    )
    early = exchange(message, "freq")
    back, enhanced, head_message = kernel_call(
        attend_last_body, "attend_last",
        [
            ((frames, long, width), BF), ((cells, width), BF),
            ((8, 3 * tm + 4 * (tm - more), 128), BF),
        ],
        hidden, border_slope, qkv, attended, grad_cells, grad_att, cotangent, qkv_weight,
        out_weight,
        scratch=[vmem((cells, wide), BF), vmem((cells, 3 * wide), BF)] + sums + [
            vmem((3, width, HEAD), F32), vmem((2, HEAD, HEAD), F32),
            vmem((frames, bins, width), F32), vmem((frames, EXTRA, width), F32),
        ],
        mflops=5000,
    )
    (early,) = kernel_call(sum_body, "sum_early", [(early.shape[1:], F32)], early)
    grads = exchange(back, "freq")
    stacked, edges, message = kernel_call(
        conv_weight_body, "conv_weight_grad",
        [
            ((frames, bins, 3 * width), BF), ((2, 1, long, width), BF),
            ((8, head_message.shape[1] + 9 * tm, 128), BF),
        ],
        grads, slope, turned, head_message,
        scratch=[vmem((18 * (width // 2), width // 2), F32), vmem((frames, EXTRA, width), F32)],
        mflops=1200,
    )
    late = exchange(message, "freq")
    edge_up, edge_down = along_tm(edges[1:], edges[:1])
    (total,) = kernel_call(
        conv_data_body, "conv_data", [((cells, width), F32)],
        grads, stacked, matrix_back, mflops=1200,
    )
    (grad_spectrum,) = kernel_call(
        conv_data_finish_body, "conv_data_finish", [((frames, bins, width), BF)],
        total, edge_up, edge_down, matrix_back, mflops=100,
    )
    (chunk,) = kernel_call(
        regroup_body, "regroup", [((tm, 32, 128), BF)],
        early, late,
        scratch=[vmem(late.shape[1:], F32), vmem((tm, 32, 128), F32)],
    )
    shares = kernel_call(
        share_body, "share", [((9, 128), F32), ((12, 128), F32), ((4, 128), F32)],
        exchange(chunk, "tm"),
        scratch=[vmem((32, 128), F32)],
    )
    return (enhanced.reshape(1, cells, width), grad_spectrum, *[s.reshape(-1) for s in shares])


def solution(mesh):
    placed = (P("tm", "freq", None), P(), P(), P(), P(("tm", "freq"), None, None))
    return jax.shard_map(
        shards,
        mesh=mesh,
        in_specs=placed,
        out_specs=(
            P(("tm", "freq"), None, None),
            P("tm", "freq", None),
            P(("tm", "freq")),
            P(("tm", "freq")),
            P(("tm", "freq")),
        ),
        check_vma=False,
    )
```

time: 461 us -> 135 us (0.29)
  waiting for transfers between devices: 267 us -> 34.6 us
  matrix products: 78.5 us -> 0 us
  Pallas kernels: 0 us -> 35.5 us
  local copies, waits for them, and re-layouts: 49.8 us -> 15.1 us
  other arithmetic: 16 us -> 0 us
  between operations: 14.6 us -> 0.84 us
  blocking collectives: 0 us -> 13.5 us
    unnamed x2 -> x0, waiting for transfers between devices: 259 us -> none
    dot_general x33 -> x0, matrix products: 78.5 us -> none  [the longest x4 15.2 us: head_pass(): jnp.dot(probs_b, values, preferred_element_type=jnp.float32)]
    pallas_call x0 -> x11, Pallas kernels: none -> 35.5 us  [kernel_call(): pl.pallas_call(body, out_shape=outs, in_specs=[pl.BlockSpec(memory_space=...]
    all_to_all x2 -> x4, waiting for transfers between devices: 0.63 us -> 29.2 us  [exchange(): return lax.all_to_all(array, axis, split_axis=0, concat_axis=0, tiled=True)]
    reshape x5 -> x0, local copies, waits for them, and re-layouts: 18.9 us -> none  [the longest x2 8.74 us: frame_pass(): split_qkv = qkv.reshape(bin_count, 3, HEADS, -1).transpose(1, 2, 0, 3)]
    all_to_all x0 -> x1, blocking collectives: none -> 13.5 us  [exchange(): return lax.all_to_all(array, axis, split_axis=0, concat_axis=0, tiled=True)]
    dynamic_update_slice x24 -> x0, local copies, waits for them, and re-layouts: 12.8 us -> none  [frame_pass(): lax.map(head_pass, (split_qkv[0], split_qkv[1], split_qkv[2], grad_split))]
    all_to_all x2 -> x4, starting transfers between devices: 10.8 us -> 21.4 us  [exchange(): return lax.all_to_all(array, axis, split_axis=0, concat_axis=0, tiled=True)]
  transfers between devices with their start and end apart: 11 -> 8, of which waited for: 5 -> 5; matrix products, arithmetic and copies ran while one was open for 7% -> 0% of each run, Pallas kernels for 0% -> 5%
where the time goes in v2:
time: 135 us; the launch traced here: 134 us
  Pallas kernels  35.5 us (26%)
  waiting for transfers between devices  34.6 us (26%)
  starting transfers between devices  34.3 us (25%)
  local copies, waits for them, and re-layouts  15.1 us (11%)
  blocking collectives  13.5 us (10%)
    pallas_call x11, Pallas kernels, kernel_call(): pl.pallas_call(body, out_shape=outs, in_specs=[pl.BlockSpec(memory_space=...  35.5 us
    all_to_all x4, waiting for transfers between devices, exchange(): return lax.all_to_all(array, axis, split_axis=0, concat_axis=0, tiled=True)  29.2 us
    all_to_all x4, starting transfers between devices, exchange(): return lax.all_to_all(array, axis, split_axis=0, concat_axis=0, tiled=True)  21.4 us
    unnamed x34, local copies, waits for them, and re-layouts  14.2 us
    all_to_all x1, blocking collectives, exchange(): return lax.all_to_all(array, axis, split_axis=0, concat_axis=0, tiled=True)  13.5 us
    ppermute x2, starting transfers between devices, along_tm(): down = lax.ppermute(first, 'tm', [(i + 1, i) for i in range(size - 1)])  9.05 us
    ppermute x2, waiting for transfers between devices, along_tm(): up = lax.ppermute(last, 'tm', [(i, i + 1) for i in range(size - 1)])  5.38 us
    ppermute x2, starting transfers between devices, along_tm(): up = lax.ppermute(last, 'tm', [(i, i + 1) for i in range(size - 1)])  3.84 us
  transfers between devices with their start and end apart: 8, of which 5 were waited for; matrix products, arithmetic and copies ran while one was open for 0% of the time, Pallas kernels for 5%

profile of v2, /device:TPU:32, one launch (start us, length us, event | category | flops | bytes accessed | tf_op | source)
XLA Modules:
  0.0 133.8 jit_solution(16521145780329332757)
XLA Ops:
  1.5 4.5 %collective-permute-start.1 = (bf16[1,128,256]{2,1,0:T(8,128)(2,1)S(1)}, bf16[1,128,256]{2,1,0:T(8,128)(2,1)S(1)}, u32[]{:S(2)}, u32[]{:S(2)}) collective-permute-start(bf16[1,128,256]{2,1,0:T(8,128)(2,1)S(1)} %get-tuple-element.51), channel_id=1, source_target_pairs={{8,0},{16,8},{24,16},{32,24},{40,32},{48,40},{56,48},{64,56},{72,6... | collective-permute-start | bytes 196616 | tf_op jit(solution)/shard_map/ppermute | solution.py:412
  6.0 1.9 %collective-permute-start = (bf16[1,128,256]{2,1,0:T(8,128)(2,1)S(1)}, bf16[1,128,256]{2,1,0:T(8,128)(2,1)S(1)}, u32[]{:S(2)}, u32[]{:S(2)}) collective-permute-start(bf16[1,128,256]{2,1,0:T(8,128)(2,1)S(1)} %get-tuple-element.52), channel_id=1, source_target_pairs={{0,8},{8,16},{16,24},{24,32},{32,40},{40,48},{48,56},{56,64},{64,7... | collective-permute-start | bytes 196616 | tf_op jit(solution)/shard_map/ppermute | solution.py:411
  7.9 1.0 copy-done
  9.0 1.1 copy-done.14
  10.0 1.5 %conv_own.1 = (f32[1024,256]{1,0:T(8,128)S(1)}, f32[2,8,256]{2,1,0:T(8,128)S(1)}, bf16[3,768,256]{2,1,0:T(8,128)(2,1)S(1)}, bf16[3,256,768]{2,1,0:T(8,128)(2,1)S(1)}) custom-call(bf16[8,128,256]{2,1,0:T(8,128)(2,1)S(1)} %copy-done, bf16[2,3,3,128,128]{4,3,2,1,0:T(8,128)(2,1)S(1)} %copy-done.14), custom_call_target="tpu_custom_call" | custom-call | flops 1200000000 | bytes 4538368 | tf_op jit(solution)/shard_map/conv_own/pallas_call | solution.py:31
  11.5 2.8 %collective-permute-done.up = bf16[1,128,256]{2,1,0:T(8,128)(2,1)S(1)} collective-permute-done((bf16[1,128,256]{2,1,0:T(8,128)(2,1)S(1)}, bf16[1,128,256]{2,1,0:T(8,128)(2,1)S(1)}, u32[]{:S(2)}, u32[]{:S(2)}) %collective-permute-start) | collective-permute-done | bytes 65568 | tf_op jit(solution)/shard_map/ppermute | solution.py:411
  14.3 1.8 %conv_finish.1 = (bf16[8,144,256]{2,1,0:T(8,128)(2,1)}, f32[8,128,256]{2,1,0:T(8,128)S(1)}) custom-call(bf16[8,128,256]{2,1,0:T(8,128)(2,1)S(1)} %copy-done, bf16[1,128,256]{2,1,0:T(8,128)(2,1)S(1)} %collective-permute-done.up, bf16[1,128,256]{2,1,0:T(8,128)(2,1)S(1)} %collective-permute-done.1.down, f32[1024,256]{1,0:T(8,128)S(1)} %get-tuple-element.28.own, ...), custom_call_target="tpu_custom_call" | custom-call | flops 200000000 | bytes 4538368 | tf_op jit(solution)/shard_map/conv_finish/pallas_call | solution.py:31
  17.0 4.3 %all-to-all-start = ((bf16[8,144,256]{2,1,0:T(8,128)(2,1)}), bf16[8,144,256]{2,1,0:T(8,128)(2,1)S(1)}, u32[]{:S(2)}, u32[]{:S(2)}) async-start(bf16[8,144,256]{2,1,0:T(8,128)(2,1)} %get-tuple-element.31), calls=%async_computation | async-start | bytes 1179648 | tf_op jit(solution)/shard_map/all_to_all | solution.py:417
  21.8 1.0 copy-done.9
  23.7 8.7 %all-to-all-done.came = bf16[8,144,256]{2,1,0:T(8,128)(2,1)S(1)} async-done(((bf16[8,144,256]{2,1,0:T(8,128)(2,1)}), bf16[8,144,256]{2,1,0:T(8,128)(2,1)S(1)}, u32[]{:S(2)}, u32[]{:S(2)}) %all-to-all-start) | async-done | bytes 589856 | tf_op jit(solution)/shard_map/all_to_all | solution.py:417
  32.3 1.2 copy-done.10
  33.6 1.1 copy-done.11
  34.7 17.0 %attend_first.1 = (bf16[1024,256]{1,0:T(8,128)(2,1)S(1)}, f32[2,8,256]{2,1,0:T(8,128)S(1)}, bf16[1024,1536]{1,0:T(8,128)(2,1)}, bf16[1024,512]{1,0:T(8,128)(2,1)...) custom-call(bf16[8,144,256]{2,1,0:T(8,128)(2,1)S(1)} %all-to-all-done.came, ...), custom_call_target="tpu_custom_call" | custom-call | flops 10000000000 | bytes 11616256 | tf_op jit(solution)/shard_map/attend_first/pallas_call | solution.py:31
  51.7 8.7 %attend_last.1 = (bf16[8,144,256]{2,1,0:T(8,128)(2,1)S(1)}, bf16[1024,256]{1,0:T(8,128)(2,1)}, bf16[8,128,128]{2,1,0:T(8,128)(2,1)S(1)}) custom-call(bf16[1024,256]{1,0:T(8,128)(2,1)S(1)} %get-tuple-element.33.hidden, f32[2,8,256]{2,1,0:T(8,128)S(1)} %get-tuple-element.34.border_slope, bf16[1024,1536]{1,0:T(8,128)(2,1)} %get-tuple-element.35.qkv, ...), custom_call_target="tpu_custom_call" | custom-call | flops 5000000000 | bytes 11878400 | tf_op jit(solution)/shard_map/attend_last/pallas_call | solution.py:31
  60.4 13.5 %all_to_all.25.came = bf16[8,144,256]{2,1,0:T(8,128)(2,1)S(1)} all-to-all(bf16[8,144,256]{2,1,0:T(8,128)(2,1)S(1)} %get-tuple-element.39), channel_id=1, replica_groups=mesh['tm'=32,'freq'=8] {'freq'}, dimensions={0} | all-to-all | bytes 1179648 | tf_op jit(solution)/shard_map/all_to_all | solution.py:417
  73.9 3.5 %all-to-all-start.2 = ((bf16[8,384,128]{2,1,0:T(8,128)(2,1)}), bf16[8,384,128]{2,1,0:T(8,128)(2,1)S(1)}, u32[]{:S(2)}, u32[]{:S(2)}) async-start(bf16[8,384,128]{2,1,0:T(8,128)(2,1)} %get-tuple-element.46), calls=%async_computation.2 | async-start | bytes 1572864 | tf_op jit(solution)/shard_map/all_to_all | solution.py:417
  77.4 1.2 copy-done.8
  78.7 1.1 copy-done.13
  79.7 1.7 %conv_weight_grad.1 = (bf16[8,128,768]{2,1,0:T(8,128)(2,1)S(1)}, bf16[2,1,144,256]{3,2,1,0:T(8,128)(2,1)S(1)}, bf16[8,416,128]{2,1,0:T(8,128)(2,1)S(1)}) custom-call(bf16[8,144,256]{2,1,0:T(8,128)(2,1)S(1)} %all_to_all.25.came, f32[8,128,256]{2,1,0:T(8,128)S(1)} %copy-done.8, bf16[256,1280]{1,0:T(8,128)(2,1)S(1)} %copy-done.13, ...), custom_call_target="tpu_custom_call" | custom-call | flops 1200000000 | bytes 5128192 | tf_op jit(solution)/shard_map/conv_weight_grad/pallas_call | solution.py:31
  82.4 1.2 copy-done.15
  83.6 6.9 %all-to-all-done.2.came = bf16[8,384,128]{2,1,0:T(8,128)(2,1)S(1)} async-done(((bf16[8,384,128]{2,1,0:T(8,128)(2,1)}), bf16[8,384,128]{2,1,0:T(8,128)(2,1)S(1)}, u32[]{:S(2)}, u32[]{:S(2)}) %all-to-all-start.2) | async-done | bytes 786464 | tf_op jit(solution)/shard_map/all_to_all | solution.py:417
  90.5 3.5 %all-to-all-start.3 = ((bf16[8,416,128]{2,1,0:T(8,128)(2,1)}), bf16[8,416,128]{2,1,0:T(8,128)(2,1)S(1)}, u32[]{:S(2)}, u32[]{:S(2)}) async-start(bf16[8,416,128]{2,1,0:T(8,128)(2,1)} %copy-done.2), calls=%async_computation.3 | async-start | bytes 1703936 | tf_op jit(solution)/shard_map/all_to_all | solution.py:417
  94.2 13.7 %all-to-all-done.3.came = bf16[8,416,128]{2,1,0:T(8,128)(2,1)S(1)} async-done(((bf16[8,416,128]{2,1,0:T(8,128)(2,1)}), bf16[8,416,128]{2,1,0:T(8,128)(2,1)S(1)}, u32[]{:S(2)}, u32[]{:S(2)}) %all-to-all-start.3) | async-done | bytes 852000 | tf_op jit(solution)/shard_map/all_to_all | solution.py:417
  107.8 1.1 regroup.1
  109.0 10.0 %all-to-all-start.4 = ((bf16[32,32,128]{2,1,0:T(8,128)(2,1)}), bf16[32,32,128]{2,1,0:T(8,128)(2,1)S(1)}, u32[]{:S(2)}, u32[]{:S(2)}) async-start(bf16[32,32,128]{2,1,0:T(8,128)(2,1)} %regroup.1), calls=%async_computation.4 | async-start | bytes 524288 | tf_op jit(solution)/shard_map/all_to_all | solution.py:417
  119.0 4.6 %collective-permute-start.3 = (bf16[1,1,144,256]{3,2,1,0:T(8,128)(2,1)S(1)}, bf16[1,1,144,256]{3,2,1,0:T(8,128)(2,1)S(1)}, u32[]{:S(2)}, u32[]{:S(2)}) collective-permute-start(bf16[1,1,144,256]{3,2,1,0:T(8,128)(2,1)S(1)} %get-tuple-element.53), channel_id=1, source_target_pairs={{8,0},{16,8},{24,16},{32,24},{40,32},{48,40},{56,48},{64,56},{72,6... | collective-permute-start | bytes 221192 | tf_op jit(solution)/shard_map/ppermute | solution.py:412
  123.6 1.9 %collective-permute-start.2 = (bf16[1,1,144,256]{3,2,1,0:T(8,128)(2,1)S(1)}, bf16[1,1,144,256]{3,2,1,0:T(8,128)(2,1)S(1)}, u32[]{:S(2)}, u32[]{:S(2)}) collective-permute-start(bf16[1,1,144,256]{3,2,1,0:T(8,128)(2,1)S(1)} %get-tuple-element.54), channel_id=1, source_target_pairs={{0,8},{8,16},{16,24},{24,32},{32,40},{40,48},{48,56},{56,64},{64,7... | collective-permute-start | bytes 221192 | tf_op jit(solution)/shard_map/ppermute | solution.py:411
  125.5 1.1 copy-done.4
  126.6 1.4 %copy-done.16 = bf16[8,128,768]{2,1,0:T(8,128)(2,1)S(1)} copy-done((bf16[8,128,768]{2,1,0:T(8,128)(2,1)S(1)}, bf16[8,128,768]{2,1,0:T(8,128)(2,1)}, u32[]{:S(2)}) %copy-start.16) | copy-done | bytes 1572888
  128.0 1.3 conv_data.1.total
  129.3 2.6 %collective-permute-done.2.up = bf16[1,1,144,256]{3,2,1,0:T(8,128)(2,1)S(1)} collective-permute-done((bf16[1,1,144,256]{3,2,1,0:T(8,128)(2,1)S(1)}, bf16[1,1,144,256]{3,2,1,0:T(8,128)(2,1)S(1)}, u32[]{:S(2)}, u32[]{:S(2)}) %collective-permute-start.2) | collective-permute-done | bytes 73760 | tf_op jit(solution)/shard_map/ppermute | solution.py:411
  132.0 1.2 conv_data_finish.1
  (32 shorter events, 4.9 us)
Async XLA Ops:
  1.5 10.0 %collective-permute-start.1 = (bf16[1,128,256]{2,1,0:T(8,128)(2,1)S(1)}, bf16[1,128,256]{2,1,0:T(8,128)(2,1)S(1)}, u32[]{:S(2)}, u32[]{:S(2)}) collective-permute-start(bf16[1,128,256]{2,1,0:T(8,128)(2,1)S(1)} %get-tuple-element.51), channel_id=1, source_target_pairs={{8,0},{16,8},{24,16},{32,24},{40,32},{48,40},{56,48},{64,56},{72,6... | collective-permute-start | bytes 196616 | tf_op jit(solution)/shard_map/ppermute | solution.py:412
  6.0 8.3 %collective-permute-start = (bf16[1,128,256]{2,1,0:T(8,128)(2,1)S(1)}, bf16[1,128,256]{2,1,0:T(8,128)(2,1)S(1)}, u32[]{:S(2)}, u32[]{:S(2)}) collective-permute-start(bf16[1,128,256]{2,1,0:T(8,128)(2,1)S(1)} %get-tuple-element.52), channel_id=1, source_target_pairs={{0,8},{8,16},{16,24},{24,32},{32,40},{40,48},{48,56},{56,64},{64,7... | collective-permute-start | bytes 196616 | tf_op jit(solution)/shard_map/ppermute | solution.py:411
  7.9 1.0 copy-start
  9.0 1.1 copy-start.14
  14.3 7.0 %copy-start.1 = (bf16[8,128,256]{2,1,0:T(8,128)(2,1)S(1)}, bf16[8,128,256]{2,1,0:T(8,128)(2,1)}, u32[]{:S(2)}) copy-start(bf16[8,128,256]{2,1,0:T(8,128)(2,1)} %mid.5) | copy-start | bytes 1572868
  14.3 7.0 %copy-start.5 = (bf16[1,1024,256]{2,1,0:T(8,128)(2,1)S(1)}, bf16[1,1024,256]{2,1,0:T(8,128)(2,1)}, u32[]{:S(2)}) copy-start(bf16[1,1024,256]{2,1,0:T(8,128)(2,1)} %param.9) | copy-start | bytes 1572868
  14.3 7.0 %copy-start.6 = (bf16[512,256]{1,0:T(8,128)(2,1)S(1)}, bf16[512,256]{1,0:T(8,128)(2,1)}, u32[]{:S(2)}) copy-start(bf16[512,256]{1,0:T(8,128)(2,1)} %out_w.3) | copy-start | bytes 786436
  16.0 1.0 copy-start.7
  17.0 15.3 %all-to-all-start = ((bf16[8,144,256]{2,1,0:T(8,128)(2,1)}), bf16[8,144,256]{2,1,0:T(8,128)(2,1)S(1)}, u32[]{:S(2)}, u32[]{:S(2)}) async-start(bf16[8,144,256]{2,1,0:T(8,128)(2,1)} %get-tuple-element.31), calls=%async_computation | async-start | bytes 1179648 | tf_op jit(solution)/shard_map/all_to_all | solution.py:417
  21.8 1.0 copy-start.9
  22.8 0.9 copy-start.12
  32.3 1.2 copy-start.10
  33.6 1.1 copy-start.11
  73.9 7.6 %copy-start.3 = (bf16[8,144,256]{2,1,0:T(8,128)(2,1)}, bf16[8,144,256]{2,1,0:T(8,128)(2,1)S(1)}, u32[]{:S(2)}) copy-start(bf16[8,144,256]{2,1,0:T(8,128)(2,1)S(1)} %all_to_all.25.came) | copy-start | bytes 1769476
  73.9 16.6 %all-to-all-start.2 = ((bf16[8,384,128]{2,1,0:T(8,128)(2,1)}), bf16[8,384,128]{2,1,0:T(8,128)(2,1)S(1)}, u32[]{:S(2)}, u32[]{:S(2)}) async-start(bf16[8,384,128]{2,1,0:T(8,128)(2,1)} %get-tuple-element.46), calls=%async_computation.2 | async-start | bytes 1572864 | tf_op jit(solution)/shard_map/all_to_all | solution.py:417
  77.4 1.2 copy-start.8
  78.6 1.1 copy-start.13
  81.5 0.9 copy-start.2
  82.4 1.2 copy-start.15
  90.5 17.3 %all-to-all-start.3 = ((bf16[8,416,128]{2,1,0:T(8,128)(2,1)}), bf16[8,416,128]{2,1,0:T(8,128)(2,1)S(1)}, u32[]{:S(2)}, u32[]{:S(2)}) async-start(bf16[8,416,128]{2,1,0:T(8,128)(2,1)} %copy-done.2), calls=%async_computation.3 | async-start | bytes 1703936 | tf_op jit(solution)/shard_map/all_to_all | solution.py:417
  109.0 24.2 %all-to-all-start.4 = ((bf16[32,32,128]{2,1,0:T(8,128)(2,1)}), bf16[32,32,128]{2,1,0:T(8,128)(2,1)S(1)}, u32[]{:S(2)}, u32[]{:S(2)}) async-start(bf16[32,32,128]{2,1,0:T(8,128)(2,1)} %regroup.1), calls=%async_computation.4 | async-start | bytes 524288 | tf_op jit(solution)/shard_map/all_to_all | solution.py:417
  119.0 10.3 %collective-permute-start.3 = (bf16[1,1,144,256]{3,2,1,0:T(8,128)(2,1)S(1)}, bf16[1,1,144,256]{3,2,1,0:T(8,128)(2,1)S(1)}, u32[]{:S(2)}, u32[]{:S(2)}) collective-permute-start(bf16[1,1,144,256]{3,2,1,0:T(8,128)(2,1)S(1)} %get-tuple-element.53), channel_id=1, source_target_pairs={{8,0},{16,8},{24,16},{32,24},{40,32},{48,40},{56,48},{64,56},{72,6... | collective-permute-start | bytes 221192 | tf_op jit(solution)/shard_map/ppermute | solution.py:412
  123.6 8.4 %collective-permute-start.2 = (bf16[1,1,144,256]{3,2,1,0:T(8,128)(2,1)S(1)}, bf16[1,1,144,256]{3,2,1,0:T(8,128)(2,1)S(1)}, u32[]{:S(2)}, u32[]{:S(2)}) collective-permute-start(bf16[1,1,144,256]{3,2,1,0:T(8,128)(2,1)S(1)} %get-tuple-element.54), channel_id=1, source_target_pairs={{0,8},{8,16},{16,24},{24,32},{32,40},{40,48},{48,56},{56,64},{64,7... | collective-permute-start | bytes 221192 | tf_op jit(solution)/shard_map/ppermute | solution.py:411
  125.5 1.1 copy-start.4
  126.6 1.4 %copy-start.16 = (bf16[8,128,768]{2,1,0:T(8,128)(2,1)S(1)}, bf16[8,128,768]{2,1,0:T(8,128)(2,1)}, u32[]{:S(2)}) copy-start(bf16[8,128,768]{2,1,0:T(8,128)(2,1)} %copy-done.15) | copy-start | bytes 4718596

commit v3 on v2

--- a/solution.py
+++ b/solution.py
@@ -25,15 +25,23 @@
     return lax.dot_general(a, b, dims, preferred_element_type=F32)
 
 
-def kernel_call(body, name, outs, *args, scratch=(), mflops=0, limit=48):
-    outs = [jax.ShapeDtypeStruct(dims, kind) for dims, kind in outs]
-    size = sum(a.size * a.dtype.itemsize for a in (*args, *outs))
+def kernel_call(body, name, outs, *args, far=(), scratch=(), copies=0, mflops=0, limit=48):
+    shapes = [
+        (pltpu.HBM if away else jax.ShapeDtypeStruct)(dims, kind) for dims, kind, away in outs
+    ]
+    args = [
+        pltpu.with_memory_space_constraint(a, pltpu.HBM) if n in far else a
+        for n, a in enumerate(args)
+    ]
+    size = sum(math.prod(a.shape) * a.dtype.itemsize for a in (*args, *shapes))
+    near, hbm = pl.BlockSpec(memory_space=pltpu.VMEM), pl.BlockSpec(memory_space=pltpu.HBM)
+    scratch = list(scratch) + ([pltpu.SemaphoreType.DMA((copies,))] if copies else [])
     return pl.pallas_call(
         body,
-        out_shape=outs,
-        in_specs=[pl.BlockSpec(memory_space=pltpu.VMEM)] * len(args),
-        out_specs=[pl.BlockSpec(memory_space=pltpu.VMEM)] * len(outs),
-        scratch_shapes=list(scratch),
+        out_shape=shapes,
+        in_specs=[hbm if n in far else near for n in range(len(args))],
+        out_specs=[hbm if away else near for _, _, away in outs],
+        scratch_shapes=scratch,
         compiler_params=pltpu.CompilerParams(vmem_limit_bytes=limit * 2**20),
         cost_estimate=pl.CostEstimate(
             flops=mflops * 10**6, bytes_accessed=size, transcendentals=0
@@ -42,6 +50,18 @@
     )(*args)
 
 
+def copier(semaphores):
+    started = []
+
+    def start(source, target):
+        copy = pltpu.make_async_copy(source, target, semaphores.at[len(started)])
+        copy.start()
+        started.append(copy)
+        return copy
+
+    return start
+
+
 def sigmoid(v):
     return 1.0 / (1.0 + jnp.exp(-v))
 
@@ -78,13 +98,12 @@
     return jnp.where(at == last, right, pltpu.roll(rows, last, 1))
 
 
-def conv_own_body(mid, weight, conv, borders, matrix, matrix_back, stacked):
+def conv_own_body(mid_far, weight_far, conv, borders, matrix, mid, weight, stacked, semaphores):
+    start = copier(semaphores)
+    load_weight, load_mid = start(weight_far, weight), start(mid_far, mid)
     frames, bins, width = mid.shape
     half = width // 2
-    wide = mid[...].astype(F32)
-    stacked[:, :, :width] = bins_before(wide, 0.0).astype(BF)
-    stacked[:, :, width : 2 * width] = mid[...]
-    stacked[:, :, 2 * width :] = bins_after(wide, 0.0).astype(BF)
+    load_weight.wait()
     for i in range(3):
         for j in range(3):
             real, imag = weight[0, i, j], weight[1, i, j]
@@ -93,10 +112,11 @@
             matrix[i, at : at + half, half:] = imag
             matrix[i, at + half : at + width, :half] = -imag
             matrix[i, at + half : at + width, half:] = real
-            matrix_back[i, :half, at : at + half] = real
-            matrix_back[i, :half, at + half : at + width] = imag
-            matrix_back[i, half:, at : at + half] = -imag
-            matrix_back[i, half:, at + half : at + width] = real
+    load_mid.wait()
+    wide = mid[...].astype(F32)
+    stacked[:, :, :width] = bins_before(wide, 0.0).astype(BF)
+    stacked[:, :, width : 2 * width] = mid[...]
+    stacked[:, :, 2 * width :] = bins_after(wide, 0.0).astype(BF)
     inner = (frames - 1) * bins
     everything = stacked[...].reshape(frames * bins, 3 * width)
     conv[...] = mm(everything, matrix[1])
@@ -106,7 +126,11 @@
     borders[1] = mid[:, bins - 1, :].astype(F32)
 
 
-def conv_finish_body(mid, up, down, own, borders, matrix, payload, slope, conv, pieces):
+def conv_finish_body(
+    mid_far, up, down, own, borders, matrix, payload, slope_far, mid, slope, conv, pieces, semaphores
+):
+    start = copier(semaphores)
+    load_mid = start(mid_far, mid)
     frames, bins, width = mid.shape
     cells = frames * bins
 
@@ -146,47 +170,63 @@
     values = conv[...]
     sigma = sigmoid(values)
     slope[...] = slope_of(values, sigma)
+    store = start(slope, slope_far)
+    load_mid.wait()
     hidden = mid[...].astype(F32) + values * sigma
     payload[:, :bins, :] = with_borders(hidden, borders[0], borders[1]).astype(BF)
     payload[:, bins:, :] = pieces[...].astype(BF)
-
-
-def prepare_body(mid, up, down, cotangent, out_w, turned, grad_att):
+    store.wait()
+
+
+def prepare_body(
+    mid_far, up, down, cotangent_far, out_w_far, turned_far, grad_att_far,
+    mid, cotangent, out_w, turned, grad_att, semaphores,
+):
+    start = copier(semaphores)
+    loads = start(mid_far, mid), start(cotangent_far, cotangent), start(out_w_far, out_w)
+    for load in loads:
+        load.wait()
     frames, bins, width = mid.shape
     turned[:, :bins] = up[0].T
     turned[:, bins : (frames + 1) * bins] = mid[...].reshape(frames * bins, width).T
     turned[:, (frames + 1) * bins :] = down[0].T
     grad_att[...] = mm(cotangent[...], out_w[...], NT).astype(BF)
-
-
-def columns(part, h):
-    at = part * HEADS * HEAD + h * HEAD
+    stores = start(turned, turned_far), start(grad_att, grad_att_far)
+    for store in stores:
+        store.wait()
+
+
+def columns(part, h, heads=HEADS):
+    at = (part * heads + h) * HEAD
     if not isinstance(h, int):
         at = pl.multiple_of(at, HEAD)
     return pl.ds(at, HEAD)
 
 
-def one_head(h, qkv, grad_att, attended, grad_cells, sum_keys, sum_values):
+def one_head(h, heads, qkv, grad_att, attended, grad_cells, sum_keys, sum_values):
+    def columns_of(part):
+        return columns(part, h, heads)
+
     cells = qkv.shape[0]
-    keys = qkv[:, columns(1, h)]
-    values = qkv[:, columns(2, h)]
+    keys = qkv[:, columns_of(1)]
+    values = qkv[:, columns_of(2)]
     values_ones = jnp.concatenate([values, jnp.ones((cells, HEAD), BF)], axis=1)
     for block in range(cells // QUERY_BLOCK):
         rows = slice(block * QUERY_BLOCK, (block + 1) * QUERY_BLOCK)
-        queries = qkv[rows, columns(0, h)]
+        queries = qkv[rows, columns_of(0)]
         scores = mm(queries, keys, NT)
         raised = jnp.exp2(scores - jnp.max(scores, axis=-1, keepdims=True))
         raised_b = raised.astype(BF)
         sums = mm(raised_b, values_ones)
         inverse = 1.0 / sums[:, HEAD:]
         result = sums[:, :HEAD] * inverse
-        attended[rows, columns(0, h)] = result.astype(BF)
-        scaled = grad_att[rows, columns(0, h)].astype(F32) * inverse
+        attended[rows, columns_of(0)] = result.astype(BF)
+        scaled = grad_att[rows, columns_of(0)].astype(F32) * inverse
         inner = jnp.sum(scaled * result, axis=-1, keepdims=True)
         scaled_b = scaled.astype(BF)
         grad_probs = mm(scaled_b, values, NT)
         grad_scores = (raised * (grad_probs - inner)).astype(BF)
-        grad_cells[rows, columns(0, h)] = (mm(grad_scores, keys) * FACTOR).astype(BF)
+        grad_cells[rows, columns_of(0)] = (mm(grad_scores, keys) * FACTOR).astype(BF)
         new_keys = mm(queries.T, grad_scores)
         new_values = mm(scaled_b.T, raised_b)
         if block == 0:
@@ -195,8 +235,8 @@
         else:
             sum_keys[...] += new_keys
             sum_values[...] += new_values
-    grad_cells[:, columns(1, h)] = (sum_keys[...] * (1.0 / LOG2E)).T.astype(BF)
-    grad_cells[:, columns(2, h)] = sum_values[...].T.astype(BF)
+    grad_cells[:, columns_of(1)] = (sum_keys[...] * (1.0 / LOG2E)).T.astype(BF)
+    grad_cells[:, columns_of(2)] = sum_values[...].T.astype(BF)
 
 
 def normed_parts(hidden_f):
@@ -217,9 +257,16 @@
 
 
 def attend_first_body(
-    came, qkv_w, grad_att, cotangent, hidden, border_slope, qkv, attended, grad_cells, message,
-    sum_keys, sum_values, grads, grads_out, pieces,
+    came, qkv_w_far, grad_att_far, cotangent_far,
+    border_slope, message, hidden_far, qkv_far, attended_far, grad_cells_far,
+    qkv_w, grad_att, cotangent, hidden, qkv, late, attended, grad_cells,
+    sum_keys, sum_values, grads, grads_out, pieces, semaphores,
 ):
+    start = copier(semaphores)
+    narrow = EARLY * HEAD
+    load_qkv_w = start(qkv_w_far, qkv_w)
+    load_grad_att = start(grad_att_far.at[:, :narrow], grad_att)
+    load_cotangent = start(cotangent_far, cotangent)
     chunks, long, width = came.shape
     bins = long - EXTRA
     wide = HEADS * HEAD
@@ -235,21 +282,31 @@
     fixed_last = came[:, bins - 1, :].astype(F32) + last * sigma_last
     cells = with_borders(came[:, :bins, :].astype(F32), fixed_first, fixed_last)
     hidden[...] = cells.astype(BF).reshape(chunks * bins, width)
+    stores = [start(hidden, hidden_far)]
     _, _, normed = normed_parts(hidden[...].astype(F32))
-    qkv[:, :wide] = (mm(normed, qkv_w[:, :wide]) * (FACTOR * LOG2E)).astype(BF)
-    qkv[:, wide:] = mm(normed, qkv_w[:, wide:]).astype(BF)
+    load_qkv_w.wait()
+    for part in range(3):
+        values = mm(normed, qkv_w[:, part * wide : (part + 1) * wide])
+        if part == 0:
+            values = values * (FACTOR * LOG2E)
+        values = values.astype(BF)
+        qkv[:, part * narrow : (part + 1) * narrow] = values[:, :narrow]
+        late[:, part * HEAD : (part + 1) * HEAD] = values[:, narrow:]
+    stores.append(start(late, qkv_far))
+    load_grad_att.wait()
 
     def head(h, carry):
-        one_head(h, qkv, grad_att, attended, grad_cells, sum_keys, sum_values)
+        one_head(h, EARLY, qkv, grad_att, attended, grad_cells, sum_keys, sum_values)
         return carry
 
     lax.fori_loop(0, EARLY, head, 0)
+    stores += [start(attended, attended_far), start(grad_cells, grad_cells_far)]
+    load_cotangent.wait()
     turned = normed.T
-    narrow = EARLY * HEAD
     for part in range(3):
-        values = mm(turned, grad_cells[:, part * wide : part * wide + narrow])
+        values = mm(turned, grad_cells[:, part * narrow : (part + 1) * narrow])
         split_columns(grads, part * EARLY, SCALE * values)
-    split_columns(grads_out, 0, SCALE * mm(attended[:, :narrow].T, cotangent[...]))
+    split_columns(grads_out, 0, SCALE * mm(attended[...].T, cotangent[...]))
     tm = width // 8
     for group in range(3 * EARLY):
         spread_rows(message, group * tm, grads, group, lambda f: f, 8, tm)
@@ -260,25 +317,38 @@
             message, 3 * EARLY * tm + group * few, grads_out, c,
             lambda f: 2 * f + b, 16, few,
         )
+    for store in stores:
+        store.wait()
 
 
 def attend_last_body(
-    hidden, border_slope, qkv, attended_in, grad_cells_in, grad_att, cotangent, qkv_w, out_w,
-    payload, enhanced, message,
-    attended, grad_cells, sum_keys, sum_values, grads, grads_out, rows_f, pieces,
+    border_slope, hidden_far, qkv_far, grad_cells_far, grad_att_far, cotangent_far, qkv_w_far,
+    payload, attended_far, late_cells_far,
+    hidden, qkv, grad_att, cotangent, qkv_w, attended, late_cells, grad_cells,
+    sum_keys, sum_values, rows_f, pieces, semaphores,
 ):
+    start = copier(semaphores)
     chunks, long, width = payload.shape
     bins = long - EXTRA
     wide = HEADS * HEAD
     narrow = EARLY * HEAD
-    attended[:, :narrow] = attended_in[:, :narrow]
+    loads = [start(qkv_far, qkv), start(grad_att_far.at[:, narrow:], grad_att)]
+    later = [
+        start(hidden_far, hidden), start(cotangent_far, cotangent), start(qkv_w_far, qkv_w)
+    ]
     for part in range(3):
-        cut = slice(part * wide, part * wide + narrow)
-        grad_cells[:, cut] = grad_cells_in[:, cut]
-    for h in range(EARLY, HEADS):
-        one_head(h, qkv, grad_att, attended, grad_cells, sum_keys, sum_values)
-    hidden_f = hidden[...].astype(F32)
-    inv_rms, normed_f, normed = normed_parts(hidden_f)
+        source = grad_cells_far.at[:, part * narrow : (part + 1) * narrow]
+        target = grad_cells.at[:, part * wide : part * wide + narrow]
+        later.append(start(source, target))
+    for load in loads:
+        load.wait()
+    one_head(0, 1, qkv, grad_att, attended, late_cells, sum_keys, sum_values)
+    stores = [start(attended, attended_far), start(late_cells, late_cells_far)]
+    for load in later:
+        load.wait()
+    for part in range(3):
+        grad_cells[:, columns(part, EARLY)] = late_cells[:, columns(part, 0, 1)]
+    inv_rms, normed_f, _ = normed_parts(hidden[...].astype(F32))
     grad_normed = mm(grad_cells[...], qkv_w[...], NT)
     mixing = jnp.mean(grad_normed * normed_f, axis=-1, keepdims=True)
     grad = cotangent[...].astype(F32) + inv_rms * (grad_normed - normed_f * mixing)
@@ -293,11 +363,32 @@
     pieces[:, 2, :] = last
     pieces[:, 3, :] = moved_up(first)
     payload[:, bins:, :] = pieces[...].astype(BF)
+    for store in stores:
+        store.wait()
+
+
+def attend_rest_body(
+    hidden_far, attended_far, attended_late_far, late_cells_far, cotangent_far, out_w_far,
+    enhanced, message_far,
+    hidden, attended, late_cells, cotangent, out_w, message, grads, grads_out, semaphores,
+):
+    start = copier(semaphores)
+    narrow = EARLY * HEAD
+    loads = [
+        start(hidden_far, hidden), start(late_cells_far, late_cells),
+        start(attended_far, attended.at[:, :narrow]),
+        start(attended_late_far, attended.at[:, narrow:]),
+        start(cotangent_far, cotangent), start(out_w_far, out_w),
+    ]
+    for load in loads:
+        load.wait()
+    width = hidden.shape[1]
+    hidden_f = hidden[...].astype(F32)
+    _, _, normed = normed_parts(hidden_f)
     enhanced[...] = (hidden_f + mm(attended[...], out_w[...])).astype(BF)
-    turned = normed.T
     tm = width // 8
+    split_columns(grads, 0, SCALE * mm(normed.T, late_cells[...]))
     for part in range(3):
-        split_columns(grads, part, SCALE * mm(turned, grad_cells[:, columns(part, EARLY)]))
         spread_rows(message, part * tm, grads, part, lambda f: f, 8, tm)
     split_columns(grads_out, 0, SCALE * mm(attended[:, narrow:].T, cotangent[...]))
     few = tm // HEADS
@@ -306,6 +397,7 @@
         spread_rows(
             message, 3 * tm + group * few, grads_out, c, lambda f: 2 * f + b, 16, few
         )
+    start(message, message_far).wait()
 
 
 def stack_back(rows, left, right):
@@ -314,13 +406,22 @@
     return jnp.concatenate([after, rows.astype(BF), before], axis=-1)
 
 
-def conv_weight_body(came, slope, turned, head_message, stacked, edges, message, grads, pieces):
+def conv_weight_body(
+    came, slope_far, turned_far, head_far, edges, message, stacked_far, grad_far,
+    slope, turned, head_message, stacked, own, grads, pieces, semaphores,
+):
+    start = copier(semaphores)
+    load_slope, load_turned = start(slope_far, slope), start(turned_far, turned)
+    load_head = start(head_far, head_message)
     frames, long, width = came.shape
     bins = long - EXTRA
     half = width // 2
     cells = frames * bins
     pieces[...] = came[:, bins:, :].astype(F32)
-    grad = came[:, :bins, :].astype(F32) * slope[...]
+    own[...] = came[:, :bins, :]
+    stores = [start(own, grad_far)]
+    load_slope.wait()
+    grad = own[...].astype(F32) * slope[...]
     grad = with_borders(grad, pieces[:, 1, :], pieces[:, 2, :])
     grad_b = grad.astype(BF)
     for side, frame in enumerate((0, frames - 1)):
@@ -329,7 +430,9 @@
     stacked[...] = stack_back(
         grad_b.astype(F32), pieces[:, 0, :][:, None, :], pieces[:, 3, :][:, None, :]
     )
+    stores.append(start(stacked, stacked_far))
     flat = stacked[...].reshape(cells, 3 * width)
+    load_turned.wait()
     for i in range(3):
         block = mm(turned[:, i * bins : i * bins + cells], flat)
         for j in range(3):
@@ -339,6 +442,7 @@
             tap = (3 * i + j) * half
             grads[tap : tap + half] = upper * SCALE
             grads[9 * half + tap : 9 * half + tap + half] = lower * SCALE
+    load_head.wait()
     early = head_message.shape[1]
     message[:, :early, :] = head_message[...]
     tm = width // 8
@@ -346,16 +450,33 @@
         for e in range(9):
             rows = grads[pl.ds(9 * f + e, tm, stride=72), :]
             message[f, early + e * tm : early + (e + 1) * tm, :] = rows.astype(BF)
-
-
-def conv_data_body(came, stacked, matrix, total):
+    for store in stores:
+        store.wait()
+
+
+def conv_data_body(
+    grad_far, stacked_far, weight_far, total, matrix, grad, stacked, weight, semaphores
+):
+    start = copier(semaphores)
+    load_weight, load_stacked = start(weight_far, weight), start(stacked_far, stacked)
+    load_grad = start(grad_far, grad)
     frames, bins, triple = stacked.shape
     width = triple // 3
+    half = width // 2
+    load_weight.wait()
+    for i in range(3):
+        for j in range(3):
+            real, imag = weight[0, i, j], weight[1, i, j]
+            at = j * width
+            matrix[i, :half, at : at + half] = real
+            matrix[i, :half, at + half : at + width] = imag
+            matrix[i, half:, at : at + half] = -imag
+            matrix[i, half:, at + half : at + width] = real
+    load_stacked.wait()
+    load_grad.wait()
     inner = (frames - 1) * bins
     flat = stacked[...].reshape(frames * bins, triple)
-    total[...] = came[:, :bins, :].reshape(frames * bins, width).astype(F32) + mm(
-        flat, matrix[1], NT
-    )
+    total[...] = grad[...].reshape(frames * bins, width).astype(F32) + mm(flat, matrix[1], NT)
     total[:inner] += mm(flat[bins:], matrix[0], NT)
     total[bins:] += mm(flat[:inner], matrix[2], NT)
 
@@ -426,87 +547,122 @@
     vmem = pltpu.VMEM
     cotangent = cotangent.reshape(cells, width)
     up, down = along_tm(spectrum[frames - 1 :], spectrum[:1])
-    own, borders, matrix, matrix_back = kernel_call(
+    tile = vmem((frames, bins, width), BF)
+    tile_f = vmem((frames, bins, width), F32)
+    pieces = vmem((frames, EXTRA, width), F32)
+    square = vmem((cells, width), BF)
+    kernels = vmem(conv_weight.shape, BF)
+    own, borders, matrix = kernel_call(
         conv_own_body, "conv_own",
         [
-            ((cells, width), F32), ((2, frames, width), F32),
-            ((3, 3 * width, width), BF), ((3, width, 3 * width), BF),
-        ],
-        spectrum, conv_weight,
-        scratch=[vmem((frames, bins, 3 * width), BF)], mflops=1200,
+            ((cells, width), F32, False), ((2, frames, width), F32, False),
+            ((3, 3 * width, width), BF, False),
+        ],
+        spectrum, conv_weight, far=(0, 1),
+        scratch=[tile, kernels, vmem((frames, bins, 3 * width), BF)], copies=2, mflops=1200,
     )
     payload, slope = kernel_call(
         conv_finish_body, "conv_finish",
-        [((frames, long, width), BF), ((frames, bins, width), F32)],
-        spectrum, up, down, own, borders, matrix,
-        scratch=[vmem((frames, bins, width), F32), vmem((frames, EXTRA, width), F32)], mflops=200,
+        [((frames, long, width), BF, False), ((frames, bins, width), F32, True)],
+        spectrum, up, down, own, borders, matrix, far=(0,),
+        scratch=[tile, tile_f, tile_f, pieces], copies=2, mflops=200,
     )
     frame = exchange(payload, "freq")
+    turned_shape = (width, cells + 2 * bins)
     turned, grad_att = kernel_call(
         prepare_body, "prepare",
-        [((width, cells + 2 * bins), BF), ((cells, wide), BF)],
-        spectrum, up, down, cotangent, out_weight, mflops=300,
+        [(turned_shape, BF, True), ((cells, wide), BF, True)],
+        spectrum, up, down, cotangent, out_weight, far=(0, 3, 4),
+        scratch=[
+            tile, square, vmem((wide, width), BF), vmem(turned_shape, BF), vmem((cells, wide), BF)
+        ],
+        copies=5, mflops=300,
     )
     sums = [vmem((HEAD, cells), F32), vmem((HEAD, cells), F32)]
+    projections = vmem((width, 3 * wide), BF)
     more = tm * EARLY // HEADS
-    hidden, border_slope, qkv, attended, grad_cells, message = kernel_call(
+    narrow = EARLY * HEAD
+    border_slope, message, hidden, qkv, attended, grad_cells = kernel_call(
         attend_first_body, "attend_first",
         [
-            ((cells, width), BF), ((2, frames, width), F32), ((cells, 3 * wide), BF),
-            ((cells, wide), BF), ((cells, 3 * wide), BF),
-            ((8, 3 * EARLY * tm + 4 * more, 128), BF),
-        ],
-        frame, qkv_weight, grad_att, cotangent,
-        scratch=sums + [
-            vmem((3 * EARLY, width, HEAD), F32), vmem((2, EARLY * HEAD, HEAD), F32),
-            vmem((frames, EXTRA, width), F32),
-        ],
-        mflops=10000,
+            ((2, frames, width), F32, False), ((8, 3 * EARLY * tm + 4 * more, 128), BF, False),
+            ((cells, width), BF, True), ((cells, 3 * HEAD), BF, True), ((cells, narrow), BF, True),
+            ((cells, 3 * narrow), BF, True),
+        ],
+        frame, qkv_weight, grad_att, cotangent, far=(1, 2, 3),
+        scratch=[
+            projections, vmem((cells, narrow), BF), square, square, vmem((cells, 3 * narrow), BF),
+            vmem((cells, 3 * HEAD), BF), vmem((cells, narrow), BF), vmem((cells, 3 * narrow), BF),
+        ] + sums + [
+            vmem((3 * EARLY, width, HEAD), F32), vmem((2, narrow, HEAD), F32), pieces,
+        ],
+        copies=7, mflops=10000,
     )
     early = exchange(message, "freq")
-    back, enhanced, head_message = kernel_call(
+    back, attended_late, late_cells = kernel_call(
         attend_last_body, "attend_last",
         [
-            ((frames, long, width), BF), ((cells, width), BF),
-            ((8, 3 * tm + 4 * (tm - more), 128), BF),
-        ],
-        hidden, border_slope, qkv, attended, grad_cells, grad_att, cotangent, qkv_weight,
-        out_weight,
-        scratch=[vmem((cells, wide), BF), vmem((cells, 3 * wide), BF)] + sums + [
-            vmem((3, width, HEAD), F32), vmem((2, HEAD, HEAD), F32),
-            vmem((frames, bins, width), F32), vmem((frames, EXTRA, width), F32),
-        ],
-        mflops=5000,
-    )
-    (early,) = kernel_call(sum_body, "sum_early", [(early.shape[1:], F32)], early)
+            ((frames, long, width), BF, False), ((cells, HEAD), BF, True),
+            ((cells, 3 * HEAD), BF, True),
+        ],
+        border_slope, hidden, qkv, grad_cells, grad_att, cotangent, qkv_weight,
+        far=(1, 2, 3, 4, 5, 6),
+        scratch=[
+            square, vmem((cells, 3 * HEAD), BF), vmem((cells, HEAD), BF), square, projections,
+            vmem((cells, HEAD), BF), vmem((cells, 3 * HEAD), BF), vmem((cells, 3 * wide), BF),
+        ] + sums + [tile_f, pieces],
+        copies=10, mflops=4000,
+    )
+    back, early = lax.optimization_barrier((back, early))
     grads = exchange(back, "freq")
-    stacked, edges, message = kernel_call(
+    (early,) = kernel_call(sum_body, "sum_early", [(early.shape[1:], F32, False)], early)
+    head_shape = (8, 3 * tm + 4 * (tm - more), 128)
+    enhanced, head_message = kernel_call(
+        attend_rest_body, "attend_rest",
+        [((cells, width), BF, False), (head_shape, BF, True)],
+        hidden, attended, attended_late, late_cells, cotangent, out_weight,
+        far=(0, 1, 2, 3, 4, 5),
+        scratch=[
+            square, vmem((cells, wide), BF), vmem((cells, 3 * HEAD), BF), square,
+            vmem((wide, width), BF), vmem(head_shape, BF), vmem((3, width, HEAD), F32),
+            vmem((2, HEAD, HEAD), F32),
+        ],
+        copies=7, mflops=1000,
+    )
+    stacked_shape = (frames, bins, 3 * width)
+    edges, message, stacked, grad_tile = kernel_call(
         conv_weight_body, "conv_weight_grad",
         [
-            ((frames, bins, 3 * width), BF), ((2, 1, long, width), BF),
-            ((8, head_message.shape[1] + 9 * tm, 128), BF),
-        ],
-        grads, slope, turned, head_message,
-        scratch=[vmem((18 * (width // 2), width // 2), F32), vmem((frames, EXTRA, width), F32)],
-        mflops=1200,
+            ((2, 1, long, width), BF, False), ((8, head_shape[1] + 9 * tm, 128), BF, False),
+            (stacked_shape, BF, True), ((frames, bins, width), BF, True),
+        ],
+        grads, slope, turned, head_message, far=(1, 2, 3),
+        scratch=[
+            tile_f, vmem(turned_shape, BF), vmem(head_shape, BF), vmem(stacked_shape, BF), tile,
+            vmem((18 * (width // 2), width // 2), F32), pieces,
+        ],
+        copies=5, mflops=1200,
     )
     late = exchange(message, "freq")
     edge_up, edge_down = along_tm(edges[1:], edges[:1])
-    (total,) = kernel_call(
-        conv_data_body, "conv_data", [((cells, width), F32)],
-        grads, stacked, matrix_back, mflops=1200,
+    total, matrix_back = kernel_call(
+        conv_data_body, "conv_data",
+        [((cells, width), F32, False), ((3, width, 3 * width), BF, False)],
+        grad_tile, stacked, conv_weight, far=(0, 1, 2),
+        scratch=[tile, vmem(stacked_shape, BF), kernels], copies=3, mflops=1200,
     )
     (grad_spectrum,) = kernel_call(
-        conv_data_finish_body, "conv_data_finish", [((frames, bins, width), BF)],
+        conv_data_finish_body, "conv_data_finish", [((frames, bins, width), BF, False)],
         total, edge_up, edge_down, matrix_back, mflops=100,
     )
+    late, grad_spectrum = lax.optimization_barrier((late, grad_spectrum))
     (chunk,) = kernel_call(
-        regroup_body, "regroup", [((tm, 32, 128), BF)],
+        regroup_body, "regroup", [((tm, 32, 128), BF, False)],
         early, late,
         scratch=[vmem(late.shape[1:], F32), vmem((tm, 32, 128), F32)],
     )
     shares = kernel_call(
-        share_body, "share", [((9, 128), F32), ((12, 128), F32), ((4, 128), F32)],
+        share_body, "share", [((9, 128), F32, False), ((12, 128), F32, False), ((4, 128), F32, False)],
         exchange(chunk, "tm"),
         scratch=[vmem((32, 128), F32)],
     )

time: 135 us -> 127 us (0.941)
  local copies, waits for them, and re-layouts: 15.1 us -> 0.9 us
  Pallas kernels: 35.5 us -> 47.6 us
  blocking collectives: 13.5 us -> 21.6 us
  waiting for transfers between devices: 34.6 us -> 27.3 us
  starting transfers between devices: 34.3 us -> 27.4 us
    unnamed x34 -> x0, local copies, waits for them, and re-layouts: 14.2 us -> none
    pallas_call x11 -> x12, Pallas kernels: 35.5 us -> 47.6 us  [kernel_call(): pl.pallas_call(body, out_shape=shapes, in_specs=[hbm if n in far else nea...]
    all_to_all x1, blocking collectives: 13.5 us -> 21.6 us  [exchange(): return lax.all_to_all(array, axis, split_axis=0, concat_axis=0, tiled=True)]
    all_to_all x4, waiting for transfers between devices: 29.2 us -> 21.8 us  [exchange(): return lax.all_to_all(array, axis, split_axis=0, concat_axis=0, tiled=True)]
    all_to_all x4, starting transfers between devices: 21.4 us -> 15.1 us  [exchange(): return lax.all_to_all(array, axis, split_axis=0, concat_axis=0, tiled=True)]
    ppermute x2, starting transfers between devices: 9.05 us -> 6.74 us  [along_tm(): down = lax.ppermute(first, 'tm', [(i + 1, i) for i in range(size - 1)])]
    ppermute x2, starting transfers between devices: 3.84 us -> 5.49 us  [along_tm(): up = lax.ppermute(last, 'tm', [(i, i + 1) for i in range(size - 1)])]
  transfers between devices with their start and end apart: 8 -> 8, of which waited for: 5 -> 6; matrix products, arithmetic and copies ran while one was open for 0% -> 0% of each run, Pallas kernels for 5% -> 17%
where the time goes in v3:
time: 127 us; the launch traced here: 126 us
  Pallas kernels  47.6 us (37%)
  starting transfers between devices  27.4 us (22%)
  waiting for transfers between devices  27.3 us (21%)
  blocking collectives  21.6 us (17%)
    pallas_call x12, Pallas kernels, kernel_call(): pl.pallas_call(body, out_shape=shapes, in_specs=[hbm if n in far else nea...  47.6 us
    all_to_all x4, waiting for transfers between devices, exchange(): return lax.all_to_all(array, axis, split_axis=0, concat_axis=0, tiled=True)  21.8 us
    all_to_all x1, blocking collectives, exchange(): return lax.all_to_all(array, axis, split_axis=0, concat_axis=0, tiled=True)  21.6 us
    all_to_all x4, starting transfers between devices, exchange(): return lax.all_to_all(array, axis, split_axis=0, concat_axis=0, tiled=True)  15.1 us
    ppermute x2, starting transfers between devices, along_tm(): down = lax.ppermute(first, 'tm', [(i + 1, i) for i in range(size - 1)])  6.74 us
    ppermute x2, waiting for transfers between devices, along_tm(): up = lax.ppermute(last, 'tm', [(i, i + 1) for i in range(size - 1)])  5.5 us
    ppermute x2, starting transfers between devices, along_tm(): up = lax.ppermute(last, 'tm', [(i, i + 1) for i in range(size - 1)])  5.49 us
  transfers between devices with their start and end apart: 8, of which 6 were waited for; matrix products, arithmetic and copies ran while one was open for 0% of the time, Pallas kernels for 17%

profile of v3, /device:TPU:32, one launch (start us, length us, event | category | flops | bytes accessed | tf_op | source)
XLA Modules:
  0.0 125.6 jit_solution(2498735873793670956)
XLA Ops:
  0.6 0.9 fusion
  1.5 4.5 %collective-permute-start.1 = (bf16[1,128,256]{2,1,0:T(8,128)(2,1)S(1)}, bf16[1,128,256]{2,1,0:T(8,128)(2,1)S(1)}, u32[]{:S(2)}, u32[]{:S(2)}) collective-permute-start(bf16[1,128,256]{2,1,0:T(8,128)(2,1)S(1)} %get-tuple-element.67), channel_id=1, source_target_pairs={{8,0},{16,8},{24,16},{32,24},{40,32},{48,40},{56,48},{64,56},{72,6... | collective-permute-start | bytes 196616 | tf_op jit(solution)/shard_map/ppermute | solution.py:533
  6.0 1.9 %collective-permute-start = (bf16[1,128,256]{2,1,0:T(8,128)(2,1)S(1)}, bf16[1,128,256]{2,1,0:T(8,128)(2,1)S(1)}, u32[]{:S(2)}, u32[]{:S(2)}) collective-permute-start(bf16[1,128,256]{2,1,0:T(8,128)(2,1)S(1)} %get-tuple-element.68), channel_id=1, source_target_pairs={{0,8},{8,16},{16,24},{24,32},{32,40},{40,48},{48,56},{56,64},{64,7... | collective-permute-start | bytes 196616 | tf_op jit(solution)/shard_map/ppermute | solution.py:532
  7.9 2.6 %conv_own.1 = (f32[1024,256]{1,0:T(8,128)S(1)}, f32[2,8,256]{2,1,0:T(8,128)S(1)}, bf16[3,768,256]{2,1,0:T(8,128)(2,1)S(1)}) custom-call(bf16[8,128,256]{2,1,0:T(8,128)(2,1)} %mid_far.5, bf16[2,3,3,128,128]{4,3,2,1,0:T(8,128)(2,1)} %weight_far.3), custom_call_target="tpu_custom_call" | custom-call | flops 1200000000 | bytes 3358720 | tf_op jit(solution)/shard_map/conv_own/pallas_call | solution.py:39
  10.5 0.0 collective-permute-done.1.down
  10.5 3.8 %collective-permute-done.up = bf16[1,128,256]{2,1,0:T(8,128)(2,1)S(1)} collective-permute-done((bf16[1,128,256]{2,1,0:T(8,128)(2,1)S(1)}, bf16[1,128,256]{2,1,0:T(8,128)(2,1)S(1)}, u32[]{:S(2)}, u32[]{:S(2)}) %collective-permute-start) | collective-permute-done | bytes 65568 | tf_op jit(solution)/shard_map/ppermute | solution.py:532
  14.3 2.6 %conv_finish.1 = (bf16[8,144,256]{2,1,0:T(8,128)(2,1)}, f32[8,128,256]{2,1,0:T(8,128)}) custom-call(bf16[8,128,256]{2,1,0:T(8,128)(2,1)} %mid_far.5, bf16[1,128,256]{2,1,0:T(8,128)(2,1)S(1)} %collective-permute-done.up, bf16[1,128,256]{2,1,0:T(8,128)(2,1)S(1)} %collective-permute-done.1.down, f32[1024,256]{1,0:T(8,128)S(1)} %get-tuple-element.36.own, ...), custom_call_target="tpu_custom_call" | custom-call | flops 200000000 | bytes 4538368 | tf_op jit(solution)/shard_map/conv_finish/pallas_call | solution.py:39
  16.8 4.3 %all-to-all-start = ((bf16[8,144,256]{2,1,0:T(8,128)(2,1)}), bf16[8,144,256]{2,1,0:T(8,128)(2,1)S(1)}, u32[]{:S(2)}, u32[]{:S(2)}) async-start(bf16[8,144,256]{2,1,0:T(8,128)(2,1)} %get-tuple-element.39), calls=%async_computation | async-start | bytes 1179648 | tf_op jit(solution)/shard_map/all_to_all | solution.py:538
  21.1 3.0 %prepare.1 = (bf16[256,1280]{1,0:T(8,128)(2,1)}, bf16[1024,512]{1,0:T(8,128)(2,1)}) custom-call(bf16[8,128,256]{2,1,0:T(8,128)(2,1)} %mid_far.5, bf16[1,128,256]{2,1,0:T(8,128)(2,1)S(1)} %collective-permute-done.up, bf16[1,128,256]{2,1,0:T(8,128)(2,1)S(1)} %collective-permute-done.1.down, bf16[1024,256]{1,0:T(8,128)(2,1)} %bitcast.5, bf16[512,256]{1,0:T(8,128)(2,1)} %out_w_far.3), custom_call_target="tpu_custom_call" | custom-call | flops 300000000 | bytes 3145728 | tf_op jit(solution)/shard_map/prepare/pallas_call | solution.py:39
  24.1 8.1 %all-to-all-done.came = bf16[8,144,256]{2,1,0:T(8,128)(2,1)S(1)} async-done(((bf16[8,144,256]{2,1,0:T(8,128)(2,1)}), bf16[8,144,256]{2,1,0:T(8,128)(2,1)S(1)}, u32[]{:S(2)}, u32[]{:S(2)}) %all-to-all-start) | async-done | bytes 589856 | tf_op jit(solution)/shard_map/all_to_all | solution.py:538
  32.2 17.6 %attend_first.1 = (f32[2,8,256]{2,1,0:T(8,128)S(1)}, bf16[8,384,128]{2,1,0:T(8,128)(2,1)}, bf16[1024,256]{1,0:T(8,128)(2,1)}, bf16[1024,384]{1,0:T(8,128)(2,1)},...) custom-call(bf16[8,144,256]{2,1,0:T(8,128)(2,1)S(1)} %all-to-all-done.came, bf16[256,1536]{1,0:T(8,128)(2,1)} %qkv_w_far.3, ...), custom_call_target="tpu_custom_call" | custom-call | flops 10000000000 | bytes 8208384 | tf_op jit(solution)/shard_map/attend_first/pallas_call | solution.py:39
  49.8 3.7 %all-to-all-start.1 = ((bf16[8,384,128]{2,1,0:T(8,128)(2,1)}), bf16[8,384,128]{2,1,0:T(8,128)(2,1)S(1)}, u32[]{:S(2)}, u32[]{:S(2)}) async-start(bf16[8,384,128]{2,1,0:T(8,128)(2,1)} %get-tuple-element.50), calls=%async_computation.1 | async-start | bytes 1572864 | tf_op jit(solution)/shard_map/all_to_all | solution.py:538
  53.5 7.6 %attend_last.1 = (bf16[8,144,256]{2,1,0:T(8,128)(2,1)}, bf16[1024,128]{1,0:T(8,128)(2,1)}, bf16[1024,384]{1,0:T(8,128)(2,1)}) custom-call(f32[2,8,256]{2,1,0:T(8,128)S(1)} %get-tuple-element.43.border_slope, bf16[1024,256]{1,0:T(8,128)(2,1)} %get-tuple-element.41.hidden_far, bf16[1024,384]{1,0:T(8,128)(2,1)} %get-tuple-element.44.qkv_far, ...), custom_call_target="tpu_custom_call" | custom-call | flops 4000000000 | bytes 7684096 | tf_op jit(solution)/shard_map/attend_last/pallas_call | solution.py:39
  61.2 5.2 %all-to-all-done.1.came = bf16[8,384,128]{2,1,0:T(8,128)(2,1)S(1)} async-done(((bf16[8,384,128]{2,1,0:T(8,128)(2,1)}), bf16[8,384,128]{2,1,0:T(8,128)(2,1)S(1)}, u32[]{:S(2)}, u32[]{:S(2)}) %all-to-all-start.1) | async-done | bytes 786464 | tf_op jit(solution)/shard_map/all_to_all | solution.py:538
  66.4 3.5 %all-to-all-start.2 = ((bf16[8,144,256]{2,1,0:T(8,128)(2,1)}), bf16[8,144,256]{2,1,0:T(8,128)(2,1)S(1)}, u32[]{:S(2)}, u32[]{:S(2)}) async-start(bf16[8,144,256]{2,1,0:T(8,128)(2,1)} %get-tuple-element.51), calls=%async_computation.2 | async-start | bytes 1179648 | tf_op jit(solution)/shard_map/all_to_all | solution.py:538
  70.0 4.4 %attend_rest.1 = (bf16[1024,256]{1,0:T(8,128)(2,1)}, bf16[8,128,128]{2,1,0:T(8,128)(2,1)}) custom-call(bf16[1024,256]{1,0:T(8,128)(2,1)} %get-tuple-element.41.hidden_far, bf16[1024,384]{1,0:T(8,128)(2,1)} %get-tuple-element.42.attended_far, bf16[1024,128]{1,0:T(8,128)(2,1)} %get-tuple-element.46.attended_late_far, ...), custom_call_target="tpu_custom_call" | custom-call | flops 1000000000 | bytes 3932160 | tf_op jit(solution)/shard_map/attend_rest/pallas_call | solution.py:39
  74.3 6.6 %all-to-all-done.2.came = bf16[8,144,256]{2,1,0:T(8,128)(2,1)S(1)} async-done(((bf16[8,144,256]{2,1,0:T(8,128)(2,1)}), bf16[8,144,256]{2,1,0:T(8,128)(2,1)S(1)}, u32[]{:S(2)}, u32[]{:S(2)}) %all-to-all-start.2) | async-done | bytes 589856 | tf_op jit(solution)/shard_map/all_to_all | solution.py:538
  80.9 4.6 %conv_weight_grad.1 = (bf16[2,1,144,256]{3,2,1,0:T(8,128)(2,1)S(1)}, bf16[8,416,128]{2,1,0:T(8,128)(2,1)}, bf16[8,128,768]{2,1,0:T(8,128)(2,1)}, bf16[8,128,256]{2,1,0:T(8,128)(2,1)}) custom-call(bf16[8,144,256]{2,1,0:T(8,128)(2,1)S(1)} %all-to-all-done.2.came, f32[8,128,256]{2,1,0:T(8,128)} %get-tuple-element.52.slope_far, ...), custom_call_target="tpu_custom_call" | custom-call | flops 1200000000 | bytes 5652480 | tf_op jit(solution)/shard_map/conv_weight_grad/pallas_call | solution.py:39
  85.6 3.6 %all-to-all-start.3 = ((bf16[8,416,128]{2,1,0:T(8,128)(2,1)}), bf16[8,416,128]{2,1,0:T(8,128)(2,1)S(1)}, u32[]{:S(2)}, u32[]{:S(2)}) async-start(bf16[8,416,128]{2,1,0:T(8,128)(2,1)} %get-tuple-element.55), calls=%async_computation.3 | async-start | bytes 1703936 | tf_op jit(solution)/shard_map/all_to_all | solution.py:538
  89.1 0.1 sum_early.1.early
  89.3 2.3 %collective-permute-start.3 = (bf16[1,1,144,256]{3,2,1,0:T(8,128)(2,1)S(1)}, bf16[1,1,144,256]{3,2,1,0:T(8,128)(2,1)S(1)}, u32[]{:S(2)}, u32[]{:S(2)}) collective-permute-start(bf16[1,1,144,256]{3,2,1,0:T(8,128)(2,1)S(1)} %get-tuple-element.69), channel_id=1, source_target_pairs={{8,0},{16,8},{24,16},{32,24},{40,32},{48,40},{56,48},{64,56},{72,6... | collective-permute-start | bytes 221192 | tf_op jit(solution)/shard_map/ppermute | solution.py:533
  91.5 3.6 %collective-permute-start.2 = (bf16[1,1,144,256]{3,2,1,0:T(8,128)(2,1)S(1)}, bf16[1,1,144,256]{3,2,1,0:T(8,128)(2,1)S(1)}, u32[]{:S(2)}, u32[]{:S(2)}) collective-permute-start(bf16[1,1,144,256]{3,2,1,0:T(8,128)(2,1)S(1)} %get-tuple-element.70), channel_id=1, source_target_pairs={{0,8},{8,16},{16,24},{24,32},{32,40},{40,48},{48,56},{56,64},{64,7... | collective-permute-start | bytes 221192 | tf_op jit(solution)/shard_map/ppermute | solution.py:532
  95.1 3.0 %conv_data.1 = (f32[1024,256]{1,0:T(8,128)S(1)}, bf16[3,256,768]{2,1,0:T(8,128)(2,1)S(1)}) custom-call(bf16[8,128,256]{2,1,0:T(8,128)(2,1)} %get-tuple-element.56.grad_far, bf16[8,128,768]{2,1,0:T(8,128)(2,1)} %get-tuple-element.57.stacked_far, bf16[2,3,3,128,128]{4,3,2,1,0:T(8,128)(2,1)} %weight_far.3), custom_call_target="tpu_custom_call" | custom-call | flops 1200000000 | bytes 4915200 | tf_op jit(solution)/shard_map/conv_data/pallas_call | solution.py:39
  98.2 0.0 collective-permute-done.3.down
  98.2 1.7 %collective-permute-done.2.up = bf16[1,1,144,256]{3,2,1,0:T(8,128)(2,1)S(1)} collective-permute-done((bf16[1,1,144,256]{3,2,1,0:T(8,128)(2,1)S(1)}, bf16[1,1,144,256]{3,2,1,0:T(8,128)(2,1)S(1)}, u32[]{:S(2)}, u32[]{:S(2)}) %collective-permute-start.2) | collective-permute-done | bytes 73760 | tf_op jit(solution)/shard_map/ppermute | solution.py:532
  99.9 1.2 conv_data_finish.1
  101.1 1.8 %all-to-all-done.3.came = bf16[8,416,128]{2,1,0:T(8,128)(2,1)S(1)} async-done(((bf16[8,416,128]{2,1,0:T(8,128)(2,1)}), bf16[8,416,128]{2,1,0:T(8,128)(2,1)S(1)}, u32[]{:S(2)}, u32[]{:S(2)}) %all-to-all-start.3) | async-done | bytes 852000 | tf_op jit(solution)/shard_map/all_to_all | solution.py:538
  102.9 0.4 regroup.1
  103.3 21.6 %all_to_all.25.came = bf16[32,32,128]{2,1,0:T(8,128)(2,1)S(1)} all-to-all(bf16[32,32,128]{2,1,0:T(8,128)(2,1)S(1)} %regroup.1), channel_id=1, replica_groups=mesh['tm'=32,'freq'=8] {'tm'}, dimensions={0} | all-to-all | bytes 524288 | tf_op jit(solution)/shard_map/all_to_all | solution.py:538
  125.0 0.6 share.1
  (1 shorter events, 0.0 us)
Async XLA Ops:
  1.5 9.0 %collective-permute-start.1 = (bf16[1,128,256]{2,1,0:T(8,128)(2,1)S(1)}, bf16[1,128,256]{2,1,0:T(8,128)(2,1)S(1)}, u32[]{:S(2)}, u32[]{:S(2)}) collective-permute-start(bf16[1,128,256]{2,1,0:T(8,128)(2,1)S(1)} %get-tuple-element.67), channel_id=1, source_target_pairs={{8,0},{16,8},{24,16},{32,24},{40,32},{48,40},{56,48},{64,56},{72,6... | collective-permute-start | bytes 196616 | tf_op jit(solution)/shard_map/ppermute | solution.py:533
  6.0 8.3 %collective-permute-start = (bf16[1,128,256]{2,1,0:T(8,128)(2,1)S(1)}, bf16[1,128,256]{2,1,0:T(8,128)(2,1)S(1)}, u32[]{:S(2)}, u32[]{:S(2)}) collective-permute-start(bf16[1,128,256]{2,1,0:T(8,128)(2,1)S(1)} %get-tuple-element.68), channel_id=1, source_target_pairs={{0,8},{8,16},{16,24},{24,32},{32,40},{40,48},{48,56},{56,64},{64,7... | collective-permute-start | bytes 196616 | tf_op jit(solution)/shard_map/ppermute | solution.py:532
  16.8 15.4 %all-to-all-start = ((bf16[8,144,256]{2,1,0:T(8,128)(2,1)}), bf16[8,144,256]{2,1,0:T(8,128)(2,1)S(1)}, u32[]{:S(2)}, u32[]{:S(2)}) async-start(bf16[8,144,256]{2,1,0:T(8,128)(2,1)} %get-tuple-element.39), calls=%async_computation | async-start | bytes 1179648 | tf_op jit(solution)/shard_map/all_to_all | solution.py:538
  49.8 16.6 %all-to-all-start.1 = ((bf16[8,384,128]{2,1,0:T(8,128)(2,1)}), bf16[8,384,128]{2,1,0:T(8,128)(2,1)S(1)}, u32[]{:S(2)}, u32[]{:S(2)}) async-start(bf16[8,384,128]{2,1,0:T(8,128)(2,1)} %get-tuple-element.50), calls=%async_computation.1 | async-start | bytes 1572864 | tf_op jit(solution)/shard_map/all_to_all | solution.py:538
  66.4 14.5 %all-to-all-start.2 = ((bf16[8,144,256]{2,1,0:T(8,128)(2,1)}), bf16[8,144,256]{2,1,0:T(8,128)(2,1)S(1)}, u32[]{:S(2)}, u32[]{:S(2)}) async-start(bf16[8,144,256]{2,1,0:T(8,128)(2,1)} %get-tuple-element.51), calls=%async_computation.2 | async-start | bytes 1179648 | tf_op jit(solution)/shard_map/all_to_all | solution.py:538
  85.6 17.3 %all-to-all-start.3 = ((bf16[8,416,128]{2,1,0:T(8,128)(2,1)}), bf16[8,416,128]{2,1,0:T(8,128)(2,1)S(1)}, u32[]{:S(2)}, u32[]{:S(2)}) async-start(bf16[8,416,128]{2,1,0:T(8,128)(2,1)} %get-tuple-element.55), calls=%async_computation.3 | async-start | bytes 1703936 | tf_op jit(solution)/shard_map/all_to_all | solution.py:538
  89.3 8.9 %collective-permute-start.3 = (bf16[1,1,144,256]{3,2,1,0:T(8,128)(2,1)S(1)}, bf16[1,1,144,256]{3,2,1,0:T(8,128)(2,1)S(1)}, u32[]{:S(2)}, u32[]{:S(2)}) collective-permute-start(bf16[1,1,144,256]{3,2,1,0:T(8,128)(2,1)S(1)} %get-tuple-element.69), channel_id=1, source_target_pairs={{8,0},{16,8},{24,16},{32,24},{40,32},{48,40},{56,48},{64,56},{72,6... | collective-permute-start | bytes 221192 | tf_op jit(solution)/shard_map/ppermute | solution.py:533
  91.5 8.4 %collective-permute-start.2 = (bf16[1,1,144,256]{3,2,1,0:T(8,128)(2,1)S(1)}, bf16[1,1,144,256]{3,2,1,0:T(8,128)(2,1)S(1)}, u32[]{:S(2)}, u32[]{:S(2)}) collective-permute-start(bf16[1,1,144,256]{3,2,1,0:T(8,128)(2,1)S(1)} %get-tuple-element.70), channel_id=1, source_target_pairs={{0,8},{8,16},{16,24},{24,32},{32,40},{40,48},{48,56},{56,64},{64,7... | collective-permute-start | bytes 221192 | tf_op jit(solution)/shard_map/ppermute | solution.py:532

commit v4 on v3

v4 whole, which is shorter than its diff:
```python
import math

import jax
import jax.numpy as jnp
from jax import lax
from jax.experimental import pallas as pl
from jax.experimental.pallas import tpu as pltpu
from jax.sharding import Mesh
from jax.sharding import PartitionSpec as P

HEADS = 4
HEAD = 128
EXTRA = 16
SCALE = 1.0 / 512
LOG2E = math.log2(math.e)
FACTOR = 1.0 / math.sqrt(HEAD)
BF = jnp.bfloat16
F32 = jnp.float32
NN = (((1,), (0,)), ((), ()))
NT = (((1,), (1,)), ((), ()))
QUERY_BLOCK = 1024
GROUPS = 26
EARLY = 16


def mm(a, b, dims=NN):
    return lax.dot_general(a, b, dims, preferred_element_type=F32)


PLACES = {"any": jax.ShapeDtypeStruct, "hbm": pltpu.HBM, "vmem": pltpu.VMEM}


def kernel_call(body, name, outs, *args, far=(), scratch=(), copies=0, mflops=0, limit=48):
    shapes = [
        PLACES[away](dims, kind) for dims, kind, away in outs
    ]
    args = [
        pltpu.with_memory_space_constraint(a, pltpu.HBM) if n in far else a
        for n, a in enumerate(args)
    ]
    size = sum(math.prod(a.shape) * a.dtype.itemsize for a in (*args, *shapes))
    near, hbm = pl.BlockSpec(memory_space=pltpu.VMEM), pl.BlockSpec(memory_space=pltpu.HBM)
    scratch = list(scratch) + ([pltpu.SemaphoreType.DMA((copies,))] if copies else [])
    return pl.pallas_call(
        body,
        out_shape=shapes,
        in_specs=[hbm if n in far else near for n in range(len(args))],
        out_specs=[hbm if away == "hbm" else near for _, _, away in outs],
        scratch_shapes=scratch,
        compiler_params=pltpu.CompilerParams(vmem_limit_bytes=limit * 2**20),
        cost_estimate=pl.CostEstimate(
            flops=mflops * 10**6, bytes_accessed=size, transcendentals=0
        ),
        name=name,
    )(*args)


def copier(semaphores):
    started = []

    def start(source, target):
        copy = pltpu.make_async_copy(source, target, semaphores.at[len(started)])
        copy.start()
        started.append(copy)
        return copy

    return start


def sigmoid(v):
    return 1.0 / (1.0 + jnp.exp(-v))


def slope_of(v, sigma):
    return sigma * (1.0 + v * (1.0 - sigma))


def moved_down(rows):
    at = lax.broadcasted_iota(jnp.int32, rows.shape, 0)
    return jnp.where(at == 0, 0.0, pltpu.roll(rows, 1, 0))


def moved_up(rows):
    last = rows.shape[0] - 1
    at = lax.broadcasted_iota(jnp.int32, rows.shape, 0)
    return jnp.where(at == last, 0.0, pltpu.roll(rows, last, 0))


def with_borders(inner, first, last):
    at = lax.broadcasted_iota(jnp.int32, inner.shape, 1)
    inner = jnp.where(at == 0, first[:, None, :], inner)
    return jnp.where(at == inner.shape[1] - 1, last[:, None, :], inner)


def bins_before(rows, left):
    at = lax.broadcasted_iota(jnp.int32, rows.shape, 1)
    return jnp.where(at == 0, left, pltpu.roll(rows, 1, 1))


def bins_after(rows, right):
    last = rows.shape[1] - 1
    at = lax.broadcasted_iota(jnp.int32, rows.shape, 1)
    return jnp.where(at == last, right, pltpu.roll(rows, last, 1))


def sort_halos(even_down, odd_down, up, down):
    odd = lax.rem(lax.axis_index("y"), 2) == 1
    first, second = even_down[...], odd_down[...]
    up[...] = jnp.where(odd, first, second)
    down[...] = jnp.where(odd, second, first)


def conv_own_body(mid_far, weight_far, conv, borders, matrix, mid, weight, stacked, semaphores):
    start = copier(semaphores)
    load_weight, load_mid = start(weight_far, weight), start(mid_far, mid)
    frames, bins, width = mid.shape
    half = width // 2
    load_weight.wait()
    for i in range(3):
        for j in range(3):
            real, imag = weight[0, i, j], weight[1, i, j]
            at = j * width
            matrix[i, at : at + half, :half] = real
            matrix[i, at : at + half, half:] = imag
            matrix[i, at + half : at + width, :half] = -imag
            matrix[i, at + half : at + width, half:] = real
    load_mid.wait()
    wide = mid[...].astype(F32)
    stacked[:, :, :width] = bins_before(wide, 0.0).astype(BF)
    stacked[:, :, width : 2 * width] = mid[...]
    stacked[:, :, 2 * width :] = bins_after(wide, 0.0).astype(BF)
    inner = (frames - 1) * bins
    everything = stacked[...].reshape(frames * bins, 3 * width)
    conv[...] = mm(everything, matrix[1])
    conv[bins:] += mm(everything[:inner], matrix[0])
    conv[:inner] += mm(everything[bins:], matrix[2])
    borders[0] = mid[:, 0, :].astype(F32)
    borders[1] = mid[:, bins - 1, :].astype(F32)


def conv_finish_body(
    mid_far, even_down, odd_down, own, borders, matrix,
    payload, slope_far, mid, slope, conv, pieces, up, down, semaphores,
):
    start = copier(semaphores)
    load_mid = start(mid_far, mid)
    sort_halos(even_down, odd_down, up, down)
    frames, bins, width = mid.shape

    def stack(row):
        wide = row[...].astype(F32)
        before = bins_before(wide, 0.0).astype(BF)
        after = bins_after(wide, 0.0).astype(BF)
        return jnp.concatenate([before[0], row[0], after[0]], axis=1)

    conv[...] = own[...].reshape(frames, bins, width)
    conv[0] += mm(stack(up), matrix[0])
    conv[frames - 1] += mm(stack(down), matrix[2])

    def beyond(bin_at, side, tap):
        rows = jnp.concatenate(
            [up[:, bin_at, :].astype(F32), borders[side], down[:, bin_at, :].astype(F32)], axis=0
        )
        total = None
        for i in range(3):
            term = mm(
                rows[i : i + frames].astype(BF), matrix[i, tap * width : (tap + 1) * width, :]
            )
            total = term if total is None else total + term
        return total

    parts = (
        beyond(0, 0, 2),
        conv[:, 0, :],
        conv[:, bins - 1, :],
        beyond(bins - 1, 1, 0),
    )
    pieces[...] = jnp.zeros(pieces.shape, F32)
    for at, part in enumerate(parts):
        high = part.astype(BF).astype(F32)
        pieces[:, 2 * at, :] = high
        pieces[:, 2 * at + 1, :] = part - high
    values = conv[...]
    sigma = sigmoid(values)
    slope[...] = slope_of(values, sigma)
    store = start(slope, slope_far)
    load_mid.wait()
    hidden = mid[...].astype(F32) + values * sigma
    payload[:, :bins, :] = with_borders(hidden, borders[0], borders[1]).astype(BF)
    payload[:, bins:, :] = pieces[...].astype(BF)
    store.wait()


def prepare_body(
    mid_far, even_down, odd_down, cotangent_far, out_w_far, turned_far, grad_att_far,
    mid, cotangent, out_w, turned, grad_att, up, down, semaphores,
):
    start = copier(semaphores)
    loads = start(mid_far, mid), start(cotangent_far, cotangent), start(out_w_far, out_w)
    sort_halos(even_down, odd_down, up, down)
    for load in loads:
        load.wait()
    frames, bins, width = mid.shape
    turned[:, :bins] = up[0].T
    turned[:, bins : (frames + 1) * bins] = mid[...].reshape(frames * bins, width).T
    turned[:, (frames + 1) * bins :] = down[0].T
    grad_att[...] = mm(cotangent[...], out_w[...], NT).astype(BF)
    stores = start(turned, turned_far), start(grad_att, grad_att_far)
    for store in stores:
        store.wait()


def columns(part, h, heads=HEADS):
    at = (part * heads + h) * HEAD
    if not isinstance(h, int):
        at = pl.multiple_of(at, HEAD)
    return pl.ds(at, HEAD)


def one_head(h, heads, qkv, grad_att, attended, grad_cells, sum_keys, sum_values):
    def columns_of(part):
        return columns(part, h, heads)

    cells = qkv.shape[0]
    keys = qkv[:, columns_of(1)]
    values = qkv[:, columns_of(2)]
    values_ones = jnp.concatenate([values, jnp.ones((cells, HEAD), BF)], axis=1)
    for block in range(cells // QUERY_BLOCK):
        rows = slice(block * QUERY_BLOCK, (block + 1) * QUERY_BLOCK)
        queries = qkv[rows, columns_of(0)]
        scores = mm(queries, keys, NT)
        raised = jnp.exp2(scores - jnp.max(scores, axis=-1, keepdims=True))
        raised_b = raised.astype(BF)
        sums = mm(raised_b, values_ones)
        inverse = 1.0 / sums[:, HEAD:]
        result = sums[:, :HEAD] * inverse
        attended[rows, columns_of(0)] = result.astype(BF)
        scaled = grad_att[rows, columns_of(0)].astype(F32) * inverse
        inner = jnp.sum(scaled * result, axis=-1, keepdims=True)
        scaled_b = scaled.astype(BF)
        grad_probs = mm(scaled_b, values, NT)
        grad_scores = (raised * (grad_probs - inner)).astype(BF)
        grad_cells[rows, columns_of(0)] = (mm(grad_scores, keys) * FACTOR).astype(BF)
        new_keys = mm(queries.T, grad_scores)
        new_values = mm(scaled_b.T, raised_b)
        if block == 0:
            sum_keys[...] = new_keys
            sum_values[...] = new_values
        else:
            sum_keys[...] += new_keys
            sum_values[...] += new_values
    grad_cells[:, columns_of(1)] = (sum_keys[...] * (1.0 / LOG2E)).T.astype(BF)
    grad_cells[:, columns_of(2)] = sum_values[...].T.astype(BF)


def normed_parts(hidden_f):
    inv_rms = lax.rsqrt(jnp.mean(hidden_f * hidden_f, axis=-1, keepdims=True) + 1e-6)
    normed_f = hidden_f * inv_rms
    return inv_rms, normed_f, normed_f.astype(BF)


def split_columns(target, at, values):
    for n in range(values.shape[1] // 128):
        target[at + n] = values[:, n * 128 : (n + 1) * 128]


def attend_body(
    came, qkv_w_far, grad_att_far, cotangent_far,
    payload, hidden_far, attended_far, grad_cells_far,
    qkv_w, grad_att, cotangent, hidden, qkv, attended, grad_cells,
    sum_keys, sum_values, rows_f, pieces, semaphores,
):
    start = copier(semaphores)
    load_qkv_w = start(qkv_w_far, qkv_w)
    load_grad_att = start(grad_att_far, grad_att)
    load_cotangent = start(cotangent_far, cotangent)
    chunks, long, width = came.shape
    bins = long - EXTRA
    wide = HEADS * HEAD
    pieces[...] = came[:, bins:, :].astype(F32)
    here_first = pieces[:, 2, :] + pieces[:, 3, :]
    here_last = pieces[:, 4, :] + pieces[:, 5, :]
    first = here_first + moved_down(pieces[:, 6, :] + pieces[:, 7, :])
    last = here_last + moved_up(pieces[:, 0, :] + pieces[:, 1, :])
    sigma_first, sigma_last = sigmoid(first), sigmoid(last)
    fixed_first = came[:, 0, :].astype(F32) + first * sigma_first
    fixed_last = came[:, bins - 1, :].astype(F32) + last * sigma_last
    cells = with_borders(came[:, :bins, :].astype(F32), fixed_first, fixed_last)
    hidden[...] = cells.astype(BF).reshape(chunks * bins, width)
    stores = [start(hidden, hidden_far)]
    _, _, normed = normed_parts(hidden[...].astype(F32))
    load_qkv_w.wait()
    qkv[:, :wide] = (mm(normed, qkv_w[:, :wide]) * (FACTOR * LOG2E)).astype(BF)
    qkv[:, wide:] = mm(normed, qkv_w[:, wide:]).astype(BF)
    load_grad_att.wait()

    def head(h, carry):
        one_head(h, HEADS, qkv, grad_att, attended, grad_cells, sum_keys, sum_values)
        return carry

    lax.fori_loop(0, HEADS, head, 0)
    stores += [start(grad_cells, grad_cells_far), start(attended, attended_far)]
    load_cotangent.wait()
    inv_rms, normed_f, _ = normed_parts(hidden[...].astype(F32))
    grad_normed = mm(grad_cells[...], qkv_w[...], NT)
    mixing = jnp.mean(grad_normed * normed_f, axis=-1, keepdims=True)
    grad = cotangent[...].astype(F32) + inv_rms * (grad_normed - normed_f * mixing)
    grad_b = grad.astype(BF).reshape(chunks, bins, width)
    payload[:, :bins, :] = grad_b
    rows_f[...] = grad_b.astype(F32)
    grad_first = rows_f[:, 0, :] * slope_of(first, sigma_first)
    grad_last = rows_f[:, bins - 1, :] * slope_of(last, sigma_last)
    pieces[...] = jnp.zeros(pieces.shape, F32)
    pieces[:, 0, :] = moved_down(grad_last)
    pieces[:, 1, :] = grad_first
    pieces[:, 2, :] = grad_last
    pieces[:, 3, :] = moved_up(grad_first)
    payload[:, bins:, :] = pieces[...].astype(BF)
    for store in stores:
        store.wait()


def deal(rows, core, groups):
    for n in range(rows.shape[0]):
        for e, (source, per, at) in enumerate(groups):
            begin = per * (2 * n + core) + at
            rows[n, 8 * e : 8 * e + 8, :] = source[pl.ds(begin, 8, stride=32 * per), :]


def attend_rest_body(
    hidden_far, attended_far, grad_cells_far, cotangent_far, out_w_far, slope_far, turned_far,
    enhanced, theirs, mine_far, slope, turned,
    hidden, attended, grad_cells, cotangent, out_w, mine, grads, grads_out, rows, semaphores,
):
    start = copier(semaphores)
    load_hidden, load_cells = start(hidden_far, hidden), start(grad_cells_far, grad_cells)
    loads = [
        start(attended_far, attended), start(cotangent_far, cotangent), start(out_w_far, out_w)
    ]
    ahead = [start(slope_far, slope), start(turned_far, turned)]
    load_hidden.wait()
    hidden_f = hidden[...].astype(F32)
    _, _, normed = normed_parts(hidden_f)
    load_cells.wait()
    split_columns(grads, 0, SCALE * mm(normed.T, grad_cells[...]))
    for load in loads:
        load.wait()
    split_columns(grads_out, 0, SCALE * mm(attended[...].T, cotangent[...]))
    groups = [(grads.at[n], 1, 0) for n in range(12)]
    groups += [(grads_out.at[n % 2], 2, n // 2) for n in range(4)]
    core = lax.axis_index("core")
    deal(rows, 1 - core, groups)
    theirs[...] = rows[...].astype(BF)
    deal(rows, core, groups)
    mine[...] = rows[...].astype(BF)
    store = start(mine, mine_far)
    enhanced[...] = (hidden_f + mm(attended[...], out_w[...])).astype(BF)
    for copy in ahead:
        copy.wait()
    store.wait()


def stack_back(rows, left, right):
    after = bins_after(rows, right).astype(BF)
    before = bins_before(rows, left).astype(BF)
    return jnp.concatenate([after, rows.astype(BF), before], axis=-1)


def conv_weight_body(
    came, slope, turned, early_far, edges, theirs, mine, early, stacked_far, grad_far,
    stacked, own, grads, rows, pieces, semaphores,
):
    start = copier(semaphores)
    load_early = start(early_far, early)
    frames, long, width = came.shape
    bins = long - EXTRA
    half = width // 2
    cells = frames * bins
    pieces[...] = came[:, bins:, :].astype(F32)
    own[...] = came[:, :bins, :]
    stores = [start(own, grad_far)]
    grad = own[...].astype(F32) * slope[...]
    grad = with_borders(grad, pieces[:, 1, :], pieces[:, 2, :])
    grad_b = grad.astype(BF)
    odd = lax.rem(lax.axis_index("y"), 2) == 1
    ends = []
    for frame in (0, frames - 1):
        ends.append(
            jnp.concatenate([grad_b[frame : frame + 1], came[frame : frame + 1, bins:, :]], axis=1)
        )
    edges[0] = jnp.where(odd, ends[0], ends[1])
    edges[1] = jnp.where(odd, ends[1], ends[0])
    stacked[...] = stack_back(
        grad_b.astype(F32), pieces[:, 0, :][:, None, :], pieces[:, 3, :][:, None, :]
    )
    stores.append(start(stacked, stacked_far))
    flat = stacked[...].reshape(cells, 3 * width)
    for i in range(3):
        block = mm(turned[:, i * bins : i * bins + cells], flat)
        for j in range(3):
            at = j * width
            upper = block[:half, at : at + half] + block[half:, at + half : at + width]
            lower = block[:half, at + half : at + width] - block[half:, at : at + half]
            tap = (3 * i + j) * half
            grads[tap : tap + half] = upper * SCALE
            grads[9 * half + tap : 9 * half + tap + half] = lower * SCALE
    core = lax.axis_index("core")
    groups = [(grads, 9, e) for e in range(9)]
    rows[:, 72:, :] = jnp.zeros((rows.shape[0], 8, 128), F32)
    deal(rows, 1 - core, groups)
    theirs[...] = rows[...].astype(BF)
    deal(rows, core, groups)
    mine[...] = rows[...].astype(BF)
    load_early.wait()
    for store in stores:
        store.wait()


def conv_data_body(
    grad_far, stacked_far, weight_far, total, matrix, grad, stacked, weight, semaphores
):
    start = copier(semaphores)
    load_weight, load_stacked = start(weight_far, weight), start(stacked_far, stacked)
    load_grad = start(grad_far, grad)
    frames, bins, triple = stacked.shape
    width = triple // 3
    half = width // 2
    load_weight.wait()
    for i in range(3):
        for j in range(3):
            real, imag = weight[0, i, j], weight[1, i, j]
            at = j * width
            matrix[i, :half, at : at + half] = real
            matrix[i, :half, at + half : at + width] = imag
            matrix[i, half:, at : at + half] = -imag
            matrix[i, half:, at + half : at + width] = real
    load_stacked.wait()
    load_grad.wait()
    inner = (frames - 1) * bins
    flat = stacked[...].reshape(frames * bins, triple)
    total[...] = grad[...].reshape(frames * bins, width).astype(F32) + mm(flat, matrix[1], NT)
    total[:inner] += mm(flat[bins:], matrix[0], NT)
    total[bins:] += mm(flat[:inner], matrix[2], NT)


def conv_data_finish_body(total, even_down, odd_down, matrix, out, up, down):
    sort_halos(even_down, odd_down, up, down)
    frames, bins, width = out.shape

    def stack(edge):
        extra = edge[:, bins:, :].astype(F32)
        rows = edge[:, :bins, :].astype(F32)
        return stack_back(rows, extra[:, 0:1, :], extra[:, 3:4, :])[0]

    out[...] = total[...].reshape(frames, bins, width).astype(BF)
    out[0] = (total[:bins] + mm(stack(up), matrix[2], NT)).astype(BF)
    out[frames - 1] = (total[(frames - 1) * bins :] + mm(stack(down), matrix[0], NT)).astype(BF)


def sum_body(came, out):
    total = came[0].astype(F32)
    for source in range(1, came.shape[0]):
        total = total + came[source].astype(F32)
    out[...] = total


def join_body(early, early_got, mine, got, message):
    cut = early.shape[1]
    message[:, :cut, :] = (early[...].astype(F32) + early_got[...].astype(F32)).astype(BF)
    message[:, cut:, :] = (mine[...].astype(F32) + got[...].astype(F32)).astype(BF)


def regroup_body(came, chunk, total, rows):
    sum_body(came, total)
    rows[...] = jnp.zeros(rows.shape, F32)
    for z in range(chunk.shape[0]):
        rows[z, 0:GROUPS, :] = total[pl.ds(z, GROUPS, stride=8), :]
    chunk[...] = rows[...].astype(BF)


def share_body(came, conv, qkv, out, total):
    sum_body(came, total)
    qkv[...] = total[0:12]
    out[...] = total[12:16]
    conv[...] = total[16:25]


def pair_exchanges(first, second):
    size = lax.axis_size("z") * lax.axis_size("y")
    near = [(i, i ^ 1) for i in range(size)]
    apart = [(i, i + 1 if i % 2 else i - 1) for i in range(1, size - 1)]
    return lax.ppermute(first, ("z", "y"), near), lax.ppermute(second, ("z", "y"), apart)


def exchange(array, axis):
    return lax.all_to_all(array, axis, split_axis=0, concat_axis=0, tiled=True)


def swap_cores(array):
    return lax.ppermute(array, "core", [(0, 1), (1, 0)])


def shards(spectrum, conv_weight, qkv_weight, out_weight, cotangent):
    frames, bins, width = spectrum.shape
    cells = frames * bins
    wide = HEADS * HEAD
    long = bins + EXTRA
    vmem = pltpu.VMEM
    cotangent = cotangent.reshape(cells, width)
    odd = lax.rem(lax.axis_index("y"), 2) == 1
    first, last = spectrum[:1], spectrum[frames - 1 :]
    halo_a, halo_b = pair_exchanges(jnp.where(odd, first, last), jnp.where(odd, last, first))
    tile = vmem((frames, bins, width), BF)
    tile_f = vmem((frames, bins, width), F32)
    pieces = vmem((frames, EXTRA, width), F32)
    square = vmem((cells, width), BF)
    kernels = vmem(conv_weight.shape, BF)
    halo = vmem((1, bins, width), BF)
    own, borders, matrix = kernel_call(
        conv_own_body, "conv_own",
        [
            ((cells, width), F32, "any"), ((2, frames, width), F32, "any"),
            ((3, 3 * width, width), BF, "any"),
        ],
        spectrum, conv_weight, far=(0, 1),
        scratch=[tile, kernels, vmem((frames, bins, 3 * width), BF)], copies=2, mflops=1200,
    )
    payload, slope = kernel_call(
        conv_finish_body, "conv_finish",
        [((frames, long, width), BF, "any"), ((frames, bins, width), F32, "hbm")],
        spectrum, halo_a, halo_b, own, borders, matrix, far=(0,),
        scratch=[tile, tile_f, tile_f, pieces, halo, halo], copies=2, mflops=200,
    )
    frame = exchange(payload, ("x", "core"))
    turned_shape = (width, cells + 2 * bins)
    turned, grad_att = kernel_call(
        prepare_body, "prepare",
        [(turned_shape, BF, "hbm"), ((cells, wide), BF, "hbm")],
        spectrum, halo_a, halo_b, cotangent, out_weight, far=(0, 3, 4),
        scratch=[
            tile, square, vmem((wide, width), BF), vmem(turned_shape, BF),
            vmem((cells, wide), BF), halo, halo,
        ],
        copies=5, mflops=300,
    )
    attended_v, cells_v = vmem((cells, wide), BF), vmem((cells, 3 * wide), BF)
    back, hidden, attended, grad_cells = kernel_call(
        attend_body, "attend",
        [
            ((frames, long, width), BF, "any"), ((cells, width), BF, "hbm"),
            ((cells, wide), BF, "hbm"), ((cells, 3 * wide), BF, "hbm"),
        ],
        frame, qkv_weight, grad_att, cotangent, far=(1, 2, 3),
        scratch=[
            vmem((width, 3 * wide), BF), attended_v, square, square, cells_v, attended_v, cells_v,
            vmem((HEAD, cells), F32), vmem((HEAD, cells), F32), tile_f, pieces,
        ],
        copies=6, mflops=15000,
    )
    grads = exchange(back, ("x", "core"))
    ring = lax.axis_size("y") * lax.axis_size("x")
    early_shape = (ring, 8 * EARLY, 128)
    late_shape = (ring, 8 * (GROUPS - EARLY), 128)
    enhanced, theirs, mine, slope, turned = kernel_call(
        attend_rest_body, "attend_rest",
        [
            ((cells, width), BF, "any"), (early_shape, BF, "any"), (early_shape, BF, "hbm"),
            ((frames, bins, width), F32, "vmem"), (turned_shape, BF, "vmem"),
        ],
        hidden, attended, grad_cells, cotangent, out_weight, slope, turned,
        far=(0, 1, 2, 3, 4, 5, 6),
        scratch=[
            square, attended_v, cells_v, square, vmem((wide, width), BF), vmem(early_shape, BF),
            vmem((12, width, HEAD), F32), vmem((2, wide, HEAD), F32), vmem(early_shape, F32),
        ],
        copies=8, mflops=1500, limit=40,
    )
    theirs, grads = lax.optimization_barrier((theirs, grads))
    got = swap_cores(theirs)
    stacked_shape = (frames, bins, 3 * width)
    edges, theirs, late_mine, early, stacked, grad_tile = kernel_call(
        conv_weight_body, "conv_weight_grad",
        [
            ((2, 1, long, width), BF, "any"), (late_shape, BF, "any"), (late_shape, BF, "any"),
            (early_shape, BF, "any"), (stacked_shape, BF, "hbm"),
            ((frames, bins, width), BF, "hbm"),
        ],
        grads, slope, turned, mine, far=(3,),
        scratch=[
            vmem(stacked_shape, BF), tile,
            vmem((18 * (width // 2), width // 2), F32), vmem(late_shape, F32), pieces,
        ],
        copies=3, mflops=1200, limit=40,
    )
    late_got = swap_cores(theirs)
    edges, late_got = lax.optimization_barrier((edges, late_got))
    (message,) = kernel_call(
        join_body, "join", [((ring, 8 * GROUPS, 128), BF, "any")], early, got, late_mine,
        late_got,
    )
    late = exchange(message, ("y", "x"))
    edge_a, edge_b = pair_exchanges(edges[0], edges[1])
    total, matrix_back = kernel_call(
        conv_data_body, "conv_data",
        [((cells, width), F32, "any"), ((3, width, 3 * width), BF, "any")],
        grad_tile, stacked, conv_weight, far=(0, 1, 2),
        scratch=[tile, vmem(stacked_shape, BF), kernels], copies=3, mflops=1200,
    )
    (grad_spectrum,) = kernel_call(
        conv_data_finish_body, "conv_data_finish", [((frames, bins, width), BF, "any")],
        total, edge_a, edge_b, matrix_back,
        scratch=[vmem((1, long, width), BF), vmem((1, long, width), BF)], mflops=100,
    )
    late, grad_spectrum = lax.optimization_barrier((late, grad_spectrum))
    (chunk,) = kernel_call(
        regroup_body, "regroup", [((lax.axis_size("z"), 32, 128), BF, "any")],
        late,
        scratch=[vmem(late.shape[1:], F32), vmem((lax.axis_size("z"), 32, 128), F32)],
    )
    shares = kernel_call(
        share_body, "share", [((9, 128), F32, "any"), ((12, 128), F32, "any"), ((4, 128), F32, "any")],
        exchange(chunk, "z"),
        scratch=[vmem((32, 128), F32)],
    )
    return (enhanced.reshape(1, cells, width), grad_spectrum, *[s.reshape(-1) for s in shares])


def solution(mesh):
    mesh = Mesh(mesh.devices.reshape(8, 4, 4, 2), ("z", "y", "x", "core"))
    every = P(("z", "y", "x", "core"))
    tiles, rows = P(("z", "y"), ("x", "core"), None), P(("z", "y", "x", "core"), None, None)
    return jax.shard_map(
        shards,
        mesh=mesh,
        in_specs=(tiles, P(), P(), P(), rows),
        out_specs=(rows, tiles, every, every, every),
        check_vma=False,
    )
```

time: 127 us -> 108 us (0.85)
  waiting for transfers between devices: 27.3 us -> 20 us
  blocking collectives: 21.6 us -> 15.7 us
  starting transfers between devices: 27.4 us -> 23.6 us
  Pallas kernels: 47.6 us -> 46 us
    all_to_all x4 -> x3, waiting for transfers between devices: 21.8 us -> 12.3 us  [exchange(): return lax.all_to_all(array, axis, split_axis=0, concat_axis=0, tiled=True)]
    all_to_all x1, blocking collectives: 21.6 us -> 15.7 us  [exchange(): return lax.all_to_all(array, axis, split_axis=0, concat_axis=0, tiled=True)]
    all_to_all x4 -> x3, starting transfers between devices: 15.1 us -> 12.5 us  [exchange(): return lax.all_to_all(array, axis, split_axis=0, concat_axis=0, tiled=True)]
    ppermute x4 -> x6, waiting for transfers between devices: 5.51 us -> 7.7 us  [the longest x2 4.07 us: pair_exchanges(): lax.ppermute(first, ('z', 'y'), near)]
    pallas_call x12 -> x11, Pallas kernels: 47.6 us -> 46 us  [kernel_call(): pl.pallas_call(body, out_shape=shapes, in_specs=[hbm if n in far else nea...]
    ppermute x4 -> x6, starting transfers between devices: 12.2 us -> 11.1 us  [the longest x2 9.06 us: pair_exchanges(): lax.ppermute(second, ('z', 'y'), apart)]
  transfers between devices with their start and end apart: 8 -> 9, of which waited for: 6 -> 8; matrix products, arithmetic and copies ran while one was open for 0% -> 0% of each run, Pallas kernels for 17% -> 19%
where the time goes in v4:
time: 108 us; the launch traced here: 107 us
  Pallas kernels  46 us (43%)
  starting transfers between devices  23.6 us (22%)
  waiting for transfers between devices  20 us (19%)
  blocking collectives  15.7 us (15%)
    pallas_call x11, Pallas kernels, kernel_call(): pl.pallas_call(body, out_shape=shapes, in_specs=[hbm if n in far else nea...  46 us
    all_to_all x1, blocking collectives, exchange(): return lax.all_to_all(array, axis, split_axis=0, concat_axis=0, tiled=True)  15.7 us
    all_to_all x3, starting transfers between devices, exchange(): return lax.all_to_all(array, axis, split_axis=0, concat_axis=0, tiled=True)  12.5 us
    all_to_all x3, waiting for transfers between devices, exchange(): return lax.all_to_all(array, axis, split_axis=0, concat_axis=0, tiled=True)  12.3 us
    ppermute x2, starting transfers between devices, pair_exchanges(): lax.ppermute(second, ('z', 'y'), apart)  9.06 us
    ppermute x2, waiting for transfers between devices, pair_exchanges(): lax.ppermute(first, ('z', 'y'), near)  4.07 us
    ppermute x2, waiting for transfers between devices, pair_exchanges(): lax.ppermute(second, ('z', 'y'), apart)  2.37 us
  transfers between devices with their start and end apart: 9, of which 8 were waited for; matrix products, arithmetic and copies ran while one was open for 0% of the time, Pallas kernels for 19%

profile of v4, /device:TPU:32, one launch (start us, length us, event | category | flops | bytes accessed | tf_op | source)
XLA Modules:
  0.0 107.0 jit_solution(796308784615626949)
XLA Ops:
  0.6 0.9 broadcast_select_fusion
  1.5 4.5 %collective-permute-start.1 = (bf16[1,128,256]{2,1,0:T(8,128)(2,1)S(1)}, bf16[1,128,256]{2,1,0:T(8,128)(2,1)S(1)}, u32[]{:S(2)}, u32[]{:S(2)}) collective-permute-start(bf16[1,128,256]{2,1,0:T(8,128)(2,1)S(1)} %get-tuple-element.71), channel_id=1, source_target_pairs={{8,16},{16,8},{24,32},{32,24},{40,48},{48,40},{56,64},{64,56},{72,... | collective-permute-start | bytes 196616 | tf_op jit(solution)/shard_map/ppermute | solution.py:492
  6.0 0.7 collective-permute-start
  6.7 2.5 %conv_own.1 = (f32[1024,256]{1,0:T(8,128)S(1)}, f32[2,8,256]{2,1,0:T(8,128)S(1)}, bf16[3,768,256]{2,1,0:T(8,128)(2,1)S(1)}) custom-call(bf16[8,128,256]{2,1,0:T(8,128)(2,1)} %mid_far.5, bf16[2,3,3,128,128]{4,3,2,1,0:T(8,128)(2,1)} %weight_far.3), custom_call_target="tpu_custom_call" | custom-call | flops 1200000000 | bytes 3358720 | tf_op jit(solution)/shard_map/conv_own/pallas_call | solution.py:44
  9.2 0.6 collective-permute-done.1.odd_down
  9.8 0.6 collective-permute-done.even_down
  10.4 2.5 %conv_finish.1 = (bf16[8,144,256]{2,1,0:T(8,128)(2,1)}, f32[8,128,256]{2,1,0:T(8,128)}) custom-call(bf16[8,128,256]{2,1,0:T(8,128)(2,1)} %mid_far.5, bf16[1,128,256]{2,1,0:T(8,128)(2,1)S(1)} %collective-permute-done.even_down, bf16[1,128,256]{2,1,0:T(8,128)(2,1)S(1)} %collective-permute-done.1.odd_down, f32[1024,256]{1,0:T(8,128)S(1)} %get-tuple-element.38.own, ...), custom_call_target="tpu_custom_call" | custom-call | flops 200000000 | bytes 4538368 | tf_op jit(solution)/shard_map/conv_finish/pallas_call | solution.py:44
  12.9 4.3 %all-to-all-start = ((bf16[8,144,256]{2,1,0:T(8,128)(2,1)}), bf16[8,144,256]{2,1,0:T(8,128)(2,1)S(1)}, u32[]{:S(2)}, u32[]{:S(2)}) async-start(bf16[8,144,256]{2,1,0:T(8,128)(2,1)} %get-tuple-element.41), calls=%async_computation | async-start | bytes 1179648 | tf_op jit(solution)/shard_map/all_to_all | solution.py:496
  17.2 3.0 %prepare.1 = (bf16[256,1280]{1,0:T(8,128)(2,1)}, bf16[1024,512]{1,0:T(8,128)(2,1)}) custom-call(bf16[8,128,256]{2,1,0:T(8,128)(2,1)} %mid_far.5, bf16[1,128,256]{2,1,0:T(8,128)(2,1)S(1)} %collective-permute-done.even_down, bf16[1,128,256]{2,1,0:T(8,128)(2,1)S(1)} %collective-permute-done.1.odd_down, bf16[1024,256]{1,0:T(8,128)(2,1)} %bitcast.9, ...), custom_call_target="tpu_custom_call" | custom-call | flops 300000000 | bytes 3145728 | tf_op jit(solution)/shard_map/prepare/pallas_call | solution.py:44
  20.2 8.0 %all-to-all-done.came = bf16[8,144,256]{2,1,0:T(8,128)(2,1)S(1)} async-done(((bf16[8,144,256]{2,1,0:T(8,128)(2,1)}), bf16[8,144,256]{2,1,0:T(8,128)(2,1)S(1)}, u32[]{:S(2)}, u32[]{:S(2)}) %all-to-all-start) | async-done | bytes 589856 | tf_op jit(solution)/shard_map/all_to_all | solution.py:496
  28.3 21.2 %attend.1 = (bf16[8,144,256]{2,1,0:T(8,128)(2,1)}, bf16[1024,256]{1,0:T(8,128)(2,1)}, bf16[1024,512]{1,0:T(8,128)(2,1)}, bf16[1024,1536]{1,0:T(8,128)(2,1)}) custom-call(bf16[8,144,256]{2,1,0:T(8,128)(2,1)S(1)} %all-to-all-done.came, bf16[256,1536]{1,0:T(8,128)(2,1)} %qkv_w_far.1, bf16[1024,512]{1,0:T(8,128)(2,1)} %get-tuple-element.42.grad_att_far, ...), custom_call_target="tpu_custom_call" | custom-call | flops 15000000512 | bytes 8257536 | tf_op jit(solution)/shard_map/attend/pallas_call | solution.py:44
  49.5 3.7 %all-to-all-start.1 = ((bf16[8,144,256]{2,1,0:T(8,128)(2,1)}), bf16[8,144,256]{2,1,0:T(8,128)(2,1)S(1)}, u32[]{:S(2)}, u32[]{:S(2)}) async-start(bf16[8,144,256]{2,1,0:T(8,128)(2,1)} %get-tuple-element.50), calls=%async_computation.1 | async-start | bytes 1179648 | tf_op jit(solution)/shard_map/all_to_all | solution.py:496
  53.2 7.1 %attend_rest.1 = (bf16[1024,256]{1,0:T(8,128)(2,1)}, bf16[16,128,128]{2,1,0:T(8,128)(2,1)S(1)}, bf16[16,128,128]{2,1,0:T(8,128)(2,1)}, f32[8,128,256]{2,1,0:T(8,128)S(1)}, bf16[256,1280]{1,0:T(8,128)(2,1)S(1)}) custom-call(bf16[1024,256]{1,0:T(8,128)(2,1)} %get-tuple-element.43.hidden_far, bf16[1024,512]{1,0:T(8,128)(2,1)} %get-tuple-element.44.attended_far, ...), custom_call_target="tpu_custom_call" | custom-call | flops 1500000000 | bytes 10485760 | tf_op jit(solution)/shard_map/attend_rest/pallas_call | solution.py:44
  60.4 3.6 %all-to-all-done.1.came = bf16[8,144,256]{2,1,0:T(8,128)(2,1)S(1)} async-done(((bf16[8,144,256]{2,1,0:T(8,128)(2,1)}), bf16[8,144,256]{2,1,0:T(8,128)(2,1)S(1)}, u32[]{:S(2)}, u32[]{:S(2)}) %all-to-all-start.1) | async-done | bytes 589856 | tf_op jit(solution)/shard_map/all_to_all | solution.py:496
  64.0 0.0 collective-permute-start.2
  64.0 3.4 %conv_weight_grad.1 = (bf16[2,1,144,256]{3,2,1,0:T(8,128)(2,1)S(1)}, bf16[16,80,128]{2,1,0:T(8,128)(2,1)S(1)}, bf16[16,80,128]{2,1,0:T(8,128)(2,1)S(1)}, bf16[16...) custom-call(bf16[8,144,256]{2,1,0:T(8,128)(2,1)S(1)} %all-to-all-done.1.came, ...), custom_call_target="tpu_custom_call" | custom-call | flops 1200000000 | bytes 6242304 | tf_op jit(solution)/shard_map/conv_weight_grad/pallas_call | solution.py:44
  67.5 0.6 collective-permute-start.3
  68.1 1.3 %collective-permute-done.3.got = bf16[16,80,128]{2,1,0:T(8,128)(2,1)S(1)} collective-permute-done((bf16[16,80,128]{2,1,0:T(8,128)(2,1)S(1)}, bf16[16,80,128]{2,1,0:T(8,128)(2,1)S(1)}, u32[]{:S(2)}, u32[]{:S(2)}) %collective-permute-start.3) | collective-permute-done | bytes 327712 | tf_op jit(solution)/shard_map/ppermute | solution.py:500
  69.3 0.0 collective-permute-done.2.early_got
  69.3 1.1 %join.1 = bf16[16,208,128]{2,1,0:T(8,128)(2,1)} custom-call(bf16[16,128,128]{2,1,0:T(8,128)(2,1)S(1)} %get-tuple-element.55.early, bf16[16,128,128]{2,1,0:T(8,128)(2,1)S(1)} %collective-permute-done.2.early_got, bf16[16,80,128]{2,1,0:T(8,128)(2,1)S(1)} %get-tuple-element.57.mine, bf16[16,80,128]{2,1,0:T(8,128)(2,1)S(1)} %collective-permute-done.3.got), custom_call_target="tpu_custom_call" | custom-call | bytes 2555904 | tf_op jit(solution)/shard_map/join/pallas_call | solution.py:44
  70.4 4.4 %all-to-all-start.2 = ((bf16[16,208,128]{2,1,0:T(8,128)(2,1)}), bf16[16,208,128]{2,1,0:T(8,128)(2,1)S(1)}, u32[]{:S(2)}, u32[]{:S(2)}) async-start(bf16[16,208,128]{2,1,0:T(8,128)(2,1)} %join.1), calls=%async_computation.2 | async-start | bytes 1703936 | tf_op jit(solution)/shard_map/all_to_all | solution.py:496
  74.9 4.6 %collective-permute-start.5 = (bf16[1,144,256]{2,1,0:T(8,128)(2,1)S(1)}, bf16[1,144,256]{2,1,0:T(8,128)(2,1)S(1)}, u32[]{:S(2)}, u32[]{:S(2)}) collective-permute-start(bf16[1,144,256]{2,1,0:T(8,128)(2,1)S(1)} %get-tuple-element.73), channel_id=1, source_target_pairs={{8,16},{16,8},{24,32},{32,24},{40,48},{48,40},{56,64},{64,56},{72,... | collective-permute-start | bytes 221192 | tf_op jit(solution)/shard_map/ppermute | solution.py:492
  79.5 0.8 collective-permute-start.4
  80.3 3.0 %conv_data.1 = (f32[1024,256]{1,0:T(8,128)S(1)}, bf16[3,256,768]{2,1,0:T(8,128)(2,1)S(1)}) custom-call(bf16[8,128,256]{2,1,0:T(8,128)(2,1)} %get-tuple-element.61.grad_far, bf16[8,128,768]{2,1,0:T(8,128)(2,1)} %get-tuple-element.62.stacked_far, bf16[2,3,3,128,128]{4,3,2,1,0:T(8,128)(2,1)} %weight_far.3), custom_call_target="tpu_custom_call" | custom-call | flops 1200000000 | bytes 4915200 | tf_op jit(solution)/shard_map/conv_data/pallas_call | solution.py:44
  83.3 1.8 %collective-permute-done.5.odd_down = bf16[1,144,256]{2,1,0:T(8,128)(2,1)S(1)} collective-permute-done((bf16[1,144,256]{2,1,0:T(8,128)(2,1)S(1)}, bf16[1,144,256]{2,1,0:T(8,128)(2,1)S(1)}, u32[]{:S(2)}, u32[]{:S(2)}) %collective-permute-start.5) | collective-permute-done | bytes 73760 | tf_op jit(solution)/shard_map/ppermute | solution.py:492
  85.1 3.5 %collective-permute-done.4.even_down = bf16[1,144,256]{2,1,0:T(8,128)(2,1)S(1)} collective-permute-done((bf16[1,144,256]{2,1,0:T(8,128)(2,1)S(1)}, bf16[1,144,256]{2,1,0:T(8,128)(2,1)S(1)}, u32[]{:S(2)}, u32[]{:S(2)}) %collective-permute-start.4) | collective-permute-done | bytes 73760 | tf_op jit(solution)/shard_map/ppermute | solution.py:492
  88.6 1.2 %conv_data_finish.1 = bf16[8,128,256]{2,1,0:T(8,128)(2,1)} custom-call(f32[1024,256]{1,0:T(8,128)S(1)} %get-tuple-element.63.total, bf16[1,144,256]{2,1,0:T(8,128)(2,1)S(1)} %collective-permute-done.4.even_down, bf16[1,144,256]{2,1,0:T(8,128)(2,1)S(1)} %collective-permute-done.5.odd_down, bf16[3,256,768]{2,1,0:T(8,128)(2,1)S(1)} %get-tuple-element.65.matrix), custom_call_target="tpu_custom_call" | custom-call | flops 100000000 | bytes 2899968 | tf_op jit(solution)/shard_map/conv_data_finish/pallas_call | solution.py:44
  89.8 0.7 all-to-all-done.2.came
  90.5 0.1 regroup.1
  90.6 15.7 %all_to_all.20.came = bf16[8,32,128]{2,1,0:T(8,128)(2,1)S(1)} all-to-all(bf16[8,32,128]{2,1,0:T(8,128)(2,1)S(1)} %regroup.1), channel_id=1, replica_groups=mesh['z'=8,'y'=4,'x'=4,'core'=2] {'z'}, dimensions={0} | all-to-all | bytes 131072 | tf_op jit(solution)/shard_map/all_to_all | solution.py:496
  106.4 0.6 share.1
  (1 shorter events, 0.0 us)
Async XLA Ops:
  1.5 8.3 %collective-permute-start.1 = (bf16[1,128,256]{2,1,0:T(8,128)(2,1)S(1)}, bf16[1,128,256]{2,1,0:T(8,128)(2,1)S(1)}, u32[]{:S(2)}, u32[]{:S(2)}) collective-permute-start(bf16[1,128,256]{2,1,0:T(8,128)(2,1)S(1)} %get-tuple-element.71), channel_id=1, source_target_pairs={{8,16},{16,8},{24,32},{32,24},{40,48},{48,40},{56,64},{64,56},{72,... | collective-permute-start | bytes 196616 | tf_op jit(solution)/shard_map/ppermute | solution.py:492
  6.0 4.4 %collective-permute-start = (bf16[1,128,256]{2,1,0:T(8,128)(2,1)S(1)}, bf16[1,128,256]{2,1,0:T(8,128)(2,1)S(1)}, u32[]{:S(2)}, u32[]{:S(2)}) collective-permute-start(bf16[1,128,256]{2,1,0:T(8,128)(2,1)S(1)} %get-tuple-element.72), channel_id=1, source_target_pairs={{0,8},{8,0},{16,24},{24,16},{32,40},{40,32},{48,56},{56,48},{64,72... | collective-permute-start | bytes 196616 | tf_op jit(solution)/shard_map/ppermute | solution.py:492
  12.9 15.4 %all-to-all-start = ((bf16[8,144,256]{2,1,0:T(8,128)(2,1)}), bf16[8,144,256]{2,1,0:T(8,128)(2,1)S(1)}, u32[]{:S(2)}, u32[]{:S(2)}) async-start(bf16[8,144,256]{2,1,0:T(8,128)(2,1)} %get-tuple-element.41), calls=%async_computation | async-start | bytes 1179648 | tf_op jit(solution)/shard_map/all_to_all | solution.py:496
  49.5 14.5 %all-to-all-start.1 = ((bf16[8,144,256]{2,1,0:T(8,128)(2,1)}), bf16[8,144,256]{2,1,0:T(8,128)(2,1)S(1)}, u32[]{:S(2)}, u32[]{:S(2)}) async-start(bf16[8,144,256]{2,1,0:T(8,128)(2,1)} %get-tuple-element.50), calls=%async_computation.1 | async-start | bytes 1179648 | tf_op jit(solution)/shard_map/all_to_all | solution.py:496
  64.0 5.3 %collective-permute-start.2 = (bf16[16,128,128]{2,1,0:T(8,128)(2,1)S(1)}, bf16[16,128,128]{2,1,0:T(8,128)(2,1)S(1)}, u32[]{:S(2)}, u32[]{:S(2)}) collective-permute-start(bf16[16,128,128]{2,1,0:T(8,128)(2,1)S(1)} %get-tuple-element.56), channel_id=1, source_target_pairs={{0,1},{1,0},{2,3},{3,2},{4,5},{5,4},{6,7},{7,6},{8,9},{9,8},{10,11... | collective-permute-start | bytes 1572872 | tf_op jit(solution)/shard_map/ppermute | solution.py:500
  67.5 1.9 %collective-permute-start.3 = (bf16[16,80,128]{2,1,0:T(8,128)(2,1)S(1)}, bf16[16,80,128]{2,1,0:T(8,128)(2,1)S(1)}, u32[]{:S(2)}, u32[]{:S(2)}) collective-permute-start(bf16[16,80,128]{2,1,0:T(8,128)(2,1)S(1)} %get-tuple-element.59), channel_id=1, source_target_pairs={{0,1},{1,0},{2,3},{3,2},{4,5},{5,4},{6,7},{7,6},{8,9},{9,8},{10,11... | collective-permute-start | bytes 983048 | tf_op jit(solution)/shard_map/ppermute | solution.py:500
  70.4 20.1 %all-to-all-start.2 = ((bf16[16,208,128]{2,1,0:T(8,128)(2,1)}), bf16[16,208,128]{2,1,0:T(8,128)(2,1)S(1)}, u32[]{:S(2)}, u32[]{:S(2)}) async-start(bf16[16,208,128]{2,1,0:T(8,128)(2,1)} %join.1), calls=%async_computation.2 | async-start | bytes 1703936 | tf_op jit(solution)/shard_map/all_to_all | solution.py:496
  74.9 10.2 %collective-permute-start.5 = (bf16[1,144,256]{2,1,0:T(8,128)(2,1)S(1)}, bf16[1,144,256]{2,1,0:T(8,128)(2,1)S(1)}, u32[]{:S(2)}, u32[]{:S(2)}) collective-permute-start(bf16[1,144,256]{2,1,0:T(8,128)(2,1)S(1)} %get-tuple-element.73), channel_id=1, source_target_pairs={{8,16},{16,8},{24,32},{32,24},{40,48},{48,40},{56,64},{64,56},{72,... | collective-permute-start | bytes 221192 | tf_op jit(solution)/shard_map/ppermute | solution.py:492
  79.5 9.2 %collective-permute-start.4 = (bf16[1,144,256]{2,1,0:T(8,128)(2,1)S(1)}, bf16[1,144,256]{2,1,0:T(8,128)(2,1)S(1)}, u32[]{:S(2)}, u32[]{:S(2)}) collective-permute-start(bf16[1,144,256]{2,1,0:T(8,128)(2,1)S(1)} %get-tuple-element.74), channel_id=1, source_target_pairs={{0,8},{8,0},{16,24},{24,16},{32,40},{40,32},{48,56},{56,48},{64,72... | collective-permute-start | bytes 221192 | tf_op jit(solution)/shard_map/ppermute | solution.py:492

commit v5 on v4

--- a/solution.py
+++ b/solution.py
@@ -140,7 +140,7 @@
 
 def conv_finish_body(
     mid_far, even_down, odd_down, own, borders, matrix,
-    payload, slope_far, mid, slope, conv, pieces, up, down, semaphores,
+    payload, conv, mid, pieces, up, down, semaphores,
 ):
     start = copier(semaphores)
     load_mid = start(mid_far, mid)
@@ -182,22 +182,22 @@
         pieces[:, 2 * at + 1, :] = part - high
     values = conv[...]
     sigma = sigmoid(values)
-    slope[...] = slope_of(values, sigma)
-    store = start(slope, slope_far)
     load_mid.wait()
     hidden = mid[...].astype(F32) + values * sigma
     payload[:, :bins, :] = with_borders(hidden, borders[0], borders[1]).astype(BF)
     payload[:, bins:, :] = pieces[...].astype(BF)
-    store.wait()
 
 
 def prepare_body(
-    mid_far, even_down, odd_down, cotangent_far, out_w_far, turned_far, grad_att_far,
-    mid, cotangent, out_w, turned, grad_att, up, down, semaphores,
+    conv, mid_far, even_down, odd_down, cotangent_far, out_w_far,
+    turned_far, grad_att_far, slope_far,
+    slope, mid, cotangent, out_w, turned, grad_att, up, down, semaphores,
 ):
     start = copier(semaphores)
     loads = start(mid_far, mid), start(cotangent_far, cotangent), start(out_w_far, out_w)
     sort_halos(even_down, odd_down, up, down)
+    slope[...] = slope_of(conv[...], sigmoid(conv[...]))
+    stores = [start(slope, slope_far)]
     for load in loads:
         load.wait()
     frames, bins, width = mid.shape
@@ -205,7 +205,7 @@
     turned[:, bins : (frames + 1) * bins] = mid[...].reshape(frames * bins, width).T
     turned[:, (frames + 1) * bins :] = down[0].T
     grad_att[...] = mm(cotangent[...], out_w[...], NT).astype(BF)
-    stores = start(turned, turned_far), start(grad_att, grad_att_far)
+    stores += [start(turned, turned_far), start(grad_att, grad_att_far)]
     for store in stores:
         store.wait()
 
@@ -268,7 +268,7 @@
     came, qkv_w_far, grad_att_far, cotangent_far,
     payload, hidden_far, attended_far, grad_cells_far,
     qkv_w, grad_att, cotangent, hidden, qkv, attended, grad_cells,
-    sum_keys, sum_values, rows_f, pieces, semaphores,
+    sum_keys, sum_values, pieces, semaphores,
 ):
     start = copier(semaphores)
     load_qkv_w = start(qkv_w_far, qkv_w)
@@ -307,9 +307,8 @@
     grad = cotangent[...].astype(F32) + inv_rms * (grad_normed - normed_f * mixing)
     grad_b = grad.astype(BF).reshape(chunks, bins, width)
     payload[:, :bins, :] = grad_b
-    rows_f[...] = grad_b.astype(F32)
-    grad_first = rows_f[:, 0, :] * slope_of(first, sigma_first)
-    grad_last = rows_f[:, bins - 1, :] * slope_of(last, sigma_last)
+    grad_first = payload[:, 0, :].astype(F32) * slope_of(first, sigma_first)
+    grad_last = payload[:, bins - 1, :].astype(F32) * slope_of(last, sigma_last)
     pieces[...] = jnp.zeros(pieces.shape, F32)
     pieces[:, 0, :] = moved_down(grad_last)
     pieces[:, 1, :] = grad_first
@@ -525,23 +524,26 @@
         spectrum, conv_weight, far=(0, 1),
         scratch=[tile, kernels, vmem((frames, bins, 3 * width), BF)], copies=2, mflops=1200,
     )
-    payload, slope = kernel_call(
+    payload, conv = kernel_call(
         conv_finish_body, "conv_finish",
-        [((frames, long, width), BF, "any"), ((frames, bins, width), F32, "hbm")],
+        [((frames, long, width), BF, "any"), ((frames, bins, width), F32, "vmem")],
         spectrum, halo_a, halo_b, own, borders, matrix, far=(0,),
-        scratch=[tile, tile_f, tile_f, pieces, halo, halo], copies=2, mflops=200,
+        scratch=[tile, pieces, halo, halo], copies=1, mflops=200,
     )
     frame = exchange(payload, ("x", "core"))
     turned_shape = (width, cells + 2 * bins)
-    turned, grad_att = kernel_call(
+    turned, grad_att, slope = kernel_call(
         prepare_body, "prepare",
-        [(turned_shape, BF, "hbm"), ((cells, wide), BF, "hbm")],
-        spectrum, halo_a, halo_b, cotangent, out_weight, far=(0, 3, 4),
+        [
+            (turned_shape, BF, "hbm"), ((cells, wide), BF, "hbm"),
+            ((frames, bins, width), F32, "hbm"),
+        ],
+        conv, spectrum, halo_a, halo_b, cotangent, out_weight, far=(1, 4, 5),
         scratch=[
-            tile, square, vmem((wide, width), BF), vmem(turned_shape, BF),
+            tile_f, tile, square, vmem((wide, width), BF), vmem(turned_shape, BF),
             vmem((cells, wide), BF), halo, halo,
         ],
-        copies=5, mflops=300,
+        copies=6, mflops=300,
     )
     attended_v, cells_v = vmem((cells, wide), BF), vmem((cells, 3 * wide), BF)
     back, hidden, attended, grad_cells = kernel_call(
@@ -553,7 +555,7 @@
         frame, qkv_weight, grad_att, cotangent, far=(1, 2, 3),
         scratch=[
             vmem((width, 3 * wide), BF), attended_v, square, square, cells_v, attended_v, cells_v,
-            vmem((HEAD, cells), F32), vmem((HEAD, cells), F32), tile_f, pieces,
+            vmem((HEAD, cells), F32), vmem((HEAD, cells), F32), pieces,
         ],
         copies=6, mflops=15000,
     )
@@ -593,29 +595,29 @@
         copies=3, mflops=1200, limit=40,
     )
     late_got = swap_cores(theirs)
-    edges, late_got = lax.optimization_barrier((edges, late_got))
     (message,) = kernel_call(
         join_body, "join", [((ring, 8 * GROUPS, 128), BF, "any")], early, got, late_mine,
         late_got,
     )
     late = exchange(message, ("y", "x"))
-    edge_a, edge_b = pair_exchanges(edges[0], edges[1])
     total, matrix_back = kernel_call(
         conv_data_body, "conv_data",
-        [((cells, width), F32, "any"), ((3, width, 3 * width), BF, "any")],
+        [((cells, width), F32, "vmem"), ((3, width, 3 * width), BF, "vmem")],
         grad_tile, stacked, conv_weight, far=(0, 1, 2),
         scratch=[tile, vmem(stacked_shape, BF), kernels], copies=3, mflops=1200,
     )
+    late, total = lax.optimization_barrier((late, total))
+    (chunk,) = kernel_call(
+        regroup_body, "regroup", [((lax.axis_size("z"), 32, 128), BF, "any")],
+        late,
+        scratch=[vmem(late.shape[1:], F32), vmem((lax.axis_size("z"), 32, 128), F32)],
+    )
+    chunk, edges = lax.optimization_barrier((chunk, edges))
+    edge_a, edge_b = pair_exchanges(edges[0], edges[1])
     (grad_spectrum,) = kernel_call(
         conv_data_finish_body, "conv_data_finish", [((frames, bins, width), BF, "any")],
         total, edge_a, edge_b, matrix_back,
         scratch=[vmem((1, long, width), BF), vmem((1, long, width), BF)], mflops=100,
-    )
-    late, grad_spectrum = lax.optimization_barrier((late, grad_spectrum))
-    (chunk,) = kernel_call(
-        regroup_body, "regroup", [((lax.axis_size("z"), 32, 128), BF, "any")],
-        late,
-        scratch=[vmem(late.shape[1:], F32), vmem((lax.axis_size("z"), 32, 128), F32)],
     )
     shares = kernel_call(
         share_body, "share", [((9, 128), F32, "any"), ((12, 128), F32, "any"), ((4, 128), F32, "any")],

time: 108 us -> 111 us (1.028)
  blocking collectives: 15.7 us -> 0 us
  waiting for transfers between devices: 20 us -> 32.2 us
  starting transfers between devices: 23.6 us -> 29.8 us
    all_to_all x1 -> x0, blocking collectives: 15.7 us -> none  [exchange(): return lax.all_to_all(array, axis, split_axis=0, concat_axis=0, tiled=True)]
    all_to_all x3 -> x4, waiting for transfers between devices: 12.3 us -> 24.2 us  [exchange(): return lax.all_to_all(array, axis, split_axis=0, concat_axis=0, tiled=True)]
    all_to_all x3 -> x4, starting transfers between devices: 12.5 us -> 21.3 us  [exchange(): return lax.all_to_all(array, axis, split_axis=0, concat_axis=0, tiled=True)]
    ppermute x2, waiting for transfers between devices: 2.37 us -> 6.16 us  [pair_exchanges(): lax.ppermute(second, ('z', 'y'), apart)]
    ppermute x2, waiting for transfers between devices: 4.07 us -> 0.56 us  [pair_exchanges(): lax.ppermute(first, ('z', 'y'), near)]
    ppermute x2, starting transfers between devices: 9.06 us -> 6.65 us  [pair_exchanges(): lax.ppermute(second, ('z', 'y'), apart)]
  transfers between devices with their start and end apart: 9 -> 10, of which waited for: 8 -> 7; matrix products, arithmetic and copies ran while one was open for 0% -> 0% of each run, Pallas kernels for 19% -> 19%
where the time goes in v5:
time: 111 us; the launch traced here: 110 us
  Pallas kernels  46.2 us (42%)
  waiting for transfers between devices  32.2 us (29%)
  starting transfers between devices  29.8 us (27%)
    pallas_call x11, Pallas kernels, kernel_call(): pl.pallas_call(body, out_shape=shapes, in_specs=[hbm if n in far else nea...  46.2 us
    all_to_all x4, waiting for transfers between devices, exchange(): return lax.all_to_all(array, axis, split_axis=0, concat_axis=0, tiled=True)  24.2 us
    all_to_all x4, starting transfers between devices, exchange(): return lax.all_to_all(array, axis, split_axis=0, concat_axis=0, tiled=True)  21.3 us
    ppermute x2, starting transfers between devices, pair_exchanges(): lax.ppermute(second, ('z', 'y'), apart)  6.65 us
    ppermute x2, waiting for transfers between devices, pair_exchanges(): lax.ppermute(second, ('z', 'y'), apart)  6.16 us
  transfers between devices with their start and end apart: 10, of which 7 were waited for; matrix products, arithmetic and copies ran while one was open for 0% of the time, Pallas kernels for 19%

profile of v5, /device:TPU:32, one launch (start us, length us, event | category | flops | bytes accessed | tf_op | source)
XLA Modules:
  0.0 109.8 jit_solution(4036510175994807559)
XLA Ops:
  0.6 0.9 broadcast_select_fusion
  1.5 4.5 %collective-permute-start.1 = (bf16[1,128,256]{2,1,0:T(8,128)(2,1)S(1)}, bf16[1,128,256]{2,1,0:T(8,128)(2,1)S(1)}, u32[]{:S(2)}, u32[]{:S(2)}) collective-permute-start(bf16[1,128,256]{2,1,0:T(8,128)(2,1)S(1)} %get-tuple-element.73), channel_id=1, source_target_pairs={{8,16},{16,8},{24,32},{32,24},{40,48},{48,40},{56,64},{64,56},{72,... | collective-permute-start | bytes 196616 | tf_op jit(solution)/shard_map/ppermute | solution.py:491
  6.0 0.7 collective-permute-start
  6.7 2.5 %conv_own.1 = (f32[1024,256]{1,0:T(8,128)S(1)}, f32[2,8,256]{2,1,0:T(8,128)S(1)}, bf16[3,768,256]{2,1,0:T(8,128)(2,1)S(1)}) custom-call(bf16[8,128,256]{2,1,0:T(8,128)(2,1)} %mid_far.5, bf16[2,3,3,128,128]{4,3,2,1,0:T(8,128)(2,1)} %weight_far.3), custom_call_target="tpu_custom_call" | custom-call | flops 1200000000 | bytes 3358720 | tf_op jit(solution)/shard_map/conv_own/pallas_call | solution.py:44
  9.2 0.6 collective-permute-done.1.odd_down
  9.8 0.6 collective-permute-done.even_down
  10.4 2.2 %conv_finish.1 = (bf16[8,144,256]{2,1,0:T(8,128)(2,1)}, f32[8,128,256]{2,1,0:T(8,128)S(1)}) custom-call(bf16[8,128,256]{2,1,0:T(8,128)(2,1)} %mid_far.5, bf16[1,128,256]{2,1,0:T(8,128)(2,1)S(1)} %collective-permute-done.even_down, bf16[1,128,256]{2,1,0:T(8,128)(2,1)S(1)} %collective-permute-done.1.odd_down, f32[1024,256]{1,0:T(8,128)S(1)} %get-tuple-element.39.own, ...), custom_call_target="tpu_custom_call" | custom-call | flops 200000000 | bytes 4538368 | tf_op jit(solution)/shard_map/conv_finish/pallas_call | solution.py:44
  12.6 4.3 %all-to-all-start = ((bf16[8,144,256]{2,1,0:T(8,128)(2,1)}), bf16[8,144,256]{2,1,0:T(8,128)(2,1)S(1)}, u32[]{:S(2)}, u32[]{:S(2)}) async-start(bf16[8,144,256]{2,1,0:T(8,128)(2,1)} %get-tuple-element.42), calls=%async_computation | async-start | bytes 1179648 | tf_op jit(solution)/shard_map/all_to_all | solution.py:495
  16.9 3.0 %prepare.1 = (bf16[256,1280]{1,0:T(8,128)(2,1)}, bf16[1024,512]{1,0:T(8,128)(2,1)}, f32[8,128,256]{2,1,0:T(8,128)}) custom-call(f32[8,128,256]{2,1,0:T(8,128)S(1)} %get-tuple-element.43.conv, bf16[8,128,256]{2,1,0:T(8,128)(2,1)} %mid_far.5, bf16[1,128,256]{2,1,0:T(8,128)(2,1)S(1)} %collective-permute-done.even_down, ...), custom_call_target="tpu_custom_call" | custom-call | flops 300000000 | bytes 5242880 | tf_op jit(solution)/shard_map/prepare/pallas_call | solution.py:44
  19.9 8.0 %all-to-all-done.came = bf16[8,144,256]{2,1,0:T(8,128)(2,1)S(1)} async-done(((bf16[8,144,256]{2,1,0:T(8,128)(2,1)}), bf16[8,144,256]{2,1,0:T(8,128)(2,1)S(1)}, u32[]{:S(2)}, u32[]{:S(2)}) %all-to-all-start) | async-done | bytes 589856 | tf_op jit(solution)/shard_map/all_to_all | solution.py:495
  28.0 21.2 %attend.1 = (bf16[8,144,256]{2,1,0:T(8,128)(2,1)}, bf16[1024,256]{1,0:T(8,128)(2,1)}, bf16[1024,512]{1,0:T(8,128)(2,1)}, bf16[1024,1536]{1,0:T(8,128)(2,1)}) custom-call(bf16[8,144,256]{2,1,0:T(8,128)(2,1)S(1)} %all-to-all-done.came, bf16[256,1536]{1,0:T(8,128)(2,1)} %qkv_w_far.1, bf16[1024,512]{1,0:T(8,128)(2,1)} %get-tuple-element.44.grad_att_far, ...), custom_call_target="tpu_custom_call" | custom-call | flops 15000000512 | bytes 8257536 | tf_op jit(solution)/shard_map/attend/pallas_call | solution.py:44
  49.1 3.7 %all-to-all-start.1 = ((bf16[8,144,256]{2,1,0:T(8,128)(2,1)}), bf16[8,144,256]{2,1,0:T(8,128)(2,1)S(1)}, u32[]{:S(2)}, u32[]{:S(2)}) async-start(bf16[8,144,256]{2,1,0:T(8,128)(2,1)} %get-tuple-element.52), calls=%async_computation.1 | async-start | bytes 1179648 | tf_op jit(solution)/shard_map/all_to_all | solution.py:495
  52.9 7.1 %attend_rest.1 = (bf16[1024,256]{1,0:T(8,128)(2,1)}, bf16[16,128,128]{2,1,0:T(8,128)(2,1)S(1)}, bf16[16,128,128]{2,1,0:T(8,128)(2,1)}, f32[8,128,256]{2,1,0:T(8,128)S(1)}, bf16[256,1280]{1,0:T(8,128)(2,1)S(1)}) custom-call(bf16[1024,256]{1,0:T(8,128)(2,1)} %get-tuple-element.45.hidden_far, bf16[1024,512]{1,0:T(8,128)(2,1)} %get-tuple-element.46.attended_far, ...), custom_call_target="tpu_custom_call" | custom-call | flops 1500000000 | bytes 10485760 | tf_op jit(solution)/shard_map/attend_rest/pallas_call | solution.py:44
  60.0 3.6 %all-to-all-done.1.came = bf16[8,144,256]{2,1,0:T(8,128)(2,1)S(1)} async-done(((bf16[8,144,256]{2,1,0:T(8,128)(2,1)}), bf16[8,144,256]{2,1,0:T(8,128)(2,1)S(1)}, u32[]{:S(2)}, u32[]{:S(2)}) %all-to-all-start.1) | async-done | bytes 589856 | tf_op jit(solution)/shard_map/all_to_all | solution.py:495
  63.7 0.0 collective-permute-start.2
  63.7 3.4 %conv_weight_grad.1 = (bf16[2,1,144,256]{3,2,1,0:T(8,128)(2,1)S(1)}, bf16[16,80,128]{2,1,0:T(8,128)(2,1)S(1)}, bf16[16,80,128]{2,1,0:T(8,128)(2,1)S(1)}, bf16[16...) custom-call(bf16[8,144,256]{2,1,0:T(8,128)(2,1)S(1)} %all-to-all-done.1.came, ...), custom_call_target="tpu_custom_call" | custom-call | flops 1200000000 | bytes 6242304 | tf_op jit(solution)/shard_map/conv_weight_grad/pallas_call | solution.py:44
  67.1 0.6 collective-permute-start.3
  67.7 1.3 %collective-permute-done.3.got = bf16[16,80,128]{2,1,0:T(8,128)(2,1)S(1)} collective-permute-done((bf16[16,80,128]{2,1,0:T(8,128)(2,1)S(1)}, bf16[16,80,128]{2,1,0:T(8,128)(2,1)S(1)}, u32[]{:S(2)}, u32[]{:S(2)}) %collective-permute-start.3) | collective-permute-done | bytes 327712 | tf_op jit(solution)/shard_map/ppermute | solution.py:499
  68.9 0.0 collective-permute-done.2.early_got
  69.0 1.1 %join.1 = bf16[16,208,128]{2,1,0:T(8,128)(2,1)} custom-call(bf16[16,128,128]{2,1,0:T(8,128)(2,1)S(1)} %get-tuple-element.57.early, bf16[16,128,128]{2,1,0:T(8,128)(2,1)S(1)} %collective-permute-done.2.early_got, bf16[16,80,128]{2,1,0:T(8,128)(2,1)S(1)} %get-tuple-element.59.mine, bf16[16,80,128]{2,1,0:T(8,128)(2,1)S(1)} %collective-permute-done.3.got), custom_call_target="tpu_custom_call" | custom-call | bytes 2555904 | tf_op jit(solution)/shard_map/join/pallas_call | solution.py:44
  70.1 4.4 %all-to-all-start.2 = ((bf16[16,208,128]{2,1,0:T(8,128)(2,1)}), bf16[16,208,128]{2,1,0:T(8,128)(2,1)S(1)}, u32[]{:S(2)}, u32[]{:S(2)}) async-start(bf16[16,208,128]{2,1,0:T(8,128)(2,1)} %join.1), calls=%async_computation.2 | async-start | bytes 1703936 | tf_op jit(solution)/shard_map/all_to_all | solution.py:495
  74.5 3.0 %conv_data.1 = (f32[1024,256]{1,0:T(8,128)S(1)}, bf16[3,256,768]{2,1,0:T(8,128)(2,1)S(1)}) custom-call(bf16[8,128,256]{2,1,0:T(8,128)(2,1)} %get-tuple-element.61.grad_far, bf16[8,128,768]{2,1,0:T(8,128)(2,1)} %get-tuple-element.62.stacked_far, bf16[2,3,3,128,128]{4,3,2,1,0:T(8,128)(2,1)} %weight_far.3), custom_call_target="tpu_custom_call" | custom-call | flops 1200000000 | bytes 4915200 | tf_op jit(solution)/shard_map/conv_data/pallas_call | solution.py:44
  77.5 12.5 %all-to-all-done.2.came = bf16[16,208,128]{2,1,0:T(8,128)(2,1)S(1)} async-done(((bf16[16,208,128]{2,1,0:T(8,128)(2,1)}), bf16[16,208,128]{2,1,0:T(8,128)(2,1)S(1)}, u32[]{:S(2)}, u32[]{:S(2)}) %all-to-all-start.2) | async-done | bytes 852000 | tf_op jit(solution)/shard_map/all_to_all | solution.py:495
  90.1 0.8 regroup.1
  90.8 8.8 %all-to-all-start.3 = ((bf16[8,32,128]{2,1,0:T(8,128)(2,1)}), bf16[8,32,128]{2,1,0:T(8,128)(2,1)S(1)}, u32[]{:S(2)}, u32[]{:S(2)}) async-start(bf16[8,32,128]{2,1,0:T(8,128)(2,1)} %regroup.1), calls=%async_computation.3 | async-start | bytes 131072 | tf_op jit(solution)/shard_map/all_to_all | solution.py:495
  99.6 2.2 %collective-permute-start.5 = (bf16[1,144,256]{2,1,0:T(8,128)(2,1)S(1)}, bf16[1,144,256]{2,1,0:T(8,128)(2,1)S(1)}, u32[]{:S(2)}, u32[]{:S(2)}) collective-permute-start(bf16[1,144,256]{2,1,0:T(8,128)(2,1)S(1)} %get-tuple-element.75), channel_id=1, source_target_pairs={{8,16},{16,8},{24,32},{32,24},{40,48},{48,40},{56,64},{64,56},{72,... | collective-permute-start | bytes 221192 | tf_op jit(solution)/shard_map/ppermute | solution.py:491
  101.8 0.6 collective-permute-start.4
  102.4 5.6 %collective-permute-done.5.odd_down = bf16[1,144,256]{2,1,0:T(8,128)(2,1)S(1)} collective-permute-done((bf16[1,144,256]{2,1,0:T(8,128)(2,1)S(1)}, bf16[1,144,256]{2,1,0:T(8,128)(2,1)S(1)}, u32[]{:S(2)}, u32[]{:S(2)}) %collective-permute-start.5) | collective-permute-done | bytes 73760 | tf_op jit(solution)/shard_map/ppermute | solution.py:491
  108.0 0.0 collective-permute-done.4.even_down
  108.0 1.2 %conv_data_finish.1 = bf16[8,128,256]{2,1,0:T(8,128)(2,1)} custom-call(f32[1024,256]{1,0:T(8,128)S(1)} %get-tuple-element.64.total, bf16[1,144,256]{2,1,0:T(8,128)(2,1)S(1)} %collective-permute-done.4.even_down, bf16[1,144,256]{2,1,0:T(8,128)(2,1)S(1)} %collective-permute-done.5.odd_down, bf16[3,256,768]{2,1,0:T(8,128)(2,1)S(1)} %get-tuple-element.68.matrix), custom_call_target="tpu_custom_call" | custom-call | flops 100000000 | bytes 2899968 | tf_op jit(solution)/shard_map/conv_data_finish/pallas_call | solution.py:44
  109.2 0.0 all-to-all-done.3.came
  109.2 0.6 share.1
  (1 shorter events, 0.0 us)
Async XLA Ops:
  1.5 8.3 %collective-permute-start.1 = (bf16[1,128,256]{2,1,0:T(8,128)(2,1)S(1)}, bf16[1,128,256]{2,1,0:T(8,128)(2,1)S(1)}, u32[]{:S(2)}, u32[]{:S(2)}) collective-permute-start(bf16[1,128,256]{2,1,0:T(8,128)(2,1)S(1)} %get-tuple-element.73), channel_id=1, source_target_pairs={{8,16},{16,8},{24,32},{32,24},{40,48},{48,40},{56,64},{64,56},{72,... | collective-permute-start | bytes 196616 | tf_op jit(solution)/shard_map/ppermute | solution.py:491
  6.0 4.4 %collective-permute-start = (bf16[1,128,256]{2,1,0:T(8,128)(2,1)S(1)}, bf16[1,128,256]{2,1,0:T(8,128)(2,1)S(1)}, u32[]{:S(2)}, u32[]{:S(2)}) collective-permute-start(bf16[1,128,256]{2,1,0:T(8,128)(2,1)S(1)} %get-tuple-element.74), channel_id=1, source_target_pairs={{0,8},{8,0},{16,24},{24,16},{32,40},{40,32},{48,56},{56,48},{64,72... | collective-permute-start | bytes 196616 | tf_op jit(solution)/shard_map/ppermute | solution.py:491
  12.6 15.4 %all-to-all-start = ((bf16[8,144,256]{2,1,0:T(8,128)(2,1)}), bf16[8,144,256]{2,1,0:T(8,128)(2,1)S(1)}, u32[]{:S(2)}, u32[]{:S(2)}) async-start(bf16[8,144,256]{2,1,0:T(8,128)(2,1)} %get-tuple-element.42), calls=%async_computation | async-start | bytes 1179648 | tf_op jit(solution)/shard_map/all_to_all | solution.py:495
  49.1 14.5 %all-to-all-start.1 = ((bf16[8,144,256]{2,1,0:T(8,128)(2,1)}), bf16[8,144,256]{2,1,0:T(8,128)(2,1)S(1)}, u32[]{:S(2)}, u32[]{:S(2)}) async-start(bf16[8,144,256]{2,1,0:T(8,128)(2,1)} %get-tuple-element.52), calls=%async_computation.1 | async-start | bytes 1179648 | tf_op jit(solution)/shard_map/all_to_all | solution.py:495
  63.7 5.3 %collective-permute-start.2 = (bf16[16,128,128]{2,1,0:T(8,128)(2,1)S(1)}, bf16[16,128,128]{2,1,0:T(8,128)(2,1)S(1)}, u32[]{:S(2)}, u32[]{:S(2)}) collective-permute-start(bf16[16,128,128]{2,1,0:T(8,128)(2,1)S(1)} %get-tuple-element.58), channel_id=1, source_target_pairs={{0,1},{1,0},{2,3},{3,2},{4,5},{5,4},{6,7},{7,6},{8,9},{9,8},{10,11... | collective-permute-start | bytes 1572872 | tf_op jit(solution)/shard_map/ppermute | solution.py:499
  67.1 1.9 %collective-permute-start.3 = (bf16[16,80,128]{2,1,0:T(8,128)(2,1)S(1)}, bf16[16,80,128]{2,1,0:T(8,128)(2,1)S(1)}, u32[]{:S(2)}, u32[]{:S(2)}) collective-permute-start(bf16[16,80,128]{2,1,0:T(8,128)(2,1)S(1)} %get-tuple-element.60), channel_id=1, source_target_pairs={{0,1},{1,0},{2,3},{3,2},{4,5},{5,4},{6,7},{7,6},{8,9},{9,8},{10,11... | collective-permute-start | bytes 983048 | tf_op jit(solution)/shard_map/ppermute | solution.py:499
  70.1 20.0 %all-to-all-start.2 = ((bf16[16,208,128]{2,1,0:T(8,128)(2,1)}), bf16[16,208,128]{2,1,0:T(8,128)(2,1)S(1)}, u32[]{:S(2)}, u32[]{:S(2)}) async-start(bf16[16,208,128]{2,1,0:T(8,128)(2,1)} %join.1), calls=%async_computation.2 | async-start | bytes 1703936 | tf_op jit(solution)/shard_map/all_to_all | solution.py:495
  90.8 18.4 %all-to-all-start.3 = ((bf16[8,32,128]{2,1,0:T(8,128)(2,1)}), bf16[8,32,128]{2,1,0:T(8,128)(2,1)S(1)}, u32[]{:S(2)}, u32[]{:S(2)}) async-start(bf16[8,32,128]{2,1,0:T(8,128)(2,1)} %regroup.1), calls=%async_computation.3 | async-start | bytes 131072 | tf_op jit(solution)/shard_map/all_to_all | solution.py:495
  99.6 8.4 %collective-permute-start.5 = (bf16[1,144,256]{2,1,0:T(8,128)(2,1)S(1)}, bf16[1,144,256]{2,1,0:T(8,128)(2,1)S(1)}, u32[]{:S(2)}, u32[]{:S(2)}) collective-permute-start(bf16[1,144,256]{2,1,0:T(8,128)(2,1)S(1)} %get-tuple-element.75), channel_id=1, source_target_pairs={{8,16},{16,8},{24,32},{32,24},{40,48},{48,40},{56,64},{64,56},{72,... | collective-permute-start | bytes 221192 | tf_op jit(solution)/shard_map/ppermute | solution.py:491
  101.8 6.2 %collective-permute-start.4 = (bf16[1,144,256]{2,1,0:T(8,128)(2,1)S(1)}, bf16[1,144,256]{2,1,0:T(8,128)(2,1)S(1)}, u32[]{:S(2)}, u32[]{:S(2)}) collective-permute-start(bf16[1,144,256]{2,1,0:T(8,128)(2,1)S(1)} %get-tuple-element.76), channel_id=1, source_target_pairs={{0,8},{8,0},{16,24},{24,16},{32,40},{40,32},{48,56},{56,48},{64,72... | collective-permute-start | bytes 221192 | tf_op jit(solution)/shard_map/ppermute | solution.py:491

commit v6 on v5

--- a/solution.py
+++ b/solution.py
@@ -294,11 +294,8 @@
     qkv[:, wide:] = mm(normed, qkv_w[:, wide:]).astype(BF)
     load_grad_att.wait()
 
-    def head(h, carry):
+    for h in range(HEADS):
         one_head(h, HEADS, qkv, grad_att, attended, grad_cells, sum_keys, sum_values)
-        return carry
-
-    lax.fori_loop(0, HEADS, head, 0)
     stores += [start(grad_cells, grad_cells_far), start(attended, attended_far)]
     load_cotangent.wait()
     inv_rms, normed_f, _ = normed_parts(hidden[...].astype(F32))
@@ -595,6 +592,7 @@
         copies=3, mflops=1200, limit=40,
     )
     late_got = swap_cores(theirs)
+    edges, late_got = lax.optimization_barrier((edges, late_got))
     (message,) = kernel_call(
         join_body, "join", [((ring, 8 * GROUPS, 128), BF, "any")], early, got, late_mine,
         late_got,
@@ -606,14 +604,13 @@
         grad_tile, stacked, conv_weight, far=(0, 1, 2),
         scratch=[tile, vmem(stacked_shape, BF), kernels], copies=3, mflops=1200,
     )
-    late, total = lax.optimization_barrier((late, total))
+    edge_a, edge_b = pair_exchanges(edges[0], edges[1])
+    late, total, edge_a, edge_b = lax.optimization_barrier((late, total, edge_a, edge_b))
     (chunk,) = kernel_call(
         regroup_body, "regroup", [((lax.axis_size("z"), 32, 128), BF, "any")],
         late,
         scratch=[vmem(late.shape[1:], F32), vmem((lax.axis_size("z"), 32, 128), F32)],
     )
-    chunk, edges = lax.optimization_barrier((chunk, edges))
-    edge_a, edge_b = pair_exchanges(edges[0], edges[1])
     (grad_spectrum,) = kernel_call(
         conv_data_finish_body, "conv_data_finish", [((frames, bins, width), BF, "any")],
         total, edge_a, edge_b, matrix_back,

time: 111 us -> 109 us (0.982)
  waiting for transfers between devices: 32.2 us -> 27.1 us
  starting transfers between devices: 29.8 us -> 32.5 us
    all_to_all x4, waiting for transfers between devices: 24.2 us -> 19.4 us  [exchange(): return lax.all_to_all(array, axis, split_axis=0, concat_axis=0, tiled=True)]
    ppermute x2, waiting for transfers between devices: 6.16 us -> 2.37 us  [pair_exchanges(): lax.ppermute(second, ('z', 'y'), apart)]
    ppermute x2, waiting for transfers between devices: 0.56 us -> 4.07 us  [pair_exchanges(): lax.ppermute(first, ('z', 'y'), near)]
    ppermute x2, starting transfers between devices: 6.65 us -> 9.06 us  [pair_exchanges(): lax.ppermute(second, ('z', 'y'), apart)]
  transfers between devices with their start and end apart: 10 -> 10, of which waited for: 7 -> 9; matrix products, arithmetic and copies ran while one was open for 0% -> 0% of each run, Pallas kernels for 19% -> 19%
where the time goes in v6:
time: 109 us; the launch traced here: 108 us
  Pallas kernels  46.4 us (43%)
  starting transfers between devices  32.5 us (30%)
  waiting for transfers between devices  27.1 us (25%)
    pallas_call x11, Pallas kernels, kernel_call(): pl.pallas_call(body, out_shape=shapes, in_specs=[hbm if n in far else nea...  46.4 us
    all_to_all x4, starting transfers between devices, exchange(): return lax.all_to_all(array, axis, split_axis=0, concat_axis=0, tiled=True)  21.3 us
    all_to_all x4, waiting for transfers between devices, exchange(): return lax.all_to_all(array, axis, split_axis=0, concat_axis=0, tiled=True)  19.4 us
    ppermute x2, starting transfers between devices, pair_exchanges(): lax.ppermute(second, ('z', 'y'), apart)  9.06 us
    ppermute x2, waiting for transfers between devices, pair_exchanges(): lax.ppermute(first, ('z', 'y'), near)  4.07 us
    ppermute x2, waiting for transfers between devices, pair_exchanges(): lax.ppermute(second, ('z', 'y'), apart)  2.37 us
  transfers between devices with their start and end apart: 10, of which 9 were waited for; matrix products, arithmetic and copies ran while one was open for 0% of the time, Pallas kernels for 19%

profile of v6, /device:TPU:32, one launch (start us, length us, event | category | flops | bytes accessed | tf_op | source)
XLA Modules:
  0.0 107.6 jit_solution(1174402937511362730)
XLA Ops:
  0.6 0.9 broadcast_select_fusion
  1.5 4.5 %collective-permute-start.1 = (bf16[1,128,256]{2,1,0:T(8,128)(2,1)S(1)}, bf16[1,128,256]{2,1,0:T(8,128)(2,1)S(1)}, u32[]{:S(2)}, u32[]{:S(2)}) collective-permute-start(bf16[1,128,256]{2,1,0:T(8,128)(2,1)S(1)} %get-tuple-element.77), channel_id=1, source_target_pairs={{8,16},{16,8},{24,32},{32,24},{40,48},{48,40},{56,64},{64,56},{72,... | collective-permute-start | bytes 196616 | tf_op jit(solution)/shard_map/ppermute | solution.py:488
  6.0 0.7 collective-permute-start
  6.7 2.5 %conv_own.1 = (f32[1024,256]{1,0:T(8,128)S(1)}, f32[2,8,256]{2,1,0:T(8,128)S(1)}, bf16[3,768,256]{2,1,0:T(8,128)(2,1)S(1)}) custom-call(bf16[8,128,256]{2,1,0:T(8,128)(2,1)} %mid_far.5, bf16[2,3,3,128,128]{4,3,2,1,0:T(8,128)(2,1)} %weight_far.3), custom_call_target="tpu_custom_call" | custom-call | flops 1200000000 | bytes 3358720 | tf_op jit(solution)/shard_map/conv_own/pallas_call | solution.py:44
  9.2 0.6 collective-permute-done.1.odd_down
  9.8 0.6 collective-permute-done.even_down
  10.4 2.2 %conv_finish.1 = (bf16[8,144,256]{2,1,0:T(8,128)(2,1)}, f32[8,128,256]{2,1,0:T(8,128)S(1)}) custom-call(bf16[8,128,256]{2,1,0:T(8,128)(2,1)} %mid_far.5, bf16[1,128,256]{2,1,0:T(8,128)(2,1)S(1)} %collective-permute-done.even_down, bf16[1,128,256]{2,1,0:T(8,128)(2,1)S(1)} %collective-permute-done.1.odd_down, f32[1024,256]{1,0:T(8,128)S(1)} %get-tuple-element.41.own, ...), custom_call_target="tpu_custom_call" | custom-call | flops 200000000 | bytes 4538368 | tf_op jit(solution)/shard_map/conv_finish/pallas_call | solution.py:44
  12.6 4.3 %all-to-all-start = ((bf16[8,144,256]{2,1,0:T(8,128)(2,1)}), bf16[8,144,256]{2,1,0:T(8,128)(2,1)S(1)}, u32[]{:S(2)}, u32[]{:S(2)}) async-start(bf16[8,144,256]{2,1,0:T(8,128)(2,1)} %get-tuple-element.44), calls=%async_computation | async-start | bytes 1179648 | tf_op jit(solution)/shard_map/all_to_all | solution.py:492
  16.9 3.0 %prepare.1 = (bf16[256,1280]{1,0:T(8,128)(2,1)}, bf16[1024,512]{1,0:T(8,128)(2,1)}, f32[8,128,256]{2,1,0:T(8,128)}) custom-call(f32[8,128,256]{2,1,0:T(8,128)S(1)} %get-tuple-element.45.conv, bf16[8,128,256]{2,1,0:T(8,128)(2,1)} %mid_far.5, bf16[1,128,256]{2,1,0:T(8,128)(2,1)S(1)} %collective-permute-done.even_down, ...), custom_call_target="tpu_custom_call" | custom-call | flops 300000000 | bytes 5242880 | tf_op jit(solution)/shard_map/prepare/pallas_call | solution.py:44
  19.9 8.0 %all-to-all-done.came = bf16[8,144,256]{2,1,0:T(8,128)(2,1)S(1)} async-done(((bf16[8,144,256]{2,1,0:T(8,128)(2,1)}), bf16[8,144,256]{2,1,0:T(8,128)(2,1)S(1)}, u32[]{:S(2)}, u32[]{:S(2)}) %all-to-all-start) | async-done | bytes 589856 | tf_op jit(solution)/shard_map/all_to_all | solution.py:492
  28.0 21.3 %attend.1 = (bf16[8,144,256]{2,1,0:T(8,128)(2,1)}, bf16[1024,256]{1,0:T(8,128)(2,1)}, bf16[1024,512]{1,0:T(8,128)(2,1)}, bf16[1024,1536]{1,0:T(8,128)(2,1)}) custom-call(bf16[8,144,256]{2,1,0:T(8,128)(2,1)S(1)} %all-to-all-done.came, bf16[256,1536]{1,0:T(8,128)(2,1)} %qkv_w_far.1, bf16[1024,512]{1,0:T(8,128)(2,1)} %get-tuple-element.46.grad_att_far, ...), custom_call_target="tpu_custom_call" | custom-call | flops 15000000512 | bytes 8257536 | tf_op jit(solution)/shard_map/attend/pallas_call | solution.py:44
  49.3 3.5 %all-to-all-start.1 = ((bf16[8,144,256]{2,1,0:T(8,128)(2,1)}), bf16[8,144,256]{2,1,0:T(8,128)(2,1)S(1)}, u32[]{:S(2)}, u32[]{:S(2)}) async-start(bf16[8,144,256]{2,1,0:T(8,128)(2,1)} %get-tuple-element.54), calls=%async_computation.1 | async-start | bytes 1179648 | tf_op jit(solution)/shard_map/all_to_all | solution.py:492
  52.8 7.1 %attend_rest.1 = (bf16[1024,256]{1,0:T(8,128)(2,1)}, bf16[16,128,128]{2,1,0:T(8,128)(2,1)S(1)}, bf16[16,128,128]{2,1,0:T(8,128)(2,1)}, f32[8,128,256]{2,1,0:T(8,128)S(1)}, bf16[256,1280]{1,0:T(8,128)(2,1)S(1)}) custom-call(bf16[1024,256]{1,0:T(8,128)(2,1)} %get-tuple-element.47.hidden_far, bf16[1024,512]{1,0:T(8,128)(2,1)} %get-tuple-element.48.attended_far, ...), custom_call_target="tpu_custom_call" | custom-call | flops 1500000000 | bytes 10485760 | tf_op jit(solution)/shard_map/attend_rest/pallas_call | solution.py:44
  60.0 3.8 %all-to-all-done.1.came = bf16[8,144,256]{2,1,0:T(8,128)(2,1)S(1)} async-done(((bf16[8,144,256]{2,1,0:T(8,128)(2,1)}), bf16[8,144,256]{2,1,0:T(8,128)(2,1)S(1)}, u32[]{:S(2)}, u32[]{:S(2)}) %all-to-all-start.1) | async-done | bytes 589856 | tf_op jit(solution)/shard_map/all_to_all | solution.py:492
  63.8 0.0 collective-permute-start.2
  63.8 3.4 %conv_weight_grad.1 = (bf16[2,1,144,256]{3,2,1,0:T(8,128)(2,1)S(1)}, bf16[16,80,128]{2,1,0:T(8,128)(2,1)S(1)}, bf16[16,80,128]{2,1,0:T(8,128)(2,1)S(1)}, bf16[16...) custom-call(bf16[8,144,256]{2,1,0:T(8,128)(2,1)S(1)} %all-to-all-done.1.came, ...), custom_call_target="tpu_custom_call" | custom-call | flops 1200000000 | bytes 6242304 | tf_op jit(solution)/shard_map/conv_weight_grad/pallas_call | solution.py:44
  67.2 0.6 collective-permute-start.3
  67.8 1.3 %collective-permute-done.3.got = bf16[16,80,128]{2,1,0:T(8,128)(2,1)S(1)} collective-permute-done((bf16[16,80,128]{2,1,0:T(8,128)(2,1)S(1)}, bf16[16,80,128]{2,1,0:T(8,128)(2,1)S(1)}, u32[]{:S(2)}, u32[]{:S(2)}) %collective-permute-start.3) | collective-permute-done | bytes 327712 | tf_op jit(solution)/shard_map/ppermute | solution.py:496
  69.1 0.0 collective-permute-done.2.early_got
  69.1 1.1 %join.1 = bf16[16,208,128]{2,1,0:T(8,128)(2,1)} custom-call(bf16[16,128,128]{2,1,0:T(8,128)(2,1)S(1)} %get-tuple-element.59.early, bf16[16,128,128]{2,1,0:T(8,128)(2,1)S(1)} %collective-permute-done.2.early_got, bf16[16,80,128]{2,1,0:T(8,128)(2,1)S(1)} %get-tuple-element.61.mine, bf16[16,80,128]{2,1,0:T(8,128)(2,1)S(1)} %collective-permute-done.3.got), custom_call_target="tpu_custom_call" | custom-call | bytes 2555904 | tf_op jit(solution)/shard_map/join/pallas_call | solution.py:44
  70.2 4.5 %all-to-all-start.2 = ((bf16[16,208,128]{2,1,0:T(8,128)(2,1)}), bf16[16,208,128]{2,1,0:T(8,128)(2,1)S(1)}, u32[]{:S(2)}, u32[]{:S(2)}) async-start(bf16[16,208,128]{2,1,0:T(8,128)(2,1)} %join.1), calls=%async_computation.2 | async-start | bytes 1703936 | tf_op jit(solution)/shard_map/all_to_all | solution.py:492
  74.7 4.6 %collective-permute-start.5 = (bf16[1,144,256]{2,1,0:T(8,128)(2,1)S(1)}, bf16[1,144,256]{2,1,0:T(8,128)(2,1)S(1)}, u32[]{:S(2)}, u32[]{:S(2)}) collective-permute-start(bf16[1,144,256]{2,1,0:T(8,128)(2,1)S(1)} %get-tuple-element.79), channel_id=1, source_target_pairs={{8,16},{16,8},{24,32},{32,24},{40,48},{48,40},{56,64},{64,56},{72,... | collective-permute-start | bytes 221192 | tf_op jit(solution)/shard_map/ppermute | solution.py:488
  79.3 0.8 collective-permute-start.4
  80.1 3.0 %conv_data.1 = (f32[1024,256]{1,0:T(8,128)S(1)}, bf16[3,256,768]{2,1,0:T(8,128)(2,1)S(1)}) custom-call(bf16[8,128,256]{2,1,0:T(8,128)(2,1)} %get-tuple-element.65.grad_far, bf16[8,128,768]{2,1,0:T(8,128)(2,1)} %get-tuple-element.66.stacked_far, bf16[2,3,3,128,128]{4,3,2,1,0:T(8,128)(2,1)} %weight_far.3), custom_call_target="tpu_custom_call" | custom-call | flops 1200000000 | bytes 4915200 | tf_op jit(solution)/shard_map/conv_data/pallas_call | solution.py:44
  83.1 1.8 %collective-permute-done.5.odd_down = bf16[1,144,256]{2,1,0:T(8,128)(2,1)S(1)} collective-permute-done((bf16[1,144,256]{2,1,0:T(8,128)(2,1)S(1)}, bf16[1,144,256]{2,1,0:T(8,128)(2,1)S(1)}, u32[]{:S(2)}, u32[]{:S(2)}) %collective-permute-start.5) | collective-permute-done | bytes 73760 | tf_op jit(solution)/shard_map/ppermute | solution.py:488
  84.9 3.5 %collective-permute-done.4.even_down = bf16[1,144,256]{2,1,0:T(8,128)(2,1)S(1)} collective-permute-done((bf16[1,144,256]{2,1,0:T(8,128)(2,1)S(1)}, bf16[1,144,256]{2,1,0:T(8,128)(2,1)S(1)}, u32[]{:S(2)}, u32[]{:S(2)}) %collective-permute-start.4) | collective-permute-done | bytes 73760 | tf_op jit(solution)/shard_map/ppermute | solution.py:488
  88.4 1.8 %all-to-all-done.2.came = bf16[16,208,128]{2,1,0:T(8,128)(2,1)S(1)} async-done(((bf16[16,208,128]{2,1,0:T(8,128)(2,1)}), bf16[16,208,128]{2,1,0:T(8,128)(2,1)S(1)}, u32[]{:S(2)}, u32[]{:S(2)}) %all-to-all-start.2) | async-done | bytes 852000 | tf_op jit(solution)/shard_map/all_to_all | solution.py:492
  90.3 0.8 regroup.1
  91.0 9.0 %all-to-all-start.3 = ((bf16[8,32,128]{2,1,0:T(8,128)(2,1)}), bf16[8,32,128]{2,1,0:T(8,128)(2,1)S(1)}, u32[]{:S(2)}, u32[]{:S(2)}) async-start(bf16[8,32,128]{2,1,0:T(8,128)(2,1)} %regroup.1), calls=%async_computation.3 | async-start | bytes 131072 | tf_op jit(solution)/shard_map/all_to_all | solution.py:492
  100.1 1.2 %conv_data_finish.1 = bf16[8,128,256]{2,1,0:T(8,128)(2,1)} custom-call(f32[1024,256]{1,0:T(8,128)S(1)} %get-tuple-element.69.total, bf16[1,144,256]{2,1,0:T(8,128)(2,1)S(1)} %collective-permute-done.4.even_down, bf16[1,144,256]{2,1,0:T(8,128)(2,1)S(1)} %collective-permute-done.5.odd_down, bf16[3,256,768]{2,1,0:T(8,128)(2,1)S(1)} %get-tuple-element.72.matrix), custom_call_target="tpu_custom_call" | custom-call | flops 100000000 | bytes 2899968 | tf_op jit(solution)/shard_map/conv_data_finish/pallas_call | solution.py:44
  101.2 5.7 %all-to-all-done.3.came = bf16[8,32,128]{2,1,0:T(8,128)(2,1)S(1)} async-done(((bf16[8,32,128]{2,1,0:T(8,128)(2,1)}), bf16[8,32,128]{2,1,0:T(8,128)(2,1)S(1)}, u32[]{:S(2)}, u32[]{:S(2)}) %all-to-all-start.3) | async-done | bytes 65568 | tf_op jit(solution)/shard_map/all_to_all | solution.py:492
  107.0 0.6 share.1
  (1 shorter events, 0.0 us)
Async XLA Ops:
  1.5 8.3 %collective-permute-start.1 = (bf16[1,128,256]{2,1,0:T(8,128)(2,1)S(1)}, bf16[1,128,256]{2,1,0:T(8,128)(2,1)S(1)}, u32[]{:S(2)}, u32[]{:S(2)}) collective-permute-start(bf16[1,128,256]{2,1,0:T(8,128)(2,1)S(1)} %get-tuple-element.77), channel_id=1, source_target_pairs={{8,16},{16,8},{24,32},{32,24},{40,48},{48,40},{56,64},{64,56},{72,... | collective-permute-start | bytes 196616 | tf_op jit(solution)/shard_map/ppermute | solution.py:488
  6.0 4.4 %collective-permute-start = (bf16[1,128,256]{2,1,0:T(8,128)(2,1)S(1)}, bf16[1,128,256]{2,1,0:T(8,128)(2,1)S(1)}, u32[]{:S(2)}, u32[]{:S(2)}) collective-permute-start(bf16[1,128,256]{2,1,0:T(8,128)(2,1)S(1)} %get-tuple-element.78), channel_id=1, source_target_pairs={{0,8},{8,0},{16,24},{24,16},{32,40},{40,32},{48,56},{56,48},{64,72... | collective-permute-start | bytes 196616 | tf_op jit(solution)/shard_map/ppermute | solution.py:488
  12.6 15.4 %all-to-all-start = ((bf16[8,144,256]{2,1,0:T(8,128)(2,1)}), bf16[8,144,256]{2,1,0:T(8,128)(2,1)S(1)}, u32[]{:S(2)}, u32[]{:S(2)}) async-start(bf16[8,144,256]{2,1,0:T(8,128)(2,1)} %get-tuple-element.44), calls=%async_computation | async-start | bytes 1179648 | tf_op jit(solution)/shard_map/all_to_all | solution.py:492
  49.3 14.5 %all-to-all-start.1 = ((bf16[8,144,256]{2,1,0:T(8,128)(2,1)}), bf16[8,144,256]{2,1,0:T(8,128)(2,1)S(1)}, u32[]{:S(2)}, u32[]{:S(2)}) async-start(bf16[8,144,256]{2,1,0:T(8,128)(2,1)} %get-tuple-element.54), calls=%async_computation.1 | async-start | bytes 1179648 | tf_op jit(solution)/shard_map/all_to_all | solution.py:492
  63.8 5.3 %collective-permute-start.2 = (bf16[16,128,128]{2,1,0:T(8,128)(2,1)S(1)}, bf16[16,128,128]{2,1,0:T(8,128)(2,1)S(1)}, u32[]{:S(2)}, u32[]{:S(2)}) collective-permute-start(bf16[16,128,128]{2,1,0:T(8,128)(2,1)S(1)} %get-tuple-element.60), channel_id=1, source_target_pairs={{0,1},{1,0},{2,3},{3,2},{4,5},{5,4},{6,7},{7,6},{8,9},{9,8},{10,11... | collective-permute-start | bytes 1572872 | tf_op jit(solution)/shard_map/ppermute | solution.py:496
  67.2 1.8 %collective-permute-start.3 = (bf16[16,80,128]{2,1,0:T(8,128)(2,1)S(1)}, bf16[16,80,128]{2,1,0:T(8,128)(2,1)S(1)}, u32[]{:S(2)}, u32[]{:S(2)}) collective-permute-start(bf16[16,80,128]{2,1,0:T(8,128)(2,1)S(1)} %get-tuple-element.63), channel_id=1, source_target_pairs={{0,1},{1,0},{2,3},{3,2},{4,5},{5,4},{6,7},{7,6},{8,9},{9,8},{10,11... | collective-permute-start | bytes 983048 | tf_op jit(solution)/shard_map/ppermute | solution.py:496
  70.2 20.1 %all-to-all-start.2 = ((bf16[16,208,128]{2,1,0:T(8,128)(2,1)}), bf16[16,208,128]{2,1,0:T(8,128)(2,1)S(1)}, u32[]{:S(2)}, u32[]{:S(2)}) async-start(bf16[16,208,128]{2,1,0:T(8,128)(2,1)} %join.1), calls=%async_computation.2 | async-start | bytes 1703936 | tf_op jit(solution)/shard_map/all_to_all | solution.py:492
  74.7 10.2 %collective-permute-start.5 = (bf16[1,144,256]{2,1,0:T(8,128)(2,1)S(1)}, bf16[1,144,256]{2,1,0:T(8,128)(2,1)S(1)}, u32[]{:S(2)}, u32[]{:S(2)}) collective-permute-start(bf16[1,144,256]{2,1,0:T(8,128)(2,1)S(1)} %get-tuple-element.79), channel_id=1, source_target_pairs={{8,16},{16,8},{24,32},{32,24},{40,48},{48,40},{56,64},{64,56},{72,... | collective-permute-start | bytes 221192 | tf_op jit(solution)/shard_map/ppermute | solution.py:488
  79.3 9.2 %collective-permute-start.4 = (bf16[1,144,256]{2,1,0:T(8,128)(2,1)S(1)}, bf16[1,144,256]{2,1,0:T(8,128)(2,1)S(1)}, u32[]{:S(2)}, u32[]{:S(2)}) collective-permute-start(bf16[1,144,256]{2,1,0:T(8,128)(2,1)S(1)} %get-tuple-element.80), channel_id=1, source_target_pairs={{0,8},{8,0},{16,24},{24,16},{32,40},{40,32},{48,56},{56,48},{64,72... | collective-permute-start | bytes 221192 | tf_op jit(solution)/shard_map/ppermute | solution.py:488
  91.0 15.9 %all-to-all-start.3 = ((bf16[8,32,128]{2,1,0:T(8,128)(2,1)}), bf16[8,32,128]{2,1,0:T(8,128)(2,1)S(1)}, u32[]{:S(2)}, u32[]{:S(2)}) async-start(bf16[8,32,128]{2,1,0:T(8,128)(2,1)} %regroup.1), calls=%async_computation.3 | async-start | bytes 131072 | tf_op jit(solution)/shard_map/all_to_all | solution.py:492

commit v7 on v6

--- a/solution.py
+++ b/solution.py
@@ -110,11 +110,22 @@
     down[...] = jnp.where(odd, second, first)
 
 
-def conv_own_body(mid_far, weight_far, conv, borders, matrix, mid, weight, stacked, semaphores):
+def begin_body(mid_far, weight_far, send_a, send_b, borders, matrix, stacked, mid, weight, semaphores):
     start = copier(semaphores)
-    load_weight, load_mid = start(weight_far, weight), start(mid_far, mid)
+    load_mid, load_weight = start(mid_far, mid), start(weight_far, weight)
     frames, bins, width = mid.shape
     half = width // 2
+    load_mid.wait()
+    odd = lax.rem(lax.axis_index("y"), 2) == 1
+    first, last = mid[0:1], mid[frames - 1 : frames]
+    send_a[...] = jnp.where(odd, first, last)
+    send_b[...] = jnp.where(odd, last, first)
+    wide = mid[...].astype(F32)
+    stacked[:, :, :width] = bins_before(wide, 0.0).astype(BF)
+    stacked[:, :, width : 2 * width] = mid[...]
+    stacked[:, :, 2 * width :] = bins_after(wide, 0.0).astype(BF)
+    borders[0] = mid[:, 0, :].astype(F32)
+    borders[1] = mid[:, bins - 1, :].astype(F32)
     load_weight.wait()
     for i in range(3):
         for j in range(3):
@@ -124,18 +135,15 @@
             matrix[i, at : at + half, half:] = imag
             matrix[i, at + half : at + width, :half] = -imag
             matrix[i, at + half : at + width, half:] = real
-    load_mid.wait()
-    wide = mid[...].astype(F32)
-    stacked[:, :, :width] = bins_before(wide, 0.0).astype(BF)
-    stacked[:, :, width : 2 * width] = mid[...]
-    stacked[:, :, 2 * width :] = bins_after(wide, 0.0).astype(BF)
+
+
+def conv_own_body(stacked, matrix, conv):
+    frames, bins, triple = stacked.shape
     inner = (frames - 1) * bins
-    everything = stacked[...].reshape(frames * bins, 3 * width)
+    everything = stacked[...].reshape(frames * bins, triple)
     conv[...] = mm(everything, matrix[1])
     conv[bins:] += mm(everything[:inner], matrix[0])
     conv[:inner] += mm(everything[bins:], matrix[2])
-    borders[0] = mid[:, 0, :].astype(F32)
-    borders[1] = mid[:, bins - 1, :].astype(F32)
 
 
 def conv_finish_body(
@@ -296,7 +304,11 @@
 
     for h in range(HEADS):
         one_head(h, HEADS, qkv, grad_att, attended, grad_cells, sum_keys, sum_values)
-    stores += [start(grad_cells, grad_cells_far), start(attended, attended_far)]
+        part = columns(0, h)
+        stores.append(start(attended.at[:, part], attended_far.at[:, part]))
+        for n in range(3):
+            part = columns(n, h)
+            stores.append(start(grad_cells.at[:, part], grad_cells_far.at[:, part]))
     load_cotangent.wait()
     inv_rms, normed_f, _ = normed_parts(hidden[...].astype(F32))
     grad_normed = mm(grad_cells[...], qkv_w[...], NT)
@@ -503,23 +515,25 @@
     long = bins + EXTRA
     vmem = pltpu.VMEM
     cotangent = cotangent.reshape(cells, width)
-    odd = lax.rem(lax.axis_index("y"), 2) == 1
-    first, last = spectrum[:1], spectrum[frames - 1 :]
-    halo_a, halo_b = pair_exchanges(jnp.where(odd, first, last), jnp.where(odd, last, first))
     tile = vmem((frames, bins, width), BF)
     tile_f = vmem((frames, bins, width), F32)
     pieces = vmem((frames, EXTRA, width), F32)
     square = vmem((cells, width), BF)
     kernels = vmem(conv_weight.shape, BF)
     halo = vmem((1, bins, width), BF)
-    own, borders, matrix = kernel_call(
-        conv_own_body, "conv_own",
+    send_a, send_b, borders, matrix, stacked = kernel_call(
+        begin_body, "begin",
         [
-            ((cells, width), F32, "any"), ((2, frames, width), F32, "any"),
-            ((3, 3 * width, width), BF, "any"),
+            ((1, bins, width), BF, "any"), ((1, bins, width), BF, "any"),
+            ((2, frames, width), F32, "any"), ((3, 3 * width, width), BF, "vmem"),
+            ((frames, bins, 3 * width), BF, "vmem"),
         ],
         spectrum, conv_weight, far=(0, 1),
-        scratch=[tile, kernels, vmem((frames, bins, 3 * width), BF)], copies=2, mflops=1200,
+        scratch=[tile, kernels], copies=2,
+    )
+    halo_a, halo_b = pair_exchanges(send_a, send_b)
+    (own,) = kernel_call(
+        conv_own_body, "conv_own", [((cells, width), F32, "any")], stacked, matrix, mflops=1200
     )
     payload, conv = kernel_call(
         conv_finish_body, "conv_finish",
@@ -554,7 +568,7 @@
             vmem((width, 3 * wide), BF), attended_v, square, square, cells_v, attended_v, cells_v,
             vmem((HEAD, cells), F32), vmem((HEAD, cells), F32), pieces,
         ],
-        copies=6, mflops=15000,
+        copies=4 + 4 * HEADS, mflops=15000,
     )
     grads = exchange(back, ("x", "core"))
     ring = lax.axis_size("y") * lax.axis_size("x")

time: 109 us -> 111 us (1.018)
  waiting for transfers between devices: 27.1 us -> 29.3 us
    ppermute x2, waiting for transfers between devices: 2.37 us -> 5.13 us  [pair_exchanges(): lax.ppermute(second, ('z', 'y'), apart)]
    pallas_call x11 -> x12, Pallas kernels: 46.4 us -> 47 us  [kernel_call(): pl.pallas_call(body, out_shape=shapes, in_specs=[hbm if n in far else nea...]
  transfers between devices with their start and end apart: 10 -> 10, of which waited for: 9 -> 8; matrix products, arithmetic and copies ran while one was open for 0% -> 0% of each run, Pallas kernels for 19% -> 17%
where the time goes in v7:
time: 111 us; the launch traced here: 110 us
  Pallas kernels  47 us (42%)
  starting transfers between devices  33.1 us (30%)
  waiting for transfers between devices  29.3 us (26%)
    pallas_call x12, Pallas kernels, kernel_call(): pl.pallas_call(body, out_shape=shapes, in_specs=[hbm if n in far else nea...  47 us
    all_to_all x4, starting transfers between devices, exchange(): return lax.all_to_all(array, axis, split_axis=0, concat_axis=0, tiled=True)  21.9 us
    all_to_all x4, waiting for transfers between devices, exchange(): return lax.all_to_all(array, axis, split_axis=0, concat_axis=0, tiled=True)  19.4 us
    ppermute x2, starting transfers between devices, pair_exchanges(): lax.ppermute(second, ('z', 'y'), apart)  8.2 us
    ppermute x2, waiting for transfers between devices, pair_exchanges(): lax.ppermute(second, ('z', 'y'), apart)  5.13 us
    ppermute x2, waiting for transfers between devices, pair_exchanges(): lax.ppermute(first, ('z', 'y'), near)  3.51 us
    ppermute x2, starting transfers between devices, pair_exchanges(): lax.ppermute(first, ('z', 'y'), near)  2.47 us
  transfers between devices with their start and end apart: 10, of which 8 were waited for; matrix products, arithmetic and copies ran while one was open for 0% of the time, Pallas kernels for 17%

profile of v7, /device:TPU:32, one launch (start us, length us, event | category | flops | bytes accessed | tf_op | source)
XLA Modules:
  0.0 110.2 jit_solution(12576210727092915412)
XLA Ops:
  0.6 1.5 %begin.1 = (bf16[1,128,256]{2,1,0:T(8,128)(2,1)S(1)}, bf16[1,128,256]{2,1,0:T(8,128)(2,1)S(1)}, f32[2,8,256]{2,1,0:T(8,128)S(1)}, bf16[3,768,256]{2,1,0:T(8,128)(2,1)S(1)}, bf16[8,128,768]{2,1,0:T(8,128)(2,1)S(1)}) custom-call(bf16[8,128,256]{2,1,0:T(8,128)(2,1)} %mid_far.5, bf16[2,3,3,128,128]{4,3,2,1,0:T(8,128)(2,1)} %weight_far.3), custom_call_target="tpu_custom_call" | custom-call | bytes 4014080 | tf_op jit(solution)/shard_map/begin/pallas_call | solution.py:44
  2.1 1.7 %collective-permute-start = (bf16[1,128,256]{2,1,0:T(8,128)(2,1)S(1)}, bf16[1,128,256]{2,1,0:T(8,128)(2,1)S(1)}, u32[]{:S(2)}, u32[]{:S(2)}) collective-permute-start(bf16[1,128,256]{2,1,0:T(8,128)(2,1)S(1)} %get-tuple-element.43), channel_id=1, source_target_pairs={{0,8},{8,0},{16,24},{24,16},{32,40},{40,32},{48,56},{56,48},{64,72... | collective-permute-start | bytes 196616 | tf_op jit(solution)/shard_map/ppermute | solution.py:500
  3.8 3.6 %collective-permute-start.1 = (bf16[1,128,256]{2,1,0:T(8,128)(2,1)S(1)}, bf16[1,128,256]{2,1,0:T(8,128)(2,1)S(1)}, u32[]{:S(2)}, u32[]{:S(2)}) collective-permute-start(bf16[1,128,256]{2,1,0:T(8,128)(2,1)S(1)} %get-tuple-element.44), channel_id=1, source_target_pairs={{8,16},{16,8},{24,32},{32,24},{40,48},{48,40},{56,64},{64,56},{72,... | collective-permute-start | bytes 196616 | tf_op jit(solution)/shard_map/ppermute | solution.py:500
  7.4 1.3 %conv_own.1.own = f32[1024,256]{1,0:T(8,128)S(1)} custom-call(bf16[8,128,768]{2,1,0:T(8,128)(2,1)S(1)} %get-tuple-element.45.stacked, bf16[3,768,256]{2,1,0:T(8,128)(2,1)S(1)} %get-tuple-element.46.matrix), custom_call_target="tpu_custom_call" | custom-call | flops 1200000000 | bytes 3801088 | tf_op jit(solution)/shard_map/conv_own/pallas_call | solution.py:44
  8.7 0.0 collective-permute-done.even_down
  8.7 3.3 %collective-permute-done.1.odd_down = bf16[1,128,256]{2,1,0:T(8,128)(2,1)S(1)} collective-permute-done((bf16[1,128,256]{2,1,0:T(8,128)(2,1)S(1)}, bf16[1,128,256]{2,1,0:T(8,128)(2,1)S(1)}, u32[]{:S(2)}, u32[]{:S(2)}) %collective-permute-start.1) | collective-permute-done | bytes 65568 | tf_op jit(solution)/shard_map/ppermute | solution.py:500
  12.1 2.2 %conv_finish.1 = (bf16[8,144,256]{2,1,0:T(8,128)(2,1)}, f32[8,128,256]{2,1,0:T(8,128)S(1)}) custom-call(bf16[8,128,256]{2,1,0:T(8,128)(2,1)} %mid_far.5, bf16[1,128,256]{2,1,0:T(8,128)(2,1)S(1)} %collective-permute-done.even_down, bf16[1,128,256]{2,1,0:T(8,128)(2,1)S(1)} %collective-permute-done.1.odd_down, f32[1024,256]{1,0:T(8,128)S(1)} %conv_own.1.own, ...), custom_call_target="tpu_custom_call" | custom-call | flops 200000000 | bytes 4538368 | tf_op jit(solution)/shard_map/conv_finish/pallas_call | solution.py:44
  14.3 4.3 %all-to-all-start = ((bf16[8,144,256]{2,1,0:T(8,128)(2,1)}), bf16[8,144,256]{2,1,0:T(8,128)(2,1)S(1)}, u32[]{:S(2)}, u32[]{:S(2)}) async-start(bf16[8,144,256]{2,1,0:T(8,128)(2,1)} %get-tuple-element.48), calls=%async_computation | async-start | bytes 1179648 | tf_op jit(solution)/shard_map/all_to_all | solution.py:504
  18.6 3.0 %prepare.1 = (bf16[256,1280]{1,0:T(8,128)(2,1)}, bf16[1024,512]{1,0:T(8,128)(2,1)}, f32[8,128,256]{2,1,0:T(8,128)}) custom-call(f32[8,128,256]{2,1,0:T(8,128)S(1)} %get-tuple-element.49.conv, bf16[8,128,256]{2,1,0:T(8,128)(2,1)} %mid_far.5, bf16[1,128,256]{2,1,0:T(8,128)(2,1)S(1)} %collective-permute-done.even_down, ...), custom_call_target="tpu_custom_call" | custom-call | flops 300000000 | bytes 5242880 | tf_op jit(solution)/shard_map/prepare/pallas_call | solution.py:44
  21.6 8.0 %all-to-all-done.came = bf16[8,144,256]{2,1,0:T(8,128)(2,1)S(1)} async-done(((bf16[8,144,256]{2,1,0:T(8,128)(2,1)}), bf16[8,144,256]{2,1,0:T(8,128)(2,1)S(1)}, u32[]{:S(2)}, u32[]{:S(2)}) %all-to-all-start) | async-done | bytes 589856 | tf_op jit(solution)/shard_map/all_to_all | solution.py:504
  29.7 21.7 %attend.1 = (bf16[8,144,256]{2,1,0:T(8,128)(2,1)}, bf16[1024,256]{1,0:T(8,128)(2,1)}, bf16[1024,512]{1,0:T(8,128)(2,1)}, bf16[1024,1536]{1,0:T(8,128)(2,1)}) custom-call(bf16[8,144,256]{2,1,0:T(8,128)(2,1)S(1)} %all-to-all-done.came, bf16[256,1536]{1,0:T(8,128)(2,1)} %qkv_w_far.1, bf16[1024,512]{1,0:T(8,128)(2,1)} %get-tuple-element.50.grad_att_far, ...), custom_call_target="tpu_custom_call" | custom-call | flops 15000000512 | bytes 8257536 | tf_op jit(solution)/shard_map/attend/pallas_call | solution.py:44
  51.4 3.5 %all-to-all-start.1 = ((bf16[8,144,256]{2,1,0:T(8,128)(2,1)}), bf16[8,144,256]{2,1,0:T(8,128)(2,1)S(1)}, u32[]{:S(2)}, u32[]{:S(2)}) async-start(bf16[8,144,256]{2,1,0:T(8,128)(2,1)} %get-tuple-element.58), calls=%async_computation.1 | async-start | bytes 1179648 | tf_op jit(solution)/shard_map/all_to_all | solution.py:504
  54.9 7.1 %attend_rest.1 = (bf16[1024,256]{1,0:T(8,128)(2,1)}, bf16[16,128,128]{2,1,0:T(8,128)(2,1)S(1)}, bf16[16,128,128]{2,1,0:T(8,128)(2,1)}, f32[8,128,256]{2,1,0:T(8,128)S(1)}, bf16[256,1280]{1,0:T(8,128)(2,1)S(1)}) custom-call(bf16[1024,256]{1,0:T(8,128)(2,1)} %get-tuple-element.51.hidden_far, bf16[1024,512]{1,0:T(8,128)(2,1)} %get-tuple-element.52.attended_far, ...), custom_call_target="tpu_custom_call" | custom-call | flops 1500000000 | bytes 10485760 | tf_op jit(solution)/shard_map/attend_rest/pallas_call | solution.py:44
  62.1 3.8 %all-to-all-done.1.came = bf16[8,144,256]{2,1,0:T(8,128)(2,1)S(1)} async-done(((bf16[8,144,256]{2,1,0:T(8,128)(2,1)}), bf16[8,144,256]{2,1,0:T(8,128)(2,1)S(1)}, u32[]{:S(2)}, u32[]{:S(2)}) %all-to-all-start.1) | async-done | bytes 589856 | tf_op jit(solution)/shard_map/all_to_all | solution.py:504
  65.9 0.0 collective-permute-start.2
  65.9 3.4 %conv_weight_grad.1 = (bf16[2,1,144,256]{3,2,1,0:T(8,128)(2,1)S(1)}, bf16[16,80,128]{2,1,0:T(8,128)(2,1)S(1)}, bf16[16,80,128]{2,1,0:T(8,128)(2,1)S(1)}, bf16[16...) custom-call(bf16[8,144,256]{2,1,0:T(8,128)(2,1)S(1)} %all-to-all-done.1.came, ...), custom_call_target="tpu_custom_call" | custom-call | flops 1200000000 | bytes 6242304 | tf_op jit(solution)/shard_map/conv_weight_grad/pallas_call | solution.py:44
  69.3 0.6 collective-permute-start.3
  69.9 1.3 %collective-permute-done.3.got = bf16[16,80,128]{2,1,0:T(8,128)(2,1)S(1)} collective-permute-done((bf16[16,80,128]{2,1,0:T(8,128)(2,1)S(1)}, bf16[16,80,128]{2,1,0:T(8,128)(2,1)S(1)}, u32[]{:S(2)}, u32[]{:S(2)}) %collective-permute-start.3) | collective-permute-done | bytes 327712 | tf_op jit(solution)/shard_map/ppermute | solution.py:508
  71.2 0.0 collective-permute-done.2.early_got
  71.2 1.1 join.1
  72.3 4.2 %all-to-all-start.2 = ((bf16[16,208,128]{2,1,0:T(8,128)(2,1)}), bf16[16,208,128]{2,1,0:T(8,128)(2,1)S(1)}, u32[]{:S(2)}, u32[]{:S(2)}) async-start(bf16[16,208,128]{2,1,0:T(8,128)(2,1)} %join.1), calls=%async_computation.2 | async-start | bytes 1703936 | tf_op jit(solution)/shard_map/all_to_all | solution.py:504
  76.5 4.6 %collective-permute-start.5 = (bf16[1,144,256]{2,1,0:T(8,128)(2,1)S(1)}, bf16[1,144,256]{2,1,0:T(8,128)(2,1)S(1)}, u32[]{:S(2)}, u32[]{:S(2)}) collective-permute-start(bf16[1,144,256]{2,1,0:T(8,128)(2,1)S(1)} %get-tuple-element.81), channel_id=1, source_target_pairs={{8,16},{16,8},{24,32},{32,24},{40,48},{48,40},{56,64},{64,56},{72,... | collective-permute-start | bytes 221192 | tf_op jit(solution)/shard_map/ppermute | solution.py:500
  81.1 0.8 collective-permute-start.4
  81.9 3.0 %conv_data.1 = (f32[1024,256]{1,0:T(8,128)S(1)}, bf16[3,256,768]{2,1,0:T(8,128)(2,1)S(1)}) custom-call(bf16[8,128,256]{2,1,0:T(8,128)(2,1)} %get-tuple-element.69.grad_far, bf16[8,128,768]{2,1,0:T(8,128)(2,1)} %get-tuple-element.70.stacked_far, bf16[2,3,3,128,128]{4,3,2,1,0:T(8,128)(2,1)} %weight_far.3), custom_call_target="tpu_custom_call" | custom-call | flops 1200000000 | bytes 4915200 | tf_op jit(solution)/shard_map/conv_data/pallas_call | solution.py:44
  84.9 1.8 %collective-permute-done.5.odd_down = bf16[1,144,256]{2,1,0:T(8,128)(2,1)S(1)} collective-permute-done((bf16[1,144,256]{2,1,0:T(8,128)(2,1)S(1)}, bf16[1,144,256]{2,1,0:T(8,128)(2,1)S(1)}, u32[]{:S(2)}, u32[]{:S(2)}) %collective-permute-start.5) | collective-permute-done | bytes 73760 | tf_op jit(solution)/shard_map/ppermute | solution.py:500
  86.7 3.5 %collective-permute-done.4.even_down = bf16[1,144,256]{2,1,0:T(8,128)(2,1)S(1)} collective-permute-done((bf16[1,144,256]{2,1,0:T(8,128)(2,1)S(1)}, bf16[1,144,256]{2,1,0:T(8,128)(2,1)S(1)}, u32[]{:S(2)}, u32[]{:S(2)}) %collective-permute-start.4) | collective-permute-done | bytes 73760 | tf_op jit(solution)/shard_map/ppermute | solution.py:500
  90.2 1.9 %all-to-all-done.2.came = bf16[16,208,128]{2,1,0:T(8,128)(2,1)S(1)} async-done(((bf16[16,208,128]{2,1,0:T(8,128)(2,1)}), bf16[16,208,128]{2,1,0:T(8,128)(2,1)S(1)}, u32[]{:S(2)}, u32[]{:S(2)}) %all-to-all-start.2) | async-done | bytes 852000 | tf_op jit(solution)/shard_map/all_to_all | solution.py:504
  92.1 0.8 regroup.1
  92.8 9.8 %all-to-all-start.3 = ((bf16[8,32,128]{2,1,0:T(8,128)(2,1)}), bf16[8,32,128]{2,1,0:T(8,128)(2,1)S(1)}, u32[]{:S(2)}, u32[]{:S(2)}) async-start(bf16[8,32,128]{2,1,0:T(8,128)(2,1)} %regroup.1), calls=%async_computation.3 | async-start | bytes 131072 | tf_op jit(solution)/shard_map/all_to_all | solution.py:504
  102.7 1.2 %conv_data_finish.1 = bf16[8,128,256]{2,1,0:T(8,128)(2,1)} custom-call(f32[1024,256]{1,0:T(8,128)S(1)} %get-tuple-element.73.total, bf16[1,144,256]{2,1,0:T(8,128)(2,1)S(1)} %collective-permute-done.4.even_down, bf16[1,144,256]{2,1,0:T(8,128)(2,1)S(1)} %collective-permute-done.5.odd_down, bf16[3,256,768]{2,1,0:T(8,128)(2,1)S(1)} %get-tuple-element.76.matrix), custom_call_target="tpu_custom_call" | custom-call | flops 100000000 | bytes 2899968 | tf_op jit(solution)/shard_map/conv_data_finish/pallas_call | solution.py:44
  103.9 5.7 %all-to-all-done.3.came = bf16[8,32,128]{2,1,0:T(8,128)(2,1)S(1)} async-done(((bf16[8,32,128]{2,1,0:T(8,128)(2,1)}), bf16[8,32,128]{2,1,0:T(8,128)(2,1)S(1)}, u32[]{:S(2)}, u32[]{:S(2)}) %all-to-all-start.3) | async-done | bytes 65568 | tf_op jit(solution)/shard_map/all_to_all | solution.py:504
  109.6 0.6 share.1
  (1 shorter events, 0.0 us)
Async XLA Ops:
  2.1 6.6 %collective-permute-start = (bf16[1,128,256]{2,1,0:T(8,128)(2,1)S(1)}, bf16[1,128,256]{2,1,0:T(8,128)(2,1)S(1)}, u32[]{:S(2)}, u32[]{:S(2)}) collective-permute-start(bf16[1,128,256]{2,1,0:T(8,128)(2,1)S(1)} %get-tuple-element.43), channel_id=1, source_target_pairs={{0,8},{8,0},{16,24},{24,16},{32,40},{40,32},{48,56},{56,48},{64,72... | collective-permute-start | bytes 196616 | tf_op jit(solution)/shard_map/ppermute | solution.py:500
  3.8 8.3 %collective-permute-start.1 = (bf16[1,128,256]{2,1,0:T(8,128)(2,1)S(1)}, bf16[1,128,256]{2,1,0:T(8,128)(2,1)S(1)}, u32[]{:S(2)}, u32[]{:S(2)}) collective-permute-start(bf16[1,128,256]{2,1,0:T(8,128)(2,1)S(1)} %get-tuple-element.44), channel_id=1, source_target_pairs={{8,16},{16,8},{24,32},{32,24},{40,48},{48,40},{56,64},{64,56},{72,... | collective-permute-start | bytes 196616 | tf_op jit(solution)/shard_map/ppermute | solution.py:500
  14.3 15.4 %all-to-all-start = ((bf16[8,144,256]{2,1,0:T(8,128)(2,1)}), bf16[8,144,256]{2,1,0:T(8,128)(2,1)S(1)}, u32[]{:S(2)}, u32[]{:S(2)}) async-start(bf16[8,144,256]{2,1,0:T(8,128)(2,1)} %get-tuple-element.48), calls=%async_computation | async-start | bytes 1179648 | tf_op jit(solution)/shard_map/all_to_all | solution.py:504
  51.4 14.5 %all-to-all-start.1 = ((bf16[8,144,256]{2,1,0:T(8,128)(2,1)}), bf16[8,144,256]{2,1,0:T(8,128)(2,1)S(1)}, u32[]{:S(2)}, u32[]{:S(2)}) async-start(bf16[8,144,256]{2,1,0:T(8,128)(2,1)} %get-tuple-element.58), calls=%async_computation.1 | async-start | bytes 1179648 | tf_op jit(solution)/shard_map/all_to_all | solution.py:504
  65.9 5.3 %collective-permute-start.2 = (bf16[16,128,128]{2,1,0:T(8,128)(2,1)S(1)}, bf16[16,128,128]{2,1,0:T(8,128)(2,1)S(1)}, u32[]{:S(2)}, u32[]{:S(2)}) collective-permute-start(bf16[16,128,128]{2,1,0:T(8,128)(2,1)S(1)} %get-tuple-element.64), channel_id=1, source_target_pairs={{0,1},{1,0},{2,3},{3,2},{4,5},{5,4},{6,7},{7,6},{8,9},{9,8},{10,11... | collective-permute-start | bytes 1572872 | tf_op jit(solution)/shard_map/ppermute | solution.py:508
  69.3 1.9 %collective-permute-start.3 = (bf16[16,80,128]{2,1,0:T(8,128)(2,1)S(1)}, bf16[16,80,128]{2,1,0:T(8,128)(2,1)S(1)}, u32[]{:S(2)}, u32[]{:S(2)}) collective-permute-start(bf16[16,80,128]{2,1,0:T(8,128)(2,1)S(1)} %get-tuple-element.67), channel_id=1, source_target_pairs={{0,1},{1,0},{2,3},{3,2},{4,5},{5,4},{6,7},{7,6},{8,9},{9,8},{10,11... | collective-permute-start | bytes 983048 | tf_op jit(solution)/shard_map/ppermute | solution.py:508
  72.3 19.8 %all-to-all-start.2 = ((bf16[16,208,128]{2,1,0:T(8,128)(2,1)}), bf16[16,208,128]{2,1,0:T(8,128)(2,1)S(1)}, u32[]{:S(2)}, u32[]{:S(2)}) async-start(bf16[16,208,128]{2,1,0:T(8,128)(2,1)} %join.1), calls=%async_computation.2 | async-start | bytes 1703936 | tf_op jit(solution)/shard_map/all_to_all | solution.py:504
  76.5 10.2 %collective-permute-start.5 = (bf16[1,144,256]{2,1,0:T(8,128)(2,1)S(1)}, bf16[1,144,256]{2,1,0:T(8,128)(2,1)S(1)}, u32[]{:S(2)}, u32[]{:S(2)}) collective-permute-start(bf16[1,144,256]{2,1,0:T(8,128)(2,1)S(1)} %get-tuple-element.81), channel_id=1, source_target_pairs={{8,16},{16,8},{24,32},{32,24},{40,48},{48,40},{56,64},{64,56},{72,... | collective-permute-start | bytes 221192 | tf_op jit(solution)/shard_map/ppermute | solution.py:500
  81.1 9.2 %collective-permute-start.4 = (bf16[1,144,256]{2,1,0:T(8,128)(2,1)S(1)}, bf16[1,144,256]{2,1,0:T(8,128)(2,1)S(1)}, u32[]{:S(2)}, u32[]{:S(2)}) collective-permute-start(bf16[1,144,256]{2,1,0:T(8,128)(2,1)S(1)} %get-tuple-element.82), channel_id=1, source_target_pairs={{0,8},{8,0},{16,24},{24,16},{32,40},{40,32},{48,56},{56,48},{64,72... | collective-permute-start | bytes 221192 | tf_op jit(solution)/shard_map/ppermute | solution.py:500
  92.8 16.8 %all-to-all-start.3 = ((bf16[8,32,128]{2,1,0:T(8,128)(2,1)}), bf16[8,32,128]{2,1,0:T(8,128)(2,1)S(1)}, u32[]{:S(2)}, u32[]{:S(2)}) async-start(bf16[8,32,128]{2,1,0:T(8,128)(2,1)} %regroup.1), calls=%async_computation.3 | async-start | bytes 131072 | tf_op jit(solution)/shard_map/all_to_all | solution.py:504

commit v8 on v5

--- a/solution.py
+++ b/solution.py
@@ -595,6 +595,7 @@
         copies=3, mflops=1200, limit=40,
     )
     late_got = swap_cores(theirs)
+    edges, late_got = lax.optimization_barrier((edges, late_got))
     (message,) = kernel_call(
         join_body, "join", [((ring, 8 * GROUPS, 128), BF, "any")], early, got, late_mine,
         late_got,
@@ -602,22 +603,21 @@
     late = exchange(message, ("y", "x"))
     total, matrix_back = kernel_call(
         conv_data_body, "conv_data",
-        [((cells, width), F32, "vmem"), ((3, width, 3 * width), BF, "vmem")],
+        [((cells, width), F32, "any"), ((3, width, 3 * width), BF, "any")],
         grad_tile, stacked, conv_weight, far=(0, 1, 2),
         scratch=[tile, vmem(stacked_shape, BF), kernels], copies=3, mflops=1200,
     )
-    late, total = lax.optimization_barrier((late, total))
-    (chunk,) = kernel_call(
-        regroup_body, "regroup", [((lax.axis_size("z"), 32, 128), BF, "any")],
-        late,
-        scratch=[vmem(late.shape[1:], F32), vmem((lax.axis_size("z"), 32, 128), F32)],
-    )
-    chunk, edges = lax.optimization_barrier((chunk, edges))
     edge_a, edge_b = pair_exchanges(edges[0], edges[1])
     (grad_spectrum,) = kernel_call(
         conv_data_finish_body, "conv_data_finish", [((frames, bins, width), BF, "any")],
         total, edge_a, edge_b, matrix_back,
         scratch=[vmem((1, long, width), BF), vmem((1, long, width), BF)], mflops=100,
+    )
+    late, grad_spectrum = lax.optimization_barrier((late, grad_spectrum))
+    (chunk,) = kernel_call(
+        regroup_body, "regroup", [((lax.axis_size("z"), 32, 128), BF, "any")],
+        late,
+        scratch=[vmem(late.shape[1:], F32), vmem((lax.axis_size("z"), 32, 128), F32)],
     )
     shares = kernel_call(
         share_body, "share", [((9, 128), F32, "any"), ((12, 128), F32, "any"), ((4, 128), F32, "any")],

time: 111 us -> 108 us (0.973)
  blocking collectives: 0 us -> 15.7 us
  waiting for transfers between devices: 32.2 us -> 20 us
  starting transfers between devices: 29.8 us -> 23.6 us
    all_to_all x0 -> x1, blocking collectives: none -> 15.7 us  [exchange(): return lax.all_to_all(array, axis, split_axis=0, concat_axis=0, tiled=True)]
    all_to_all x4 -> x3, waiting for transfers between devices: 24.2 us -> 12.3 us  [exchange(): return lax.all_to_all(array, axis, split_axis=0, concat_axis=0, tiled=True)]
    all_to_all x4 -> x3, starting transfers between devices: 21.3 us -> 12.5 us  [exchange(): return lax.all_to_all(array, axis, split_axis=0, concat_axis=0, tiled=True)]
    ppermute x2, waiting for transfers between devices: 6.16 us -> 2.37 us  [pair_exchanges(): lax.ppermute(second, ('z', 'y'), apart)]
    ppermute x2, waiting for transfers between devices: 0.56 us -> 4.07 us  [pair_exchanges(): lax.ppermute(first, ('z', 'y'), near)]
    ppermute x2, starting transfers between devices: 6.65 us -> 9.06 us  [pair_exchanges(): lax.ppermute(second, ('z', 'y'), apart)]
  transfers between devices with their start and end apart: 10 -> 9, of which waited for: 7 -> 8; matrix products, arithmetic and copies ran while one was open for 0% -> 0% of each run, Pallas kernels for 19% -> 19%
where the time goes in v8:
time: 108 us; the launch traced here: 107 us
  Pallas kernels  45.6 us (42%)
  starting transfers between devices  23.6 us (22%)
  waiting for transfers between devices  20 us (19%)
  blocking collectives  15.7 us (15%)
    pallas_call x11, Pallas kernels, kernel_call(): pl.pallas_call(body, out_shape=shapes, in_specs=[hbm if n in far else nea...  45.6 us
    all_to_all x1, blocking collectives, exchange(): return lax.all_to_all(array, axis, split_axis=0, concat_axis=0, tiled=True)  15.7 us
    all_to_all x3, starting transfers between devices, exchange(): return lax.all_to_all(array, axis, split_axis=0, concat_axis=0, tiled=True)  12.5 us
    all_to_all x3, waiting for transfers between devices, exchange(): return lax.all_to_all(array, axis, split_axis=0, concat_axis=0, tiled=True)  12.3 us
    ppermute x2, starting transfers between devices, pair_exchanges(): lax.ppermute(second, ('z', 'y'), apart)  9.06 us
    ppermute x2, waiting for transfers between devices, pair_exchanges(): lax.ppermute(first, ('z', 'y'), near)  4.07 us
    ppermute x2, waiting for transfers between devices, pair_exchanges(): lax.ppermute(second, ('z', 'y'), apart)  2.37 us
  transfers between devices with their start and end apart: 9, of which 8 were waited for; matrix products, arithmetic and copies ran while one was open for 0% of the time, Pallas kernels for 19%

profile of v8, /device:TPU:32, one launch (start us, length us, event | category | flops | bytes accessed | tf_op | source)
XLA Modules:
  0.0 106.6 jit_solution(780767848769390724)
XLA Ops:
  0.6 0.9 broadcast_select_fusion
  1.5 4.5 %collective-permute-start.1 = (bf16[1,128,256]{2,1,0:T(8,128)(2,1)S(1)}, bf16[1,128,256]{2,1,0:T(8,128)(2,1)S(1)}, u32[]{:S(2)}, u32[]{:S(2)}) collective-permute-start(bf16[1,128,256]{2,1,0:T(8,128)(2,1)S(1)} %get-tuple-element.73), channel_id=1, source_target_pairs={{8,16},{16,8},{24,32},{32,24},{40,48},{48,40},{56,64},{64,56},{72,... | collective-permute-start | bytes 196616 | tf_op jit(solution)/shard_map/ppermute | solution.py:491
  6.0 0.7 collective-permute-start
  6.7 2.5 %conv_own.1 = (f32[1024,256]{1,0:T(8,128)S(1)}, f32[2,8,256]{2,1,0:T(8,128)S(1)}, bf16[3,768,256]{2,1,0:T(8,128)(2,1)S(1)}) custom-call(bf16[8,128,256]{2,1,0:T(8,128)(2,1)} %mid_far.5, bf16[2,3,3,128,128]{4,3,2,1,0:T(8,128)(2,1)} %weight_far.3), custom_call_target="tpu_custom_call" | custom-call | flops 1200000000 | bytes 3358720 | tf_op jit(solution)/shard_map/conv_own/pallas_call | solution.py:44
  9.2 0.6 collective-permute-done.1.odd_down
  9.8 0.6 collective-permute-done.even_down
  10.4 2.2 %conv_finish.1 = (bf16[8,144,256]{2,1,0:T(8,128)(2,1)}, f32[8,128,256]{2,1,0:T(8,128)S(1)}) custom-call(bf16[8,128,256]{2,1,0:T(8,128)(2,1)} %mid_far.5, bf16[1,128,256]{2,1,0:T(8,128)(2,1)S(1)} %collective-permute-done.even_down, bf16[1,128,256]{2,1,0:T(8,128)(2,1)S(1)} %collective-permute-done.1.odd_down, f32[1024,256]{1,0:T(8,128)S(1)} %get-tuple-element.39.own, ...), custom_call_target="tpu_custom_call" | custom-call | flops 200000000 | bytes 4538368 | tf_op jit(solution)/shard_map/conv_finish/pallas_call | solution.py:44
  12.6 4.3 %all-to-all-start = ((bf16[8,144,256]{2,1,0:T(8,128)(2,1)}), bf16[8,144,256]{2,1,0:T(8,128)(2,1)S(1)}, u32[]{:S(2)}, u32[]{:S(2)}) async-start(bf16[8,144,256]{2,1,0:T(8,128)(2,1)} %get-tuple-element.42), calls=%async_computation | async-start | bytes 1179648 | tf_op jit(solution)/shard_map/all_to_all | solution.py:495
  16.9 3.0 %prepare.1 = (bf16[256,1280]{1,0:T(8,128)(2,1)}, bf16[1024,512]{1,0:T(8,128)(2,1)}, f32[8,128,256]{2,1,0:T(8,128)}) custom-call(f32[8,128,256]{2,1,0:T(8,128)S(1)} %get-tuple-element.43.conv, bf16[8,128,256]{2,1,0:T(8,128)(2,1)} %mid_far.5, bf16[1,128,256]{2,1,0:T(8,128)(2,1)S(1)} %collective-permute-done.even_down, ...), custom_call_target="tpu_custom_call" | custom-call | flops 300000000 | bytes 5242880 | tf_op jit(solution)/shard_map/prepare/pallas_call | solution.py:44
  19.9 8.0 %all-to-all-done.came = bf16[8,144,256]{2,1,0:T(8,128)(2,1)S(1)} async-done(((bf16[8,144,256]{2,1,0:T(8,128)(2,1)}), bf16[8,144,256]{2,1,0:T(8,128)(2,1)S(1)}, u32[]{:S(2)}, u32[]{:S(2)}) %all-to-all-start) | async-done | bytes 589856 | tf_op jit(solution)/shard_map/all_to_all | solution.py:495
  28.0 21.2 %attend.1 = (bf16[8,144,256]{2,1,0:T(8,128)(2,1)}, bf16[1024,256]{1,0:T(8,128)(2,1)}, bf16[1024,512]{1,0:T(8,128)(2,1)}, bf16[1024,1536]{1,0:T(8,128)(2,1)}) custom-call(bf16[8,144,256]{2,1,0:T(8,128)(2,1)S(1)} %all-to-all-done.came, bf16[256,1536]{1,0:T(8,128)(2,1)} %qkv_w_far.1, bf16[1024,512]{1,0:T(8,128)(2,1)} %get-tuple-element.44.grad_att_far, ...), custom_call_target="tpu_custom_call" | custom-call | flops 15000000512 | bytes 8257536 | tf_op jit(solution)/shard_map/attend/pallas_call | solution.py:44
  49.1 3.7 %all-to-all-start.1 = ((bf16[8,144,256]{2,1,0:T(8,128)(2,1)}), bf16[8,144,256]{2,1,0:T(8,128)(2,1)S(1)}, u32[]{:S(2)}, u32[]{:S(2)}) async-start(bf16[8,144,256]{2,1,0:T(8,128)(2,1)} %get-tuple-element.52), calls=%async_computation.1 | async-start | bytes 1179648 | tf_op jit(solution)/shard_map/all_to_all | solution.py:495
  52.9 7.1 %attend_rest.1 = (bf16[1024,256]{1,0:T(8,128)(2,1)}, bf16[16,128,128]{2,1,0:T(8,128)(2,1)S(1)}, bf16[16,128,128]{2,1,0:T(8,128)(2,1)}, f32[8,128,256]{2,1,0:T(8,128)S(1)}, bf16[256,1280]{1,0:T(8,128)(2,1)S(1)}) custom-call(bf16[1024,256]{1,0:T(8,128)(2,1)} %get-tuple-element.45.hidden_far, bf16[1024,512]{1,0:T(8,128)(2,1)} %get-tuple-element.46.attended_far, ...), custom_call_target="tpu_custom_call" | custom-call | flops 1500000000 | bytes 10485760 | tf_op jit(solution)/shard_map/attend_rest/pallas_call | solution.py:44
  60.0 3.6 %all-to-all-done.1.came = bf16[8,144,256]{2,1,0:T(8,128)(2,1)S(1)} async-done(((bf16[8,144,256]{2,1,0:T(8,128)(2,1)}), bf16[8,144,256]{2,1,0:T(8,128)(2,1)S(1)}, u32[]{:S(2)}, u32[]{:S(2)}) %all-to-all-start.1) | async-done | bytes 589856 | tf_op jit(solution)/shard_map/all_to_all | solution.py:495
  63.7 0.0 collective-permute-start.2
  63.7 3.4 %conv_weight_grad.1 = (bf16[2,1,144,256]{3,2,1,0:T(8,128)(2,1)S(1)}, bf16[16,80,128]{2,1,0:T(8,128)(2,1)S(1)}, bf16[16,80,128]{2,1,0:T(8,128)(2,1)S(1)}, bf16[16...) custom-call(bf16[8,144,256]{2,1,0:T(8,128)(2,1)S(1)} %all-to-all-done.1.came, ...), custom_call_target="tpu_custom_call" | custom-call | flops 1200000000 | bytes 6242304 | tf_op jit(solution)/shard_map/conv_weight_grad/pallas_call | solution.py:44
  67.1 0.6 collective-permute-start.3
  67.7 1.3 %collective-permute-done.3.got = bf16[16,80,128]{2,1,0:T(8,128)(2,1)S(1)} collective-permute-done((bf16[16,80,128]{2,1,0:T(8,128)(2,1)S(1)}, bf16[16,80,128]{2,1,0:T(8,128)(2,1)S(1)}, u32[]{:S(2)}, u32[]{:S(2)}) %collective-permute-start.3) | collective-permute-done | bytes 327712 | tf_op jit(solution)/shard_map/ppermute | solution.py:499
  69.0 0.0 collective-permute-done.2.early_got
  69.0 1.1 %join.1 = bf16[16,208,128]{2,1,0:T(8,128)(2,1)} custom-call(bf16[16,128,128]{2,1,0:T(8,128)(2,1)S(1)} %get-tuple-element.57.early, bf16[16,128,128]{2,1,0:T(8,128)(2,1)S(1)} %collective-permute-done.2.early_got, bf16[16,80,128]{2,1,0:T(8,128)(2,1)S(1)} %get-tuple-element.59.mine, bf16[16,80,128]{2,1,0:T(8,128)(2,1)S(1)} %collective-permute-done.3.got), custom_call_target="tpu_custom_call" | custom-call | bytes 2555904 | tf_op jit(solution)/shard_map/join/pallas_call | solution.py:44
  70.1 4.4 %all-to-all-start.2 = ((bf16[16,208,128]{2,1,0:T(8,128)(2,1)}), bf16[16,208,128]{2,1,0:T(8,128)(2,1)S(1)}, u32[]{:S(2)}, u32[]{:S(2)}) async-start(bf16[16,208,128]{2,1,0:T(8,128)(2,1)} %join.1), calls=%async_computation.2 | async-start | bytes 1703936 | tf_op jit(solution)/shard_map/all_to_all | solution.py:495
  74.5 4.6 %collective-permute-start.5 = (bf16[1,144,256]{2,1,0:T(8,128)(2,1)S(1)}, bf16[1,144,256]{2,1,0:T(8,128)(2,1)S(1)}, u32[]{:S(2)}, u32[]{:S(2)}) collective-permute-start(bf16[1,144,256]{2,1,0:T(8,128)(2,1)S(1)} %get-tuple-element.75), channel_id=1, source_target_pairs={{8,16},{16,8},{24,32},{32,24},{40,48},{48,40},{56,64},{64,56},{72,... | collective-permute-start | bytes 221192 | tf_op jit(solution)/shard_map/ppermute | solution.py:491
  79.1 0.8 collective-permute-start.4
  79.9 3.0 %conv_data.1 = (f32[1024,256]{1,0:T(8,128)S(1)}, bf16[3,256,768]{2,1,0:T(8,128)(2,1)S(1)}) custom-call(bf16[8,128,256]{2,1,0:T(8,128)(2,1)} %get-tuple-element.63.grad_far, bf16[8,128,768]{2,1,0:T(8,128)(2,1)} %get-tuple-element.64.stacked_far, bf16[2,3,3,128,128]{4,3,2,1,0:T(8,128)(2,1)} %weight_far.3), custom_call_target="tpu_custom_call" | custom-call | flops 1200000000 | bytes 4915200 | tf_op jit(solution)/shard_map/conv_data/pallas_call | solution.py:44
  83.0 1.8 %collective-permute-done.5.odd_down = bf16[1,144,256]{2,1,0:T(8,128)(2,1)S(1)} collective-permute-done((bf16[1,144,256]{2,1,0:T(8,128)(2,1)S(1)}, bf16[1,144,256]{2,1,0:T(8,128)(2,1)S(1)}, u32[]{:S(2)}, u32[]{:S(2)}) %collective-permute-start.5) | collective-permute-done | bytes 73760 | tf_op jit(solution)/shard_map/ppermute | solution.py:491
  84.8 3.5 %collective-permute-done.4.even_down = bf16[1,144,256]{2,1,0:T(8,128)(2,1)S(1)} collective-permute-done((bf16[1,144,256]{2,1,0:T(8,128)(2,1)S(1)}, bf16[1,144,256]{2,1,0:T(8,128)(2,1)S(1)}, u32[]{:S(2)}, u32[]{:S(2)}) %collective-permute-start.4) | collective-permute-done | bytes 73760 | tf_op jit(solution)/shard_map/ppermute | solution.py:491
  88.3 1.2 %conv_data_finish.1 = bf16[8,128,256]{2,1,0:T(8,128)(2,1)} custom-call(f32[1024,256]{1,0:T(8,128)S(1)} %get-tuple-element.65.total, bf16[1,144,256]{2,1,0:T(8,128)(2,1)S(1)} %collective-permute-done.4.even_down, bf16[1,144,256]{2,1,0:T(8,128)(2,1)S(1)} %collective-permute-done.5.odd_down, bf16[3,256,768]{2,1,0:T(8,128)(2,1)S(1)} %get-tuple-element.67.matrix), custom_call_target="tpu_custom_call" | custom-call | flops 100000000 | bytes 2899968 | tf_op jit(solution)/shard_map/conv_data_finish/pallas_call | solution.py:44
  89.5 0.6 all-to-all-done.2.came
  90.1 0.1 regroup.1
  90.3 15.7 %all_to_all.20.came = bf16[8,32,128]{2,1,0:T(8,128)(2,1)S(1)} all-to-all(bf16[8,32,128]{2,1,0:T(8,128)(2,1)S(1)} %regroup.1), channel_id=1, replica_groups=mesh['z'=8,'y'=4,'x'=4,'core'=2] {'z'}, dimensions={0} | all-to-all | bytes 131072 | tf_op jit(solution)/shard_map/all_to_all | solution.py:495
  106.0 0.6 share.1
  (1 shorter events, 0.0 us)
Async XLA Ops:
  1.5 8.3 %collective-permute-start.1 = (bf16[1,128,256]{2,1,0:T(8,128)(2,1)S(1)}, bf16[1,128,256]{2,1,0:T(8,128)(2,1)S(1)}, u32[]{:S(2)}, u32[]{:S(2)}) collective-permute-start(bf16[1,128,256]{2,1,0:T(8,128)(2,1)S(1)} %get-tuple-element.73), channel_id=1, source_target_pairs={{8,16},{16,8},{24,32},{32,24},{40,48},{48,40},{56,64},{64,56},{72,... | collective-permute-start | bytes 196616 | tf_op jit(solution)/shard_map/ppermute | solution.py:491
  6.0 4.4 %collective-permute-start = (bf16[1,128,256]{2,1,0:T(8,128)(2,1)S(1)}, bf16[1,128,256]{2,1,0:T(8,128)(2,1)S(1)}, u32[]{:S(2)}, u32[]{:S(2)}) collective-permute-start(bf16[1,128,256]{2,1,0:T(8,128)(2,1)S(1)} %get-tuple-element.74), channel_id=1, source_target_pairs={{0,8},{8,0},{16,24},{24,16},{32,40},{40,32},{48,56},{56,48},{64,72... | collective-permute-start | bytes 196616 | tf_op jit(solution)/shard_map/ppermute | solution.py:491
  12.6 15.4 %all-to-all-start = ((bf16[8,144,256]{2,1,0:T(8,128)(2,1)}), bf16[8,144,256]{2,1,0:T(8,128)(2,1)S(1)}, u32[]{:S(2)}, u32[]{:S(2)}) async-start(bf16[8,144,256]{2,1,0:T(8,128)(2,1)} %get-tuple-element.42), calls=%async_computation | async-start | bytes 1179648 | tf_op jit(solution)/shard_map/all_to_all | solution.py:495
  49.1 14.5 %all-to-all-start.1 = ((bf16[8,144,256]{2,1,0:T(8,128)(2,1)}), bf16[8,144,256]{2,1,0:T(8,128)(2,1)S(1)}, u32[]{:S(2)}, u32[]{:S(2)}) async-start(bf16[8,144,256]{2,1,0:T(8,128)(2,1)} %get-tuple-element.52), calls=%async_computation.1 | async-start | bytes 1179648 | tf_op jit(solution)/shard_map/all_to_all | solution.py:495
  63.7 5.3 %collective-permute-start.2 = (bf16[16,128,128]{2,1,0:T(8,128)(2,1)S(1)}, bf16[16,128,128]{2,1,0:T(8,128)(2,1)S(1)}, u32[]{:S(2)}, u32[]{:S(2)}) collective-permute-start(bf16[16,128,128]{2,1,0:T(8,128)(2,1)S(1)} %get-tuple-element.58), channel_id=1, source_target_pairs={{0,1},{1,0},{2,3},{3,2},{4,5},{5,4},{6,7},{7,6},{8,9},{9,8},{10,11... | collective-permute-start | bytes 1572872 | tf_op jit(solution)/shard_map/ppermute | solution.py:499
  67.1 1.8 %collective-permute-start.3 = (bf16[16,80,128]{2,1,0:T(8,128)(2,1)S(1)}, bf16[16,80,128]{2,1,0:T(8,128)(2,1)S(1)}, u32[]{:S(2)}, u32[]{:S(2)}) collective-permute-start(bf16[16,80,128]{2,1,0:T(8,128)(2,1)S(1)} %get-tuple-element.61), channel_id=1, source_target_pairs={{0,1},{1,0},{2,3},{3,2},{4,5},{5,4},{6,7},{7,6},{8,9},{9,8},{10,11... | collective-permute-start | bytes 983048 | tf_op jit(solution)/shard_map/ppermute | solution.py:499
  70.1 20.1 %all-to-all-start.2 = ((bf16[16,208,128]{2,1,0:T(8,128)(2,1)}), bf16[16,208,128]{2,1,0:T(8,128)(2,1)S(1)}, u32[]{:S(2)}, u32[]{:S(2)}) async-start(bf16[16,208,128]{2,1,0:T(8,128)(2,1)} %join.1), calls=%async_computation.2 | async-start | bytes 1703936 | tf_op jit(solution)/shard_map/all_to_all | solution.py:495
  74.5 10.2 %collective-permute-start.5 = (bf16[1,144,256]{2,1,0:T(8,128)(2,1)S(1)}, bf16[1,144,256]{2,1,0:T(8,128)(2,1)S(1)}, u32[]{:S(2)}, u32[]{:S(2)}) collective-permute-start(bf16[1,144,256]{2,1,0:T(8,128)(2,1)S(1)} %get-tuple-element.75), channel_id=1, source_target_pairs={{8,16},{16,8},{24,32},{32,24},{40,48},{48,40},{56,64},{64,56},{72,... | collective-permute-start | bytes 221192 | tf_op jit(solution)/shard_map/ppermute | solution.py:491
  79.1 9.2 %collective-permute-start.4 = (bf16[1,144,256]{2,1,0:T(8,128)(2,1)S(1)}, bf16[1,144,256]{2,1,0:T(8,128)(2,1)S(1)}, u32[]{:S(2)}, u32[]{:S(2)}) collective-permute-start(bf16[1,144,256]{2,1,0:T(8,128)(2,1)S(1)} %get-tuple-element.76), channel_id=1, source_target_pairs={{0,8},{8,0},{16,24},{24,16},{32,40},{40,32},{48,56},{56,48},{64,72... | collective-permute-start | bytes 221192 | tf_op jit(solution)/shard_map/ppermute | solution.py:491
